TPU v7x, 32 devices: a whole 2x2x4 slice. The times are simulated.
32 devices in a mesh: seq: 16 (over z, y, x), head: 2 (over core).
Axes of the slice: x: 2, y: 2, z: 4, core: 2. Of those that a mesh axis runs over, the one named last changes fastest.
Arguments:
- tokens: bfloat16 [2, 4096, 1024], P(None, 'seq'), may hold values from -6 to 6
- w_query: bfloat16 [1024, 512], P(None, 'head'), may hold values from -0.1875 to 0.1875
- w_key: bfloat16 [1024, 512], P(None, 'head'), may hold values from -0.1875 to 0.1875
- w_value: bfloat16 [1024, 1024], P(None, 'head'), may hold values from -0.1875 to 0.1875
- w_outgate: bfloat16 [1024, 1024], P(None, 'head'), may hold values from -0.1875 to 0.1875
- w_gates: bfloat16 [2, 1024, 4], P(None, None, 'head'), may hold values from -0.1875 to 0.1875
- gate_bias: float32 [2, 4], P(None, 'head'), may hold values from -6.5 to 11.5
- conv_query: float32 [4, 512], P(None, 'head'), may hold values from -3 to 3
- conv_key: float32 [4, 512], P(None, 'head'), may hold values from -3 to 3
- conv_value: float32 [4, 1024], P(None, 'head'), may hold values from -3 to 3
- out_gain: float32 [256], replicated, may hold values from 0.5 to 1.5
- w_out: bfloat16 [1024, 1024], P('head'), may hold values from -0.375 to 0.375
- mix_gain: float32 [1024], replicated, may hold values from 0.5 to 1.5
- ffn_gain: float32 [1024], replicated, may hold values from 0.5 to 1.5
- w_gate: bfloat16 [1024, 2816], P(None, 'head'), may hold values from -0.1875 to 0.1875
- w_up: bfloat16 [1024, 2816], P(None, 'head'), may hold values from -0.1875 to 0.1875
- w_down: bfloat16 [2816, 1024], P('head'), may hold values from -0.15625 to 0.15625
- cotangent: bfloat16 [2, 4096, 1024], P(None, 'seq'), may hold values from -6 to 6
Outputs:
- result: bfloat16 [2, 4096, 1024], P(None, 'seq')
- grad_input: float32 [2, 4096, 1024], P(None, 'seq')
- grad_w_query: float32 [1024, 512], P('seq', 'head')
- grad_w_key: float32 [1024, 512], P('seq', 'head')
- grad_w_value: float32 [1024, 1024], P('seq', 'head')
- grad_w_outgate: float32 [1024, 1024], P('seq', 'head')
- grad_w_gates: float32 [2, 1024, 4], P(None, 'seq', 'head')
- grad_gate_bias: float32 [2, 4], P(None, 'head')
- grad_conv_query: float32 [4, 512], P(None, 'head')
- grad_conv_key: float32 [4, 512], P(None, 'head')
- grad_conv_value: float32 [4, 1024], P(None, 'head')
- grad_out_gain: float32 [256], replicated
- grad_w_out: float32 [1024, 1024], P('head', 'seq')
- grad_mix_gain: float32 [1024], P('seq')
- grad_ffn_gain: float32 [1024], P('seq')
- grad_w_gate: float32 [1024, 2816], P('seq', 'head')
- grad_w_up: float32 [1024, 2816], P('seq', 'head')
- grad_w_down: float32 [2816, 1024], P('head', 'seq')
All inputs are finite; a program needn't handle non-finite values.
Results may differ from a plain program's by a relative error of at most 0.013.
Values may be sent and summed in bfloat16 or wider, within the bound.
No kernel may reach another device: no remote copies, remote signals or barrier semaphores. Data moves between devices by JAX's collectives and lax.ppermute only.
A program may use at most 448 MiB of HBM per device.

v0:
```python
import copy
import functools

import jax
import jax.numpy as jnp
from jax import lax
from jax.experimental import pallas as pl
from jax.experimental.pallas import tpu as pltpu
from jax.sharding import PartitionSpec as P

DK = 128
DV = 256
CONV = 4
HALO = 16
LANES = 128
SCALE = DK ** (-0.5)
F32 = jnp.float32
BF16 = jnp.bfloat16
NN = ((1,), (0,))
NT = ((1,), (1,))
TN = ((0,), (0,))
NOTE = 16
VMEM_LIMIT = 48 * 1024 * 1024
SMALL_LIMIT = 20 * 1024 * 1024


def dot(left, right, dims=NN):
    return lax.dot_general(
        left.astype(BF16), right.astype(BF16), (dims, ((), ())), preferred_element_type=F32
    )


def halves(field):
    high = field.astype(BF16)
    return high, (field - high.astype(F32)).astype(BF16)


def dot3(left, right, dims=NN):
    left_high, left_low = halves(left)
    right_high, right_low = halves(right)
    return dot(left_high, right_high, dims) + (
        dot(left_high, right_low, dims) + dot(left_low, right_high, dims)
    )


def ones_dot(ones, field):
    high, low = halves(field)
    lowest = field - high.astype(F32) - low.astype(F32)
    return dot(ones, high) + (dot(ones, low) + dot(ones, lowest))


def rows_cols(size):
    return (
        lax.broadcasted_iota(jnp.int32, (size, size), 0),
        lax.broadcasted_iota(jnp.int32, (size, size), 1),
    )


def log1p_small(value):
    shifted = 1.0 + value
    same = shifted == 1.0
    safe = jnp.where(same, 1.0, shifted - 1.0)
    return jnp.where(same, value, jnp.log(shifted) * (value / safe))


def log_sigmoid(value):
    return jnp.minimum(value, 0.0) - log1p_small(jnp.exp(-jnp.abs(value)))


def sigmoid(value):
    return 1.0 / (1.0 + jnp.exp(-value))


def row_sum(field):
    return jnp.sum(field, axis=-1, keepdims=True)


def inverse_unit(lowers, rows, cols):
    size = lowers[0].shape[0]
    same = (rows // 16) == (cols // 16)
    eye = (rows == cols).astype(F32)
    powers = [jnp.where(same, -lower, 0.0) for lower in lowers]
    inverses = [eye + power for power in powers]
    for _ in range(3):
        powers = [dot3(power, power) for power in powers]
        inverses = [inv + dot3(inv, power) for inv, power in zip(inverses, powers)]
    block = 16
    while block * 2 <= size:
        inside = ((rows // (2 * block)) == (cols // (2 * block))) & (
            (rows // block) != (cols // block)
        )
        parts = [
            dot3(jnp.where(inside, lower, 0.0), inv) for lower, inv in zip(lowers, inverses)
        ]
        inverses = [inv - dot3(inv, part) for inv, part in zip(inverses, parts)]
        block *= 2
    return inverses


def conv_pre(extended, taps):
    total = taps[CONV - 1 : CONV] * extended
    for offset in range(CONV - 1):
        total = total + taps[offset : offset + 1] * pltpu.roll(extended, CONV - 1 - offset, 0)
    return total[HALO:]


def silu(value):
    return value * sigmoid(value)


def silu_slope(value):
    gate = sigmoid(value)
    return gate * (1.0 + value * (1.0 - gate))


def unit(field):
    inverse = lax.rsqrt(row_sum(field * field) + 1e-06)
    return field * inverse, inverse


def first_body(
    heads, x_ref, gain_ref, wq_ref, wk_ref, wv_ref, wg_ref, wgates_ref, bias_ref, cq_ref, ck_ref,
    cv_ref, proj_ref, pg_ref, gates_ref, sums_ref, inv_ref, mapk_ref, fresh_ref,
    score_ref, reach_ref, local_ref, decay_ref, piece_ref, low_ref, maplow_ref, log_ref, turned_ref,
):
    x = x_ref[0].astype(F32)
    mixed = x * lax.rsqrt(jnp.mean(x * x, axis=-1, keepdims=True) + 1e-06) * gain_ref[...]
    mixed = mixed.astype(BF16)
    main = mixed[HALO:]
    turned_ref[...] = jnp.transpose(main)
    proj_q = dot(mixed, wq_ref[...]).astype(BF16)
    proj_k = dot(mixed, wk_ref[...]).astype(BF16)
    proj_v = dot(mixed, wv_ref[...]).astype(BF16)
    wide = heads * DK
    proj_ref[0, :, :wide] = proj_q
    proj_ref[0, :, wide : 2 * wide] = proj_k
    proj_ref[0, :, 2 * wide :] = proj_v
    pg_ref[0] = dot(main, wg_ref[...])
    gates = dot(main, wgates_ref[...]) + bias_ref[...]
    gates_ref[0] = gates
    size = main.shape[0]
    rows, cols = rows_cols(size)
    lower = rows >= cols
    strict = rows > cols
    sums = ones_dot(lower.astype(BF16), log_sigmoid(gates))
    sums_ref[0] = sums
    sums_t = jnp.transpose(sums)
    conv_q = silu(conv_pre(proj_q.astype(F32), cq_ref[...]))
    conv_k = silu(conv_pre(proj_k.astype(F32), ck_ref[...]))
    conv_v = silu(conv_pre(proj_v.astype(F32), cv_ref[...]))
    each = range(heads)
    queries = [unit(conv_q[:, h * DK : (h + 1) * DK])[0] * SCALE for h in each]
    keys = [unit(conv_k[:, h * DK : (h + 1) * DK])[0] for h in each]
    values = [conv_v[:, h * DV : (h + 1) * DV] for h in each]
    beta = [sigmoid(gates[:, h : h + 1]) for h in each]
    total = [sums[:, heads + h : heads + h + 1] for h in each]
    decay = [
        jnp.where(
            lower, jnp.exp(jnp.minimum(total[h] - sums_t[heads + h : heads + h + 1, :], 0.0)), 0.0
        )
        for h in each
    ]
    scaled = [beta[h] * keys[h] for h in each]
    lowers = [jnp.where(strict, dot3(keys[h], scaled[h], NT) * decay[h], 0.0) for h in each]
    inverses = inverse_unit(lowers, rows, cols)
    growth = [jnp.exp(total[h]) for h in each]
    last = [total[h][size - 1 : size] for h in each]
    tail = [jnp.exp(last[h] - total[h]) * scaled[h] for h in each]
    mapk = [dot3(inverses[h], growth[h] * keys[h]) for h in each]
    fresh = [dot3(inverses[h], values[h]) for h in each]
    scores = [dot(queries[h], scaled[h], NT) * decay[h] for h in each]
    moved = [-dot3(tail[h], mapk[h], TN) for h in each]
    shift = [dot3(tail[h], fresh[h], TN) for h in each]
    reach = [growth[h] * queries[h] - dot(scores[h], mapk[h]) for h in each]
    local = [dot(scores[h], fresh[h]) for h in each]
    for h in each:
        piece_ref[0, h, :, :DK] = moved[h]
        piece_ref[0, h, :, DK:] = shift[h]
        note = log_rows(last[h])
        log_ref[0, h] = jnp.broadcast_to(last[h], (8, LANES))
        maplow_ref[0, h, :DK] = moved[h].astype(BF16)
        maplow_ref[0, h, DK:] = note
        low_ref[0, h, :DK, :DK] = moved[h].astype(BF16)
        low_ref[0, h, :DK, DK:] = shift[h].astype(BF16)
        low_ref[0, h, DK:] = jnp.concatenate([note] * (1 + DV // DK), axis=1)
        inv_ref[0, h] = inverses[h]
        mapk_ref[0, h] = mapk[h]
        fresh_ref[0, h] = fresh[h]
        score_ref[0, h] = scores[h]
        reach_ref[0, h] = reach[h]
        local_ref[0, h] = local[h]
        decay_ref[0, h] = decay[h]


def log_rows(log):
    log = jnp.broadcast_to(log, (1, LANES))
    high = log.astype(BF16).astype(F32)
    middle = (log - high).astype(BF16).astype(F32)
    rest = log - high - middle
    place = lax.broadcasted_iota(jnp.int32, (NOTE, LANES), 0)
    zero = jnp.zeros((NOTE, LANES), F32)
    rows = jnp.where(place == 0, high, jnp.where(place == 1, middle, jnp.where(place == 2, rest, zero)))
    return rows.astype(BF16)


def log_of(rows):
    return jnp.sum(rows.astype(F32), axis=0, keepdims=True)


def join_body(
    pairs, last, piece_ref, log_ref, got_ref, out_ref, newlog_ref, low_ref, maplow_ref, *far_ref
):
    wide = 1 + DV // DK
    for p in range(pairs):
        own = piece_ref[p]
        got_low = got_ref[p, :DK]
        got = got_low.astype(F32)
        own_log = log_ref[p, :1]
        got_log = log_of(got_ref[p, DK:, :LANES])
        mine = jnp.concatenate([jnp.exp(own_log)] * wide, axis=1)
        high, low = halves(own[:, :DK])
        moved = dot(high, got_low) + dot(low, got_low) + mine * got
        map_part = moved[:, :DK] + jnp.exp(got_log) * own[:, :DK]
        shift_part = moved[:, DK:] + own[:, DK:]
        new_log = own_log + got_log
        out_ref[p, :, :DK] = map_part
        out_ref[p, :, DK:] = shift_part
        newlog_ref[p] = jnp.broadcast_to(new_log, (8, LANES))
        low_ref[p, :DK, :DK] = map_part.astype(BF16)
        low_ref[p, :DK, DK:] = shift_part.astype(BF16)
        note = log_rows(new_log)
        low_ref[p, DK:] = jnp.concatenate([note] * wide, axis=1)
        maplow_ref[p, :DK] = map_part.astype(BF16)
        maplow_ref[p, DK:] = note
        if last:
            far_ref[0][p] = shift_part.astype(BF16)


def entry_body(pairs, near_ref, far_ref, out_ref):
    for p in range(pairs):
        far = far_ref[p]
        scale = jnp.exp(log_of(near_ref[p, DK:, DK:]))
        moved = dot(near_ref[p, :DK, :DK], far) + scale * far.astype(F32)
        out_ref[p] = moved + near_ref[p, :DK, DK:].astype(F32)


def back_body(pairs, map_ref, own_ref, got_ref, out_ref, low_ref):
    for p in range(pairs):
        got = got_ref[p]
        scale = jnp.concatenate([jnp.exp(log_of(map_ref[p, DK:]))] * (DV // DK), axis=1)
        out = own_ref[p] + dot(map_ref[p, :DK], got, TN) + scale * got.astype(F32)
        out_ref[p] = out
        low_ref[p] = out.astype(BF16)


def exit_body(pairs, map_ref, near_ref, far_ref, out_ref):
    for p in range(pairs):
        far = far_ref[p]
        scale = jnp.concatenate([jnp.exp(log_of(map_ref[p, DK:]))] * (DV // DK), axis=1)
        moved = dot(map_ref[p, :DK], far, TN) + scale * far.astype(F32)
        out_ref[p] = near_ref[p].astype(F32) + moved


def mixer_out_body(
    heads, state_ref, fresh_ref, mapk_ref, reach_ref, local_ref, pg_ref, gain_ref, wout_ref,
    made_ref, output_ref, gated_ref, attn_ref,
):
    for h in range(heads):
        state = state_ref[0, h]
        made_ref[0, h] = fresh_ref[0, h] - dot3(mapk_ref[0, h], state)
        output = local_ref[0, h] + dot(reach_ref[0, h], state)
        output_ref[0, :, h * DV : (h + 1) * DV] = output
        scale = lax.rsqrt(jnp.mean(output * output, axis=-1, keepdims=True) + 1e-05)
        gate = pg_ref[0, :, h * DV : (h + 1) * DV]
        gated_ref[0, :, h * DV : (h + 1) * DV] = (
            output * scale * gain_ref[...] * silu(gate)
        ).astype(BF16)
    attn_ref[0] = dot(gated_ref[0], wout_ref[...]).astype(BF16)


def feed_body(
    x_ref, mine_ref, other_ref, cot_ref, gain_ref, wgate_ref, wup_ref, wdown_ref, resid_ref,
    hidden_ref, dgate_ref, dup_ref, down_ref, dnorm_ref, normed_ref, cot_turned_ref,
):
    attn = mine_ref[0].astype(F32) + other_ref[0].astype(F32)
    resid = x_ref[0].astype(F32) + attn
    resid_ref[0] = resid
    normed = resid * lax.rsqrt(jnp.mean(resid * resid, axis=-1, keepdims=True) + 1e-06)
    normed = (normed * gain_ref[...]).astype(BF16)
    normed_ref[...] = jnp.transpose(normed)
    cot_turned_ref[...] = jnp.transpose(cot_ref[0])
    gate = dot(normed, wgate_ref[...])
    up = dot(normed, wup_ref[...])
    d_hidden = dot(cot_ref[0], wdown_ref[...], NT)
    sig = sigmoid(gate)
    active = gate * sig
    hidden = (active * up).astype(BF16)
    hidden_ref[0] = hidden
    d_gate = (d_hidden * up * (sig + active * (1.0 - sig))).astype(BF16)
    d_up = (d_hidden * active).astype(BF16)
    dgate_ref[0] = d_gate
    dup_ref[0] = d_up
    down_ref[0] = dot(hidden, wdown_ref[...]).astype(BF16)
    dnorm_ref[0] = (dot(d_gate, wgate_ref[...], NT) + dot(d_up, wup_ref[...], NT)).astype(BF16)


def mixer_back_body(
    heads, resid_ref, mine_ref, other_ref, cot_ref, output_ref, pg_ref, reach_ref, gain_ref,
    wout_ref, ogain_ref, dresid_ref, dout_ref, dpg_ref, back_ref, low_ref, dattn_ref, dgain_ref,
    dogain_ref,
):
    step = pl.program_id(0)
    resid = resid_ref[0]
    inverse = lax.rsqrt(jnp.mean(resid * resid, axis=-1, keepdims=True) + 1e-06)
    unit_resid = resid * inverse
    d_normed = mine_ref[0].astype(F32) + other_ref[0].astype(F32)
    d_gain = jnp.sum(d_normed * unit_resid, axis=0, keepdims=True)
    d_unit = d_normed * gain_ref[...]
    d_resid = inverse * (
        d_unit - unit_resid * jnp.mean(d_unit * unit_resid, axis=-1, keepdims=True)
    )
    d_resid = d_resid + cot_ref[0].astype(F32)
    dresid_ref[0] = d_resid
    d_attn = d_resid.astype(BF16)
    dattn_ref[...] = jnp.transpose(d_attn)
    d_gated = dot(d_attn, wout_ref[...], NT)
    d_ogain = jnp.zeros((1, DV), F32)
    for h in range(heads):
        part = slice(h * DV, (h + 1) * DV)
        output = output_ref[0, :, part]
        inverse = lax.rsqrt(jnp.mean(output * output, axis=-1, keepdims=True) + 1e-05)
        unit_out = output * inverse
        gate = pg_ref[0, :, part]
        grad = d_gated[:, part]
        active = silu(gate)
        d_ogain = d_ogain + jnp.sum(grad * unit_out * active, axis=0, keepdims=True)
        dpg_ref[0, :, part] = (grad * unit_out * ogain_ref[...] * silu_slope(gate)).astype(BF16)
        d_unit = grad * ogain_ref[...] * active
        d_out = inverse * (d_unit - unit_out * jnp.mean(d_unit * unit_out, axis=-1, keepdims=True))
        dout_ref[0, :, part] = d_out
        back = dot(reach_ref[0, h], d_out, TN)
        back_ref[0, h] = back
        low_ref[0, h] = back.astype(BF16)

    @pl.when(step == 0)
    def _():
        dgain_ref[...] = d_gain
        dogain_ref[...] = d_ogain

    @pl.when(step > 0)
    def _():
        dgain_ref[...] += d_gain
        dogain_ref[...] += d_ogain


def conv_back(grad, extended, taps, pre):
    d_pre = grad * silu_slope(pre)
    padded = jnp.concatenate([jnp.zeros((HALO, d_pre.shape[1]), F32), d_pre], axis=0)
    length = padded.shape[0]
    d_ext = taps[CONV - 1 : CONV] * padded
    d_taps = []
    for offset in range(CONV):
        back = CONV - 1 - offset
        if back:
            d_ext = d_ext + taps[offset : offset + 1] * pltpu.roll(padded, length - back, 0)
            shifted = pltpu.roll(extended, back, 0)
        else:
            shifted = extended
        d_taps.append(jnp.sum(padded * shifted, axis=0, keepdims=True))
    return d_ext, jnp.concatenate(d_taps, axis=0)


def early_body(
    heads, proj_ref, gates_ref, sums_ref, dout_ref, state_ref, made_ref, inv_ref, score_ref,
    decay_ref, cq_ref, ck_ref, xone_ref, xmap_ref, dkey_ref, dcol_ref, dext_ref, dtap_ref,
):
    step = pl.program_id(0)
    wide = heads * DK
    ext_q = proj_ref[0, :, :wide].astype(F32)
    ext_k = proj_ref[0, :, wide : 2 * wide].astype(F32)
    pre_q = conv_pre(ext_q, cq_ref[...])
    conv_q = silu(pre_q)
    conv_k = silu(conv_pre(ext_k, ck_ref[...]))
    gates = gates_ref[0]
    sums = sums_ref[0]
    size = gates.shape[0]
    each = range(heads)
    units = [unit(conv_q[:, h * DK : (h + 1) * DK]) for h in each]
    queries = [units[h][0] * SCALE for h in each]
    keys = [unit(conv_k[:, h * DK : (h + 1) * DK])[0] for h in each]
    beta = [sigmoid(gates[:, h : h + 1]) for h in each]
    total = [sums[:, heads + h : heads + h + 1] for h in each]
    growth = [jnp.exp(total[h]) for h in each]
    tail = [jnp.exp(total[h][size - 1 : size] - total[h]) * beta[h] * keys[h] for h in each]
    d_out = [dout_ref[0, :, h * DV : (h + 1) * DV] for h in each]
    d_made = [dot(score_ref[0, h], d_out[h], TN) for h in each]
    d_score = [dot(d_out[h], made_ref[0, h], NT) * decay_ref[0, h] for h in each]
    d_query = [
        dot3(d_score[h], beta[h] * keys[h]) + dot(growth[h] * d_out[h], state_ref[0, h], NT)
        for h in each
    ]
    d_key = [dot3(d_score[h], queries[h], TN) for h in each]
    x_one = [dot(inv_ref[0, h], d_made[h], TN) for h in each]
    x_map = [dot(inv_ref[0, h], tail[h], TN) for h in each]
    lanes = lax.broadcasted_iota(jnp.int32, (size, LANES), 1)
    cols = jnp.zeros((size, LANES), F32)
    grads = []
    for h in each:
        xone_ref[0, h] = x_one[h]
        xmap_ref[0, h] = x_map[h]
        dkey_ref[0, h] = beta[h] * d_key[h]
        key_sum = row_sum(d_key[h] * keys[h])
        cols = cols + jnp.where(lanes == h, key_sum, 0.0)
        d_total = row_sum(d_query[h] * queries[h]) - beta[h] * key_sum
        cols = cols + jnp.where(lanes == heads + h, d_total, 0.0)
        unit_q, inverse = units[h]
        d_unit = d_query[h] * SCALE
        grads.append(inverse * (d_unit - unit_q * row_sum(d_unit * unit_q)))
    dcol_ref[0] = cols
    d_ext, d_taps = conv_back(jnp.concatenate(grads, axis=1), ext_q, cq_ref[...], pre_q)
    dext_ref[0] = d_ext

    @pl.when(step == 0)
    def _():
        dtap_ref[...] = d_taps

    @pl.when(step > 0)
    def _():
        dtap_ref[...] += d_taps


def late_body(
    heads, proj_ref, gates_ref, sums_ref, dend_ref, state_ref, made_ref, decay_ref, xone_ref,
    xmap_ref, dkey_ref, dcol_ref, dextq_ref, ck_ref, cv_ref, dext_ref, dgates_ref, dtap_ref, dbias_ref,
):
    step = pl.program_id(0)
    wide = heads * DK
    ext_k = proj_ref[0, :, wide : 2 * wide].astype(F32)
    ext_v = proj_ref[0, :, 2 * wide :].astype(F32)
    pre_k = conv_pre(ext_k, ck_ref[...])
    pre_v = conv_pre(ext_v, cv_ref[...])
    conv_k = silu(pre_k)
    gates = gates_ref[0]
    sums = sums_ref[0]
    size = gates.shape[0]
    rows, cols = rows_cols(size)
    strict = rows > cols
    each = range(heads)
    units = [unit(conv_k[:, h * DK : (h + 1) * DK]) for h in each]
    keys = [units[h][0] for h in each]
    beta = [sigmoid(gates[:, h : h + 1]) for h in each]
    total = [sums[:, heads + h : heads + h + 1] for h in each]
    growth = [jnp.exp(total[h]) for h in each]
    left = [jnp.exp(total[h][size - 1 : size] - total[h]) for h in each]
    d_end = [dend_ref[0, h] for h in each]
    made = [made_ref[0, h] for h in each]
    state = [state_ref[0, h] for h in each]
    d_rhs = [xone_ref[0, h] + dot(xmap_ref[0, h], d_end[h]) for h in each]
    d_tail = [dot(made[h], d_end[h], NT) for h in each]
    d_lower = [
        jnp.where(strict, -dot(d_rhs[h], made[h], NT) * decay_ref[0, h], 0.0) for h in each
    ]
    d_plain = [
        dot3(d_lower[h], beta[h] * keys[h]) - dot(growth[h] * d_rhs[h], state[h], NT) for h in each
    ]
    d_turned = [dot3(d_lower[h], keys[h], TN) for h in each]
    lanes = lax.broadcasted_iota(jnp.int32, (size, LANES), 1)
    places = lax.broadcasted_iota(jnp.int32, (size, 1), 0)
    d_col = dcol_ref[0]
    grads_k = []
    for h in each:
        turned = row_sum(d_turned[h] * keys[h])
        tails = row_sum(d_tail[h] * keys[h])
        tail_weight = left[h] * beta[h]
        d_key = d_plain[h] + beta[h] * d_turned[h] + tail_weight * d_tail[h] + dkey_ref[0, h]
        d_total = row_sum(d_plain[h] * keys[h]) - beta[h] * turned - tail_weight * tails
        ended = jnp.sum(tail_weight * tails, axis=0, keepdims=True)
        whole = jnp.sum(row_sum(d_end[h] * state[h]), axis=0, keepdims=True)
        ended = ended + growth[h][size - 1 : size] * whole
        d_total = d_total + jnp.where(places == size - 1, ended, 0.0)
        d_col = d_col + jnp.where(lanes == h, turned + left[h] * tails, 0.0)
        d_col = d_col + jnp.where(lanes == heads + h, d_total, 0.0)
        unit_k, inverse = units[h]
        grads_k.append(inverse * (d_key - unit_k * row_sum(d_key * unit_k)))
    upper = (rows <= cols).astype(BF16)
    d_decay = ones_dot(upper, d_col)
    rate = sigmoid(gates)
    d_gates = jnp.where(
        lanes < heads, d_col * rate * (1.0 - rate), d_decay / (1.0 + jnp.exp(gates))
    )
    d_gates = jnp.where(lanes < 2 * heads, d_gates, 0.0)
    dgates_ref[0] = d_gates.astype(BF16)
    d_bias = jnp.sum(d_gates, axis=0, keepdims=True)
    dext_k, dtaps_k = conv_back(jnp.concatenate(grads_k, axis=1), ext_k, ck_ref[...], pre_k)
    dext_v, dtaps_v = conv_back(jnp.concatenate(d_rhs, axis=1), ext_v, cv_ref[...], pre_v)
    dext_ref[0, :, :wide] = dextq_ref[0]
    dext_ref[0, :, wide : 2 * wide] = dext_k
    dext_ref[0, :, 2 * wide :] = dext_v

    @pl.when(step == 0)
    def _():
        dtap_ref[:, :wide] = dtaps_k
        dtap_ref[:, wide:] = dtaps_v
        dbias_ref[...] = d_bias

    @pl.when(step > 0)
    def _():
        dtap_ref[:, :wide] += dtaps_k
        dtap_ref[:, wide:] += dtaps_v
        dbias_ref[...] += d_bias


def input_back_body(
    dext_ref, edge_ref, dpg_ref, dgates_ref, wq_ref, wk_ref, wv_ref, wg_ref, wgates_ref,
    dqk_ref, dv_ref, dmixed_ref,
):
    wide = wq_ref.shape[1]
    own = dext_ref[0, HALO:]
    size = own.shape[0]
    d_proj = jnp.concatenate([own[: size - HALO], own[size - HALO :] + edge_ref[0]], axis=0)
    d_proj = d_proj.astype(BF16)
    dqk_ref[0] = d_proj[:, : 2 * wide]
    dv_ref[0] = d_proj[:, 2 * wide :]
    d_mixed = dot(d_proj[:, :wide], wq_ref[...], NT)
    d_mixed = d_mixed + dot(d_proj[:, wide : 2 * wide], wk_ref[...], NT)
    d_mixed = d_mixed + dot(d_proj[:, 2 * wide :], wv_ref[...], NT)
    d_mixed = d_mixed + dot(dpg_ref[0], wg_ref[...], NT)
    d_mixed = d_mixed + dot(dgates_ref[0], wgates_ref[...], NT)
    dmixed_ref[0] = d_mixed.astype(BF16)


def last_body(
    x_ref, mine_ref, other_ref, dresid_ref, gain_ref, grad_ref, dgain_ref,
):
    x = x_ref[0].astype(F32)
    inverse = lax.rsqrt(jnp.mean(x * x, axis=-1, keepdims=True) + 1e-06)
    unit_x = x * inverse
    d_mixed = mine_ref[0].astype(F32) + other_ref[0].astype(F32)
    d_unit = d_mixed * gain_ref[...]
    back = inverse * (d_unit - unit_x * jnp.mean(d_unit * unit_x, axis=-1, keepdims=True))
    grad_ref[0] = dresid_ref[0] + back
    d_gain = jnp.sum(d_mixed * unit_x, axis=0, keepdims=True)
    step = pl.program_id(0)

    @pl.when(step == 0)
    def _():
        dgain_ref[...] = d_gain

    @pl.when(step > 0)
    def _():
        dgain_ref[...] += d_gain


def result_body(resid_ref, down_ref, downother_ref, result_ref):
    down = down_ref[0].astype(F32) + downother_ref[0].astype(F32)
    result_ref[0] = (resid_ref[0] + down).astype(BF16)


def held_rows(left_refs, index_ref, first, blocks, held):
    share = left_refs[0].shape[1]
    for number, left_ref in enumerate(left_refs):
        for place in range(blocks):
            held[number, place * share : (place + 1) * share] = left_ref[index_ref[first + place]]


def send_body(terms, first, blocks, lefts, index_ref, *refs):
    out_ref, held = refs[-2:]
    held_rows(refs[:lefts], index_ref, first, blocks, held)
    at = 0
    for left, right, width in terms:
        out_ref[:, at : at + width] = dot(held[left], refs[lefts + right][...]).astype(BF16)
        at += width


def keep_body(terms, blocks, parts, lefts, index_ref, *refs):
    rights = len(terms)
    got_ref = refs[lefts + rights]
    keep_ref, held = refs[lefts + rights + 1], refs[-1]
    send_refs = refs[lefts + rights + 2 : -1]
    held_rows(refs[:lefts], index_ref, 0, blocks, held)
    rows = keep_ref.shape[0]
    at = 0
    for left, right, width in terms:
        total = dot(held[left], refs[lefts + right][...])
        total = total + got_ref[:, at : at + width].astype(F32)
        keep_ref[:, at : at + width] = total[:rows]
        for part in range(1, parts):
            send_refs[part - 1][:, at : at + width] = total[part * rows : (part + 1) * rows].astype(BF16)
        at += width


def add_body(parts, gots, keep_ref, *refs):
    total = keep_ref[...]
    for got_ref in refs[:gots]:
        total = total + got_ref[...].astype(F32)
    out_ref = refs[gots]
    rows = out_ref.shape[0]
    out_ref[...] = total[:rows]
    for part in range(1, parts):
        refs[gots + part][...] = total[part * rows : (part + 1) * rows].astype(BF16)


def joined_body(widths, *refs):
    keep_ref, send_ref = refs[-2:]
    rows = keep_ref.shape[0]
    at = 0
    for number, width in enumerate(widths):
        total = refs[2 * number][...] + refs[2 * number + 1][...].astype(F32)
        keep_ref[:, at : at + width] = total[:rows]
        send_ref[:, at : at + width] = total[rows:].astype(BF16)
        at += width


def total_body(cuts, gots, *refs):
    at = 0
    for ref, width in zip(refs[1 + gots :], cuts):
        total = refs[0][:, at : at + width]
        for got_ref in refs[1 : 1 + gots]:
            total = total + got_ref[:, at : at + width].astype(F32)
        ref[...] = total
        at += width


def pack_body(tapq_ref, tapkv_ref, bias_ref, ffn_ref, mix_ref, ogain_ref, other_ref, out_ref):
    wide = tapq_ref.shape[1]
    out_ref[...] = jnp.zeros_like(out_ref)
    out_ref[:CONV, :wide] = tapq_ref[...]
    out_ref[:CONV, wide:] = tapkv_ref[...]
    out_ref[4:5, :LANES] = bias_ref[...]
    out_ref[5:6] = ffn_ref[...]
    out_ref[6:7] = mix_ref[...]
    out_ref[7:8, :DV] = ogain_ref[...] + other_ref[...]


def sum_body(count, *refs):
    total = refs[0][...]
    for ref in refs[1:count]:
        total = total + ref[...]
    refs[count][...] = total


def by_seq(shape):
    rest = len(shape) - 1
    return pl.BlockSpec((1,) + tuple(shape[1:]), lambda s: (s,) + (0,) * rest)


def whole(shape):
    rest = len(shape)
    return pl.BlockSpec(tuple(shape), lambda s: (0,) * rest)


def without(body, position, count):
    def shorter(*refs):
        return body(*refs[:position], *refs[position + count :])

    return shorter if count else body


def call(body, name, seqs, parts, shared, outs, sums=(), turned=(), after=(), flops=0):
    operands = list(parts) + list(shared)
    listed = list(outs) + list(turned) + list(sums)
    out_shape = [jax.ShapeDtypeStruct(shape, kind) for shape, kind in listed]
    moved = sum(a.size * a.dtype.itemsize for a in operands + out_shape)
    return pl.pallas_call(
        without(body, len(operands), len(after)),
        grid=(seqs,),
        in_specs=[by_seq(a.shape) for a in parts]
        + [whole(a.shape) for a in shared]
        + [pl.BlockSpec(memory_space=pl.ANY)] * len(after),
        out_specs=[by_seq(shape) for shape, _ in outs]
        + [pl.BlockSpec((shape[0], shape[1] // seqs), lambda s: (0, s)) for shape, _ in turned]
        + [whole(shape) for shape, _ in sums],
        out_shape=out_shape,
        compiler_params=pltpu.CompilerParams(vmem_limit_bytes=VMEM_LIMIT),
        cost_estimate=pl.CostEstimate(flops=int(flops), bytes_accessed=int(moved), transcendentals=0),
        name=name,
    )(*operands, *after)


def small_call(body, name, arrays, outs, after=(), scalars=(), scratch=(), flops=2e8):
    out_shape = [jax.ShapeDtypeStruct(shape, kind) for shape, kind in outs]
    moved = sum(a.size * a.dtype.itemsize for a in list(arrays) + out_shape)
    return pl.pallas_call(
        without(body, len(scalars) + len(arrays), len(after)),
        in_specs=[pl.BlockSpec(memory_space=pltpu.SMEM)] * len(scalars)
        + [pl.BlockSpec(memory_space=pltpu.VMEM)] * len(arrays)
        + [pl.BlockSpec(memory_space=pl.ANY)] * len(after),
        out_specs=[pl.BlockSpec(memory_space=pltpu.VMEM)] * len(outs),
        out_shape=out_shape,
        scratch_shapes=list(scratch),
        compiler_params=pltpu.CompilerParams(vmem_limit_bytes=SMALL_LIMIT),
        cost_estimate=pl.CostEstimate(flops=int(flops), bytes_accessed=int(moved), transcendentals=0),
        name=name,
    )(*scalars, *arrays, *after)


class Halved:
    def __init__(self, name, steps, me, lefts, rights, terms):
        self.name, self.lefts, self.rights, self.terms = (name, lefts, rights, terms)
        order = [bit for step in steps for bit in step]
        self.steps = steps
        self.index = block_index(order, me)
        self.count = 1 << len(order)
        _, self.share, self.tokens = lefts[0].shape
        self.columns = sum(width for _, _, width in terms)
        self.done = 0

    def trade(self, sends):
        bits = self.steps[self.done]
        self.done += 1
        self.gots = []
        for part, send in enumerate(sends, 1):
            moved = sum(
                ((part >> (len(bits) - 1 - place)) & 1) << bit for place, bit in enumerate(bits)
            )
            self.gots.append(traded(send, moved))

    def multiplied(self, body, suffix, extra, outs, after):
        blocks = self.count // 2
        return small_call(
            body, self.name + suffix, list(self.lefts) + list(self.rights) + extra, outs, after,
            scalars=[self.index],
            scratch=[pltpu.VMEM((len(self.lefts), blocks * self.share, self.tokens), BF16)],
            flops=2 * blocks * self.share * self.tokens * self.columns,
        )

    def outs(self, rows):
        parts = 1 << len(self.steps[self.done])
        return parts, [((rows // parts, self.columns), F32)] + [
            ((rows // parts, self.columns), BF16)
        ] * (parts - 1)

    def send(self, *after):
        blocks = self.count // 2
        body = functools.partial(send_body, self.terms, blocks, blocks, len(self.lefts))
        rows = blocks * self.share
        sends = self.multiplied(body, "_send", [], [((rows, self.columns), BF16)], after)
        self.trade(sends)
        return sends[0]

    def keep(self, *after):
        blocks = self.count // 2
        parts, outs = self.outs(blocks * self.share)
        body = functools.partial(keep_body, self.terms, blocks, parts, len(self.lefts))
        self.kept, *sends = self.multiplied(body, "_keep", self.gots, outs, after)
        self.trade(sends)
        return self.kept

    def add(self, *after):
        parts, outs = self.outs(self.kept.shape[0])
        body = functools.partial(add_body, parts, len(self.gots))
        self.kept, *sends = small_call(
            body, self.name + "_add", [self.kept] + self.gots, outs, after, flops=1e6
        )
        self.trade(sends)
        return self.kept

    def left(self):
        return len(self.steps) - self.done

    def total(self, cuts, *after):
        rows = self.kept.shape[0]
        outs = [((rows, width), F32) for width in cuts]
        return small_call(
            functools.partial(total_body, tuple(cuts), len(self.gots)), self.name + "_total",
            [self.kept] + self.gots, outs, after, flops=1e6,
        )


def joined(name, groups, *after):
    whole_sum = copy.copy(groups[0])
    whole_sum.name = name
    whole_sum.columns = sum(group.columns for group in groups)
    rows = groups[0].kept.shape[0] // 2
    shape = (rows, whole_sum.columns)
    operands = [array for group in groups for array in [group.kept] + group.gots]
    body = functools.partial(joined_body, [group.columns for group in groups])
    whole_sum.kept, send = small_call(
        body, name, operands, [(shape, F32), (shape, BF16)], after, flops=1e6
    )
    whole_sum.trade([send])
    return whole_sum


def halving_steps(count, first):
    bits = list(range(count.bit_length() - 1))
    return [[bit] for bit in first] + [[bit] for bit in bits if bit not in first]


def block_index(order, me):
    count = 1 << len(order)
    moved = [
        sum(((place >> (len(order) - 1 - step)) & 1) << bit for step, bit in enumerate(order))
        for place in range(count)
    ]
    return jnp.bitwise_xor(jnp.array(moved, jnp.int32), me)


def traded(block, moved):
    count = lax.axis_size("seq")
    return lax.ppermute(block, "seq", [(i, i ^ moved) for i in range(count)])


def passed_along(block, axis, distance):
    devices = range(lax.axis_size(axis))
    route = [(i - distance, i) for i in devices if i - distance in devices]
    return lax.ppermute(block, axis, route)


def swapped(block):
    count = lax.axis_size("head")
    return lax.ppermute(block, "head", [(i, i ^ 1) for i in range(count)])


def on_device(
    tokens, w_query, w_key, w_value, w_outgate, w_gates, gate_bias, conv_query, conv_key,
    conv_value, out_gain, w_out, mix_gain, ffn_gain, w_gate, w_up, w_down, cotangent,
):
    seqs, size, width = tokens.shape
    heads = gate_bias.shape[1]
    pairs = seqs * heads
    units = w_gate.shape[1]
    count, me = lax.axis_size("seq"), lax.axis_index("seq")
    wide = heads * DK
    out_wide = heads * DV
    proj_wide = 2 * wide + out_wide

    halo = passed_along(tokens[:, size - HALO :], "seq", 1)
    x_ext = jnp.concatenate([halo, tokens], axis=1)
    gates_w = jnp.swapaxes(w_gates, 0, 1).reshape(width, 2 * heads)
    gates_w = jnp.pad(gates_w, ((0, 0), (0, LANES - 2 * heads)))
    bias = jnp.pad(gate_bias.reshape(1, 2 * heads), ((0, 0), (0, LANES - 2 * heads)))
    mix_row = mix_gain.reshape(1, width)
    ffn_row = ffn_gain.reshape(1, width)
    out_row = out_gain.reshape(1, DV)
    square = (seqs, heads, size, size)
    by_key = (seqs, heads, size, DK)
    by_value = (seqs, heads, size, DV)
    tokens_here = seqs * size
    steps_x, steps_y = halving_steps(count, (0, 1)), halving_steps(count, (1, 0))
    steps_yzx, steps_zxy = halving_steps(count, (1, 2, 0)), halving_steps(count, (2, 0, 1))
    turned_shape = (width, tokens_here)
    share = width // count

    def in_blocks(turned):
        return turned.reshape(count, share, tokens_here)

    def flat(field):
        return field.reshape(tokens_here, field.shape[2])

    (
        proj, proj_g, gates, sums, inv, mapk, fresh, score, reach, local, decay, piece, low,
        map_low, log, mixed_t,
    ) = call(
        functools.partial(first_body, heads), "project_and_local", seqs, [x_ext],
        [mix_row, w_query, w_key, w_value, w_outgate, gates_w, bias, conv_query, conv_key, conv_value],
        [
            ((seqs, size + HALO, proj_wide), BF16),
            ((seqs, size, out_wide), F32), ((seqs, size, LANES), F32), ((seqs, size, LANES), F32),
            (square, F32), (by_key, F32), (by_value, F32), (square, F32), (by_key, F32),
            (by_value, F32), (square, F32), ((seqs, heads, DK, DK + DV), F32),
            ((seqs, heads, DK + NOTE, DK + DV), BF16),
            ((seqs, heads, DK + NOTE, DK), BF16), ((seqs, heads, 8, LANES), F32),
        ],
        turned=[(turned_shape, BF16)],
        flops=1e10,
    )

    piece = piece.reshape(pairs, DK, DK + DV)
    low = low.reshape(pairs, DK + NOTE, DK + DV)
    log = log.reshape(pairs, 8, LANES)
    maps = [map_low.reshape(pairs, DK + NOTE, DK)]
    state_shape = (pairs, DK, DV)
    dists = []
    reach_by = 1
    while reach_by * 2 < count:
        dists.append(reach_by)
        reach_by *= 2
    for level, d in enumerate(dists):
        got = passed_along(low, "seq", d)
        last = level + 1 == len(dists)
        outs = [(piece.shape, F32), (log.shape, F32), (low.shape, BF16), (maps[0].shape, BF16)]
        if last:
            outs.append((state_shape, BF16))
        piece, log, low, map_low, *far = small_call(
            functools.partial(join_body, pairs, last), "join", [piece, log, got], outs
        )
        maps.append(map_low)
    near = passed_along(low, "seq", 1)
    far = passed_along(far[0], "seq", 1 + reach_by)
    back_maps = [maps[0]]
    for level in range(1, len(dists)):
        back_maps.append(passed_along(maps[level], "seq", 1 - dists[level]))
    near_map = passed_along(maps[-1], "seq", -reach_by)
    (state,) = small_call(
        functools.partial(entry_body, pairs), "entry", [near, far], [(state_shape, F32)]
    )
    state = state.reshape(seqs, heads, DK, DV)

    made, output, gated, attn = call(
        functools.partial(mixer_out_body, heads), "mixer_out", seqs,
        [state, fresh, mapk, reach, local, proj_g], [out_row, w_out],
        [
            (by_value, F32), ((seqs, size, out_wide), F32), ((seqs, size, out_wide), BF16),
            ((seqs, size, width), BF16),
        ],
        after=[near_map] + back_maps[1:],
        flops=1.5e9,
    )
    attn_other = swapped(attn)

    resid, hidden, d_gate, d_up, down, d_norm, normed_t, cot_t = call(
        feed_body, "feed_forward", seqs, [tokens, attn, attn_other, cotangent],
        [ffn_row, w_gate, w_up, w_down],
        [
            ((seqs, size, width), F32), ((seqs, size, units), BF16), ((seqs, size, units), BF16),
            ((seqs, size, units), BF16), ((seqs, size, width), BF16), ((seqs, size, width), BF16),
        ],
        turned=[(turned_shape, BF16), (turned_shape, BF16)],
        flops=1.2e10,
    )
    d_norm_other = swapped(d_norm)
    down_other = swapped(down)

    normed_b, cot_b, mixed_b = in_blocks(normed_t), in_blocks(cot_t), in_blocks(mixed_t)
    gate_sum = Halved("gate", steps_x, me, [normed_b], [flat(d_gate)], ((0, 0, units),))
    up_sum = Halved("up", steps_yzx, me, [normed_b], [flat(d_up)], ((0, 0, units),))
    down_sum = Halved("down", steps_zxy, me, [cot_b], [flat(hidden)], ((0, 0, units),))
    done = down_sum.send(up_sum.send(gate_sum.send()))

    d_resid, d_out, d_pg, back, low, d_attn_t, d_ffn_gain, d_out_gain = call(
        functools.partial(mixer_back_body, heads), "mixer_back", seqs,
        [resid, d_norm, d_norm_other, cotangent, output, proj_g, reach],
        [ffn_row, w_out, out_row],
        [
            ((seqs, size, width), F32), ((seqs, size, out_wide), F32),
            ((seqs, size, out_wide), BF16), ((seqs, heads, DK, DV), F32),
            ((seqs, heads, DK, DV), BF16),
        ],
        [((1, width), F32), ((1, DV), F32)],
        turned=[(turned_shape, BF16)],
        after=[done],
        flops=1.5e9,
    )

    outs_sum = Halved(
        "outs", steps_zxy, me, [in_blocks(d_attn_t), mixed_b], [flat(gated), flat(d_pg)],
        ((0, 0, out_wide), (1, 1, out_wide)),
    )
    back = back.reshape(state_shape)
    low = low.reshape(state_shape)
    x_one, x_map, d_key, d_col, dext_q, dtap_q = call(
        functools.partial(early_body, heads), "delta_back_early", seqs,
        [proj, gates, sums, d_out, state, made, inv, score, decay], [conv_query, conv_key],
        [
            (by_value, F32), (by_key, F32), (by_key, F32), ((seqs, size, LANES), F32),
            ((seqs, size + HALO, wide), F32),
        ],
        [((CONV, wide), F32)],
        flops=3e9,
    )
    (result,) = call(
        result_body, "result", seqs, [resid, down, down_other], [],
        [((seqs, size, width), BF16)], after=[d_col],
    )
    done = result
    for level, d in enumerate(dists):
        got = passed_along(low, "seq", -d)
        if level == 1:
            done = down_sum.keep(up_sum.keep(gate_sum.keep(done)))
        back, low = small_call(
            functools.partial(back_body, pairs), "join_back", [back_maps[level], back, got],
            [(state_shape, F32), (state_shape, BF16)], after=[done],
        )
        done = low
    near = passed_along(low, "seq", -1)
    far = passed_along(low, "seq", -1 - reach_by)
    done = down_sum.add(up_sum.add(gate_sum.add(done)))
    (d_end,) = small_call(
        functools.partial(exit_body, pairs), "exit", [near_map, near, far], [(state_shape, F32)],
        after=[done],
    )
    done = outs_sum.send(d_end)
    d_end = d_end.reshape(seqs, heads, DK, DV)
    d_ext, d_gates, dtap_kv, d_bias = call(
        functools.partial(late_body, heads), "delta_back_late", seqs,
        [
            proj, gates, sums, d_end, state, made, decay, x_one, x_map, d_key, d_col, dext_q,
        ],
        [conv_key, conv_value],
        [((seqs, size + HALO, proj_wide), F32), ((seqs, size, LANES), BF16)],
        [((CONV, wide + out_wide), F32), ((1, LANES), F32)],
        after=[done],
        flops=3e9,
    )
    edges = passed_along(d_ext[:, :HALO], "seq", -1)
    feed_sum = joined("feed_last", [gate_sum, up_sum, down_sum], d_bias)
    done = feed_sum.kept
    d_qk, d_v, d_mixed = call(
        input_back_body, "input_back", seqs, [d_ext, edges, d_pg, d_gates],
        [w_query, w_key, w_value, w_outgate, gates_w],
        [
            ((seqs, size, 2 * wide), BF16), ((seqs, size, out_wide), BF16),
            ((seqs, size, width), BF16),
        ],
        after=[done],
        flops=1.7e9,
    )
    d_mixed_other = swapped(d_mixed)
    query_sum = Halved(
        "query_key", steps_x, me, [mixed_b], [flat(d_qk), flat(d_gates)],
        ((0, 0, 2 * wide), (0, 1, LANES)),
    )
    value_sum = Halved("value", steps_y, me, [mixed_b], [flat(d_v)], ((0, 0, out_wide),))
    done = outs_sum.keep(value_sum.send(query_sum.send(d_mixed)))
    grad_input, d_mix_gain = call(
        last_body, "first_norm_back", seqs, [tokens, d_mixed, d_mixed_other, d_resid], [mix_row],
        [((seqs, size, width), F32)], [((1, width), F32)], after=[done],
    )

    (small,) = small_call(
        pack_body, "pack",
        [dtap_q, dtap_kv, d_bias, d_ffn_gain, d_mix_gain, d_out_gain, swapped(d_out_gain)],
        [((8, width), F32)], flops=1e4,
    )

    def finish(group, cuts, done):
        while group.left():
            done = group.add(done)
        return group.total(cuts, done)

    def small_step(bit, done):
        return small_call(
            functools.partial(sum_body, 2), "small_sum", [small, traded(small, 1 << bit)],
            [(small.shape, F32)], after=[done], flops=1e4,
        )[0]

    bits = [step[0] for step in steps_x]
    done = value_sum.keep(query_sum.keep(small))
    grad_gate, grad_up, grad_down = finish(feed_sum, [units] * 3, done)
    done = outs_sum.add(grad_gate)
    done = small = small_step(bits.pop(0), done)
    ins_sum = joined("ins_join", [query_sum, value_sum], done)
    done = small = small_step(bits.pop(0), ins_sum.kept)
    ins_sum = joined("ins_last", [ins_sum, outs_sum], done)
    done = small = small_step(bits.pop(0), ins_sum.kept)
    grad_query, grad_key, grad_gates, grad_value, grad_out, grad_outgate = finish(
        ins_sum, [wide, wide, LANES, out_wide, out_wide, out_wide], done
    )
    done = grad_query
    while bits:
        done = small = small_step(bits.pop(0), done)
    grad_gates = grad_gates[:, : 2 * heads].reshape(share, 2, heads)

    def mine_of(row):
        return lax.dynamic_slice(small, (row, me * share), (1, share)).reshape(share)

    return (
        result,
        grad_input,
        grad_query,
        grad_key,
        grad_value,
        grad_outgate,
        jnp.swapaxes(grad_gates, 0, 1),
        small[4, : 2 * heads].reshape(2, heads),
        small[:CONV, :wide],
        small[:CONV, wide : 2 * wide],
        small[:CONV, 2 * wide : proj_wide],
        small[7, :DV],
        jnp.swapaxes(grad_out, 0, 1),
        mine_of(6),
        mine_of(5),
        grad_gate,
        grad_up,
        jnp.swapaxes(grad_down, 0, 1),
    )


def solution(mesh):
    return jax.shard_map(
        on_device,
        mesh=mesh,
        in_specs=(
            P(None, "seq", None),
            P(None, "head"),
            P(None, "head"),
            P(None, "head"),
            P(None, "head"),
            P(None, None, "head"),
            P(None, "head"),
            P(None, "head"),
            P(None, "head"),
            P(None, "head"),
            P(),
            P("head", None),
            P(),
            P(),
            P(None, "head"),
            P(None, "head"),
            P("head", None),
            P(None, "seq", None),
        ),
        out_specs=(
            P(None, "seq", None),
            P(None, "seq", None),
            P("seq", "head"),
            P("seq", "head"),
            P("seq", "head"),
            P("seq", "head"),
            P(None, "seq", "head"),
            P(None, "head"),
            P(None, "head"),
            P(None, "head"),
            P(None, "head"),
            P(),
            P("head", "seq"),
            P("seq"),
            P("seq"),
            P("seq", "head"),
            P("seq", "head"),
            P("head", "seq"),
        ),
        check_vma=False,
    )
```

profile of v0, /device:TPU:0, one launch (start us, length us, event | category | flops | bytes accessed | tf_op | source)
XLA Modules:
  0.0 314.5 jit_solution(3246607064997236647)
XLA Ops:
  1.5 4.8 %collective-permute-start = (bf16[2,16,1024]{2,1,0:T(8,128)(2,1)S(1)}, bf16[2,16,1024]{2,1,0:T(8,128)(2,1)S(1)}, u32[]{:S(2)}, u32[]{:S(2)}) collective-permute-start(bf16[2,16,1024]{2,1,0:T(8,128)(2,1)S(1)} %slice.24), channel_id=1, source_target_pairs={{0,2},{2,4},{4,6},{6,8},{8,10},{10,12},{12,14},{14,16},{16,18},{18... | collective-permute-start | bytes 196616 | tf_op jit(solution)/shard_map/ppermute | solution.py:807
  8.3 2.3 pad_maximum_fusion.x_ref
  10.6 18.2 %project_and_local.1 = (bf16[2,272,1024]{2,1,0:T(8,128)(2,1)}, f32[2,256,512]{2,1,0:T(8,128)S(1)}, f32[2,256,128]{2,1,0:T(8,128)S(1)}, f32[2,256,128]{2,1,0:T(8,...) custom-call(bf16[2,272,1024]{2,1,0:T(8,128)(2,1)} %pad_maximum_fusio, ...), custom_call_target="tpu_custom_call" | custom-call | flops 10000000000 | bytes 15962624 | tf_op jit(solution)/shard_map/project_and_local/pallas_call | solution.py:664
  30.2 4.2 %collective-permute-start.1 = (bf16[4,144,384]{2,1,0:T(8,128)(2,1)S(1)}, bf16[4,144,384]{2,1,0:T(8,128)(2,1)S(1)}, u32[]{:S(2)}, u32[]{:S(2)}) collective-permute-start(bf16[4,144,384]{2,1,0:T(8,128)(2,1)S(1)} %bitcast.82), channel_id=1, source_target_pairs={{0,2},{2,4},{4,6},{6,8},{8,10},{10,12},{12,14},{14,16},{16,18},{18... | collective-permute-start | bytes 1327112 | tf_op jit(solution)/shard_map/ppermute | solution.py:807
  34.4 8.3 %collective-permute-done.1.got_ref = bf16[4,144,384]{2,1,0:T(8,128)(2,1)S(1)} collective-permute-done((bf16[4,144,384]{2,1,0:T(8,128)(2,1)S(1)}, bf16[4,144,384]{2,1,0:T(8,128)(2,1)S(1)}, u32[]{:S(2)}, u32[]{:S(2)}) %collective-permute-start.1) | collective-permute-done | bytes 442400 | tf_op jit(solution)/shard_map/ppermute | solution.py:807
  43.0 6.2 %collective-permute-start.2 = (bf16[4,144,384]{2,1,0:T(8,128)(2,1)S(1)}, bf16[4,144,384]{2,1,0:T(8,128)(2,1)S(1)}, u32[]{:S(2)}, u32[]{:S(2)}) collective-permute-start(bf16[4,144,384]{2,1,0:T(8,128)(2,1)S(1)} %get-tuple-element.125), channel_id=1, source_target_pairs={{0,4},{2,6},{4,8},{6,10},{8,12},{10,14},{12,16},{14,18},{16,20},{1... | collective-permute-start | bytes 1327112 | tf_op jit(solution)/shard_map/ppermute | solution.py:807
  49.3 7.3 %collective-permute-done.2.got_ref = bf16[4,144,384]{2,1,0:T(8,128)(2,1)S(1)} collective-permute-done((bf16[4,144,384]{2,1,0:T(8,128)(2,1)S(1)}, bf16[4,144,384]{2,1,0:T(8,128)(2,1)S(1)}, u32[]{:S(2)}, u32[]{:S(2)}) %collective-permute-start.2) | collective-permute-done | bytes 442400 | tf_op jit(solution)/shard_map/ppermute | solution.py:807
  57.0 7.1 %collective-permute-start.3 = (bf16[4,144,384]{2,1,0:T(8,128)(2,1)S(1)}, bf16[4,144,384]{2,1,0:T(8,128)(2,1)S(1)}, u32[]{:S(2)}, u32[]{:S(2)}) collective-permute-start(bf16[4,144,384]{2,1,0:T(8,128)(2,1)S(1)} %get-tuple-element.128), channel_id=1, source_target_pairs={{0,8},{2,10},{4,12},{6,14},{8,16},{10,18},{12,20},{14,22},{16,24},... | collective-permute-start | bytes 1327112 | tf_op jit(solution)/shard_map/ppermute | solution.py:807
  64.1 6.4 %collective-permute-done.3.got_ref = bf16[4,144,384]{2,1,0:T(8,128)(2,1)S(1)} collective-permute-done((bf16[4,144,384]{2,1,0:T(8,128)(2,1)S(1)}, bf16[4,144,384]{2,1,0:T(8,128)(2,1)S(1)}, u32[]{:S(2)}, u32[]{:S(2)}) %collective-permute-start.3) | collective-permute-done | bytes 442400 | tf_op jit(solution)/shard_map/ppermute | solution.py:807
  70.4 1.3 join.5
  71.7 1.3 collective-permute-start.4
  73.0 6.7 %collective-permute-start.5 = (bf16[4,128,256]{2,1,0:T(8,128)(2,1)S(1)}, bf16[4,128,256]{2,1,0:T(8,128)(2,1)S(1)}, u32[]{:S(2)}, u32[]{:S(2)}) collective-permute-start(bf16[4,128,256]{2,1,0:T(8,128)(2,1)S(1)} %get-tuple-element.130), channel_id=1, source_target_pairs={{0,18},{2,20},{4,22},{6,24},{8,26},{10,28},{12,30},{1,19},{3,21},{... | collective-permute-start | bytes 786440 | tf_op jit(solution)/shard_map/ppermute | solution.py:807
  79.7 1.3 collective-permute-start.7
  81.0 1.3 collective-permute-start.8
  82.3 1.5 collective-permute-start.6
  84.7 3.1 collective-permute-done.7.refs_9_.refs_0_
  87.8 3.6 %collective-permute-done.8.refs_10_.refs_0_ = bf16[4,144,128]{2,1,0:T(8,128)(2,1)S(1)} collective-permute-done((bf16[4,144,128]{2,1,0:T(8,128)(2,1)S(1)}, bf16[4,144,128]{2,1,0:T(8,128)(2,1)S(1)}, u32[]{:S(2)}, u32[]{:S(2)}) %collective-permute-start.8) | collective-permute-done | bytes 147488 | tf_op jit(solution)/shard_map/ppermute | solution.py:807
  91.4 2.2 collective-permute-done.6.refs_8_.refs_0_
  93.6 3.7 %mixer_out.1 = (f32[2,2,256,256]{3,2,1,0:T(8,128)S(1)}, f32[2,256,512]{2,1,0:T(8,128)S(1)}, bf16[2,256,512]{2,1,0:T(8,128)(2,1)S(1)}, bf16[2,256,1024]{2,1,0:T(8,128)(2,1)S(1)}) custom-call(f32[2,2,128,256]{3,2,1,0:T(8,128)S(1)} %bitcast.61, f32[2,2,256,256]{3,2,1,0:T(8,128)} %get-tuple-element.131.refs_1_, ...), custom_call_target="tpu_custom_call" | custom-call | flops 1500000000 | bytes 9438208 | tf_op jit(solution)/shard_map/mixer_out/pallas_call | solution.py:664
  100.2 2.7 collective-permute-done.9.other_ref
  102.9 15.5 %feed_forward.1 = (f32[2,256,1024]{2,1,0:T(8,128)}, bf16[2,256,1408]{2,1,0:T(8,128)(2,1)}, bf16[2,256,1408]{2,1,0:T(8,128)(2,1)}, bf16[2,256,1408]{2,1,0:T(8,128...) custom-call(bf16[2,256,1024]{2,1,0:T(8,128)(2,1)S(1)} %copy-done.9, ...), custom_call_target="tpu_custom_call" | custom-call | flops 12000000000 | bytes 23465984 | tf_op jit(solution)/shard_map/feed_forward/pallas_call | solution.py:664
  118.6 1.6 copy-done.3
  120.2 1.5 gate_send.1.refs_3_
  121.7 1.3 collective-permute-start.16
  123.0 1.5 up_send.1.refs_3_
  124.5 2.1 collective-permute-start.15
  126.6 1.5 down_send.1.refs_10_
  128.2 2.4 collective-permute-start.14
  132.8 6.5 %mixer_back.1 = (f32[2,256,1024]{2,1,0:T(8,128)}, f32[2,256,512]{2,1,0:T(8,128)S(1)}, bf16[2,256,512]{2,1,0:T(8,128)(2,1)S(1)}, f32[2,2,128,256]{3,2,1,0:T(8,128...) custom-call(f32[2,256,1024]{2,1,0:T(8,128)} %get-tuple-element.140.r, ...), custom_call_target="tpu_custom_call" | custom-call | flops 1500000000 | bytes 14428160 | tf_op jit(solution)/shard_map/mixer_back/pallas_call | solution.py:664
  141.9 1.5 collective-permute-start.12
  149.0 5.5 %delta_back_early.1 = (f32[2,2,256,256]{3,2,1,0:T(8,128)S(1)}, f32[2,2,256,128]{3,2,1,0:T(8,128)S(1)}, f32[2,2,256,128]{3,2,1,0:T(8,128)S(1)}, f32[2,256,128]{2,...) custom-call(bf16[2,272,1024]{2,1,0:T(8,128)(2,1)} %get-tuple-element.142.proj_ref.refs_0_, ...), custom_call_target="tpu_custom_call" | custom-call | flops 3000000000 | bytes 10334208 | tf_op jit(solution)/shard_map/delta_back_early/pallas_call | solution.py:664
  157.1 2.8 result.1.refs_3_
  159.9 1.3 collective-permute-done.12.refs_2_
  163.6 1.3 collective-permute-start.13
  165.0 2.4 gate_keep.1
  167.4 2.8 collective-permute-start.22
  170.1 2.5 up_keep.1
  172.6 6.1 %collective-permute-start.21 = (bf16[256,1408]{1,0:T(8,128)(2,1)S(1)}, bf16[256,1408]{1,0:T(8,128)(2,1)S(1)}, u32[]{:S(2)}, u32[]{:S(2)}) collective-permute-start(bf16[256,1408]{1,0:T(8,128)(2,1)S(1)} %get-tuple-element.170), channel_id=1, source_target_pairs={{0,8},{2,10},{4,12},{6,14},{8,0},{10,2},{12,4},{14,6},{16,24},{18,... | collective-permute-start | bytes 2162696 | tf_op jit(solution)/shard_map/ppermute | solution.py:801
  178.7 2.4 down_keep.1
  181.1 2.9 collective-permute-start.20
  184.3 1.3 collective-permute-start.17
  185.6 13.5 %collective-permute-done.17.refs_2_ = bf16[4,128,256]{2,1,0:T(8,128)(2,1)S(1)} collective-permute-done((bf16[4,128,256]{2,1,0:T(8,128)(2,1)S(1)}, bf16[4,128,256]{2,1,0:T(8,128)(2,1)S(1)}, u32[]{:S(2)}, u32[]{:S(2)}) %collective-permute-start.17) | collective-permute-done | bytes 262176 | tf_op jit(solution)/shard_map/ppermute | solution.py:807
  200.2 1.3 collective-permute-start.18
  201.4 1.3 collective-permute-start.19
  203.3 5.8 %collective-permute-start.26 = (bf16[128,1408]{1,0:T(8,128)(2,1)S(1)}, bf16[128,1408]{1,0:T(8,128)(2,1)S(1)}, u32[]{:S(2)}, u32[]{:S(2)}) collective-permute-start(bf16[128,1408]{1,0:T(8,128)(2,1)S(1)} %get-tuple-element.187), channel_id=1, source_target_pairs={{0,4},{2,6},{4,0},{6,2},{8,12},{10,14},{12,8},{14,10},{16,20},{18,... | collective-permute-start | bytes 1081352 | tf_op jit(solution)/shard_map/ppermute | solution.py:801
  209.8 5.9 %collective-permute-done.18.refs_1_ = bf16[4,128,256]{2,1,0:T(8,128)(2,1)S(1)} collective-permute-done((bf16[4,128,256]{2,1,0:T(8,128)(2,1)S(1)}, bf16[4,128,256]{2,1,0:T(8,128)(2,1)S(1)}, u32[]{:S(2)}, u32[]{:S(2)}) %collective-permute-start.18) | collective-permute-done | bytes 262176 | tf_op jit(solution)/shard_map/ppermute | solution.py:807
  215.7 3.8 %collective-permute-done.19.refs_2_ = bf16[4,128,256]{2,1,0:T(8,128)(2,1)S(1)} collective-permute-done((bf16[4,128,256]{2,1,0:T(8,128)(2,1)S(1)}, bf16[4,128,256]{2,1,0:T(8,128)(2,1)S(1)}, u32[]{:S(2)}, u32[]{:S(2)}) %collective-permute-start.19) | collective-permute-done | bytes 262176 | tf_op jit(solution)/shard_map/ppermute | solution.py:807
  222.2 9.2 %delta_back_late.1 = (f32[2,272,1024]{2,1,0:T(8,128)}, bf16[2,256,128]{2,1,0:T(8,128)(2,1)S(1)}, f32[4,768]{1,0:T(4,128)S(1)}, f32[1,128]{1,0:T(1,128)S(1)}) custom-call(bf16[2,272,1024]{2,1,0:T(8,128)(2,1)} %get-tuple-element.142.proj_ref.refs_0_, f32[2,256,128]{2,1,0:T(8,128)S(1)} %copy-done.77, f32[2,256,128]{2,1,0:T(8,128)S(1)} %copy-done.80, ...), custom_call_target="tpu_custom_call" | custom-call | flops 3000000000 | bytes 10084864 | tf_op jit(solution)/shard_map/delta_back_late/pallas_call | solution.py:664
  232.3 1.6 collective-permute-start.23
  233.9 7.6 %collective-permute-start.28 = (bf16[512,1024]{1,0:T(8,128)(2,1)S(1)}, bf16[512,1024]{1,0:T(8,128)(2,1)S(1)}, u32[]{:S(2)}, u32[]{:S(2)}) collective-permute-start(bf16[512,1024]{1,0:T(8,128)(2,1)S(1)} %copy-done.28), channel_id=1, source_target_pairs={{0,8},{2,10},{4,12},{6,14},{8,0},{10,2},{12,4},{14,6},{16,24},{18,... | collective-permute-start | bytes 3145736 | tf_op jit(solution)/shard_map/ppermute | solution.py:801
  243.4 3.9 %input_back.1 = (bf16[2,256,512]{2,1,0:T(8,128)(2,1)S(1)}, bf16[2,256,512]{2,1,0:T(8,128)(2,1)S(1)}, bf16[2,256,1024]{2,1,0:T(8,128)(2,1)S(1)}) custom-call(f32[2,272,1024]{2,1,0:T(8,128)} %get-tuple-element.183.refs_0_, f32[2,16,1024]{2,1,0:T(8,128)S(1)} %collective-permute-done.23.refs_1_, bf16[2,256,512]{2,1,0:T(8,128)(2,1)S(1)} %copy-done.8, ...), custom_call_target="tpu_custom_call" | custom-call | flops 1700000000 | bytes 8519680 | tf_op jit(solution)/shard_map/input_back/pallas_call | solution.py:664
  249.6 5.1 %collective-permute-start.32 = (bf16[512,512]{1,0:T(8,128)(2,1)S(1)}, bf16[512,512]{1,0:T(8,128)(2,1)S(1)}, u32[]{:S(2)}, u32[]{:S(2)}) collective-permute-start(bf16[512,512]{1,0:T(8,128)(2,1)S(1)} %value_send.1.refs_6_), channel_id=1, source_target_pairs={{0,4},{2,6},{4,0},{6,2},{8,12},{10,14},{12,8},{14,10},{16,20},{18,... | collective-permute-start | bytes 1572872 | tf_op jit(solution)/shard_map/ppermute | solution.py:801
  254.7 11.1 %collective-permute-done.28.refs_5_ = bf16[512,1024]{1,0:T(8,128)(2,1)S(1)} collective-permute-done((bf16[512,1024]{1,0:T(8,128)(2,1)S(1)}, bf16[512,1024]{1,0:T(8,128)(2,1)S(1)}, u32[]{:S(2)}, u32[]{:S(2)}) %collective-permute-start.28) | collective-permute-done | bytes 1048608 | tf_op jit(solution)/shard_map/ppermute | solution.py:801
  265.8 1.3 outs_keep.1
  267.2 3.6 %first_norm_back.1 = (f32[2,256,1024]{2,1,0:T(8,128)}, f32[1,1024]{1,0:T(1,128)S(1)}) custom-call(bf16[2,256,1024]{2,1,0:T(8,128)(2,1)S(1)} %copy-done.10, bf16[2,256,1024]{2,1,0:T(8,128)(2,1)S(1)} %get-tuple-element.190.refs_4_.refs_1_, bf16[2,256,1024]{2,1,0:T(8,128)(2,1)S(1)} %collective-permute-done.27.refs_2_, ...), custom_call_target="tpu_custom_call" | custom-call | bytes 7348224 | tf_op jit(solution)/shard_map/first_norm_back/pallas_call | solution.py:664
  273.0 2.0 collective-permute-start.33
  275.1 6.2 %collective-permute-done.36.refs_1_ = bf16[64,4224]{1,0:T(8,128)(2,1)S(1)} collective-permute-done((bf16[64,4224]{1,0:T(8,128)(2,1)S(1)}, bf16[64,4224]{1,0:T(8,128)(2,1)S(1)}, u32[]{:S(2)}, u32[]{:S(2)}) %collective-permute-start.36) | collective-permute-done | bytes 540704 | tf_op jit(solution)/shard_map/ppermute | solution.py:801
  283.7 1.4 collective-permute-start.37
  285.1 1.7 collective-permute-start.38
  287.2 6.6 %collective-permute-done.39.refs_1_ = f32[8,1024]{1,0:T(8,128)S(1)} collective-permute-done((f32[8,1024]{1,0:T(8,128)S(1)}, f32[8,1024]{1,0:T(8,128)S(1)}, u32[]{:S(2)}, u32[]{:S(2)}) %collective-permute-start.39) | collective-permute-done | bytes 32800 | tf_op jit(solution)/shard_map/ppermute | solution.py:801
  293.9 2.5 collective-permute-start.40
  296.5 4.4 %collective-permute-done.41.refs_1_ = f32[8,1024]{1,0:T(8,128)S(1)} collective-permute-done((f32[8,1024]{1,0:T(8,128)S(1)}, f32[8,1024]{1,0:T(8,128)S(1)}, u32[]{:S(2)}, u32[]{:S(2)}) %collective-permute-start.41) | collective-permute-done | bytes 32800 | tf_op jit(solution)/shard_map/ppermute | solution.py:801
  300.9 4.1 %collective-permute-start.42 = (f32[8,1024]{1,0:T(8,128)S(1)}, f32[8,1024]{1,0:T(8,128)S(1)}, u32[]{:S(2)}, u32[]{:S(2)}) collective-permute-start(f32[8,1024]{1,0:T(8,128)S(1)} %small_sum.6.refs_2_.refs_0_), channel_id=1, source_target_pairs={{0,16},{2,18},{4,20},{6,22},{8,24},{10,26},{12,28},{14,30},{16,0},... | collective-permute-start | bytes 98312 | tf_op jit(solution)/shard_map/ppermute | solution.py:801
  305.0 4.2 %collective-permute-done.40.refs_1_ = bf16[64,2176]{1,0:T(8,128)(2,1)S(1)} collective-permute-done((bf16[64,2176]{1,0:T(8,128)(2,1)S(1)}, bf16[64,2176]{1,0:T(8,128)(2,1)S(1)}, u32[]{:S(2)}, u32[]{:S(2)}) %collective-permute-start.40) | collective-permute-done | bytes 278560 | tf_op jit(solution)/shard_map/ppermute | solution.py:801
  (254 shorter events, 44.8 us)
Async XLA Ops:
  1.5 6.7 %collective-permute-start = (bf16[2,16,1024]{2,1,0:T(8,128)(2,1)S(1)}, bf16[2,16,1024]{2,1,0:T(8,128)(2,1)S(1)}, u32[]{:S(2)}, u32[]{:S(2)}) collective-permute-start(bf16[2,16,1024]{2,1,0:T(8,128)(2,1)S(1)} %slice.24), channel_id=1, source_target_pairs={{0,2},{2,4},{4,6},{6,8},{8,10},{10,12},{12,14},{14,16},{16,18},{18... | collective-permute-start | bytes 196616 | tf_op jit(solution)/shard_map/ppermute | solution.py:807
  30.2 41.5 %copy-start.15 = (f32[2,256,512]{2,1,0:T(8,128)}, f32[2,256,512]{2,1,0:T(8,128)S(1)}, u32[]{:S(2)}) copy-start(f32[2,256,512]{2,1,0:T(8,128)S(1)} %get-tuple-element.135.refs_5_) | copy-start | bytes 3145732
  30.2 41.5 %copy-start.47 = (bf16[2,2,144,128]{3,2,1,0:T(8,128)(2,1)}, bf16[2,2,144,128]{3,2,1,0:T(8,128)(2,1)S(1)}, u32[]{:S(2)}) copy-start(bf16[2,2,144,128]{3,2,1,0:T(8,128)(2,1)S(1)} %get-tuple-element.158) | copy-start | bytes 442372
  30.2 63.4 %copy-start.24 = (f32[2,2,256,128]{3,2,1,0:T(8,128)}, f32[2,2,256,128]{3,2,1,0:T(8,128)S(1)}, u32[]{:S(2)}) copy-start(f32[2,2,256,128]{3,2,1,0:T(8,128)S(1)} %get-tuple-element.133.refs_3_.refs_6_) | copy-start | bytes 1572868
  30.2 12.5 %collective-permute-start.1 = (bf16[4,144,384]{2,1,0:T(8,128)(2,1)S(1)}, bf16[4,144,384]{2,1,0:T(8,128)(2,1)S(1)}, u32[]{:S(2)}, u32[]{:S(2)}) collective-permute-start(bf16[4,144,384]{2,1,0:T(8,128)(2,1)S(1)} %bitcast.82), channel_id=1, source_target_pairs={{0,2},{2,4},{4,6},{6,8},{8,10},{10,12},{12,14},{14,16},{16,18},{18... | collective-permute-start | bytes 1327112 | tf_op jit(solution)/shard_map/ppermute | solution.py:807
  43.0 13.5 %collective-permute-start.2 = (bf16[4,144,384]{2,1,0:T(8,128)(2,1)S(1)}, bf16[4,144,384]{2,1,0:T(8,128)(2,1)S(1)}, u32[]{:S(2)}, u32[]{:S(2)}) collective-permute-start(bf16[4,144,384]{2,1,0:T(8,128)(2,1)S(1)} %get-tuple-element.125), channel_id=1, source_target_pairs={{0,4},{2,6},{4,8},{6,10},{8,12},{10,14},{12,16},{14,18},{16,20},{1... | collective-permute-start | bytes 1327112 | tf_op jit(solution)/shard_map/ppermute | solution.py:807
  57.0 36.6 %copy-start.51 = (f32[256]{0:T(256)S(1)}, f32[256]{0:T(256)}, u32[]{:S(2)}) copy-start(f32[256]{0:T(256)} %param.34) | copy-start | bytes 3076
  57.0 13.5 %collective-permute-start.3 = (bf16[4,144,384]{2,1,0:T(8,128)(2,1)S(1)}, bf16[4,144,384]{2,1,0:T(8,128)(2,1)S(1)}, u32[]{:S(2)}, u32[]{:S(2)}) collective-permute-start(bf16[4,144,384]{2,1,0:T(8,128)(2,1)S(1)} %get-tuple-element.128), channel_id=1, source_target_pairs={{0,8},{2,10},{4,12},{6,14},{8,16},{10,18},{12,20},{14,22},{16,24},... | collective-permute-start | bytes 1327112 | tf_op jit(solution)/shard_map/ppermute | solution.py:807
  71.7 12.7 %collective-permute-start.4 = (bf16[4,144,384]{2,1,0:T(8,128)(2,1)S(1)}, bf16[4,144,384]{2,1,0:T(8,128)(2,1)S(1)}, u32[]{:S(2)}, u32[]{:S(2)}) collective-permute-start(bf16[4,144,384]{2,1,0:T(8,128)(2,1)S(1)} %get-tuple-element.129), channel_id=1, source_target_pairs={{0,2},{2,4},{4,6},{6,8},{8,10},{10,12},{12,14},{14,16},{16,18},{18... | collective-permute-start | bytes 1327112 | tf_op jit(solution)/shard_map/ppermute | solution.py:807
  73.0 11.4 %collective-permute-start.5 = (bf16[4,128,256]{2,1,0:T(8,128)(2,1)S(1)}, bf16[4,128,256]{2,1,0:T(8,128)(2,1)S(1)}, u32[]{:S(2)}, u32[]{:S(2)}) collective-permute-start(bf16[4,128,256]{2,1,0:T(8,128)(2,1)S(1)} %get-tuple-element.130), channel_id=1, source_target_pairs={{0,18},{2,20},{4,22},{6,24},{8,26},{10,28},{12,30},{1,19},{3,21},{... | collective-permute-start | bytes 786440 | tf_op jit(solution)/shard_map/ppermute | solution.py:807
  79.7 8.1 %collective-permute-start.7 = (bf16[4,144,128]{2,1,0:T(8,128)(2,1)S(1)}, bf16[4,144,128]{2,1,0:T(8,128)(2,1)S(1)}, u32[]{:S(2)}, u32[]{:S(2)}) collective-permute-start(bf16[4,144,128]{2,1,0:T(8,128)(2,1)S(1)} %get-tuple-element.137), channel_id=1, source_target_pairs={{2,0},{4,2},{6,4},{8,6},{10,8},{12,10},{14,12},{16,14},{18,16},{20... | collective-permute-start | bytes 442376 | tf_op jit(solution)/shard_map/ppermute | solution.py:807
  81.0 10.4 %collective-permute-start.8 = (bf16[4,144,128]{2,1,0:T(8,128)(2,1)S(1)}, bf16[4,144,128]{2,1,0:T(8,128)(2,1)S(1)}, u32[]{:S(2)}, u32[]{:S(2)}) collective-permute-start(bf16[4,144,128]{2,1,0:T(8,128)(2,1)S(1)} %get-tuple-element.138), channel_id=1, source_target_pairs={{6,0},{8,2},{10,4},{12,6},{14,8},{16,10},{18,12},{20,14},{22,16},{... | collective-permute-start | bytes 442376 | tf_op jit(solution)/shard_map/ppermute | solution.py:807
  82.3 11.3 %collective-permute-start.6 = (bf16[4,144,128]{2,1,0:T(8,128)(2,1)S(1)}, bf16[4,144,128]{2,1,0:T(8,128)(2,1)S(1)}, u32[]{:S(2)}, u32[]{:S(2)}) collective-permute-start(bf16[4,144,128]{2,1,0:T(8,128)(2,1)S(1)} %get-tuple-element.136), channel_id=1, source_target_pairs={{16,0},{18,2},{20,4},{22,6},{24,8},{26,10},{28,12},{30,14},{17,1},... | collective-permute-start | bytes 442376 | tf_op jit(solution)/shard_map/ppermute | solution.py:807
  84.7 12.7 %copy-start.21 = (f32[4,128,256]{2,1,0:T(8,128)}, f32[4,128,256]{2,1,0:T(8,128)S(1)}, u32[]{:S(2)}) copy-start(f32[4,128,256]{2,1,0:T(8,128)S(1)} %entry.1) | copy-start | bytes 1572868
  87.8 9.6 %copy-start.34 = (bf16[4,144,128]{2,1,0:T(8,128)(2,1)}, bf16[4,144,128]{2,1,0:T(8,128)(2,1)S(1)}, u32[]{:S(2)}) copy-start(bf16[4,144,128]{2,1,0:T(8,128)(2,1)S(1)} %collective-permute-done.7.refs_9_.refs_0_) | copy-start | bytes 442372
  93.6 9.3 %copy-start.9 = (bf16[2,256,1024]{2,1,0:T(8,128)(2,1)S(1)}, bf16[2,256,1024]{2,1,0:T(8,128)(2,1)}, u32[]{:S(2)}) copy-start(bf16[2,256,1024]{2,1,0:T(8,128)(2,1)} %refs_0_.1) | copy-start | bytes 3145732
  93.6 9.3 %copy-start.50 = (f32[1024]{0:T(1024)S(1)}, f32[1024]{0:T(1024)}, u32[]{:S(2)}) copy-start(f32[1024]{0:T(1024)} %param.37) | copy-start | bytes 12292
  100.1 2.8 collective-permute-start.9
  118.4 8.2 %copy-start.17 = (bf16[1024,512]{1,0:T(8,128)(2,1)}, bf16[1024,512]{1,0:T(8,128)(2,1)S(1)}, u32[]{:S(2)}) copy-start(bf16[1024,512]{1,0:T(8,128)(2,1)S(1)} %get-tuple-element.147) | copy-start | bytes 3145732
  118.4 12.2 %collective-permute-start.11 = (bf16[2,256,1024]{2,1,0:T(8,128)(2,1)S(1)}, bf16[2,256,1024]{2,1,0:T(8,128)(2,1)S(1)}, u32[]{:S(2)}, u32[]{:S(2)}) collective-permute-start(bf16[2,256,1024]{2,1,0:T(8,128)(2,1)S(1)} %get-tuple-element.145.refs_1_), channel_id=1, source_target_pairs={{0,1},{1,0},{2,3},{3,2},{4,5},{5,4},{6,7},{7,6},{8,9},{9,8},{10,11... | collective-permute-start | bytes 3145736 | tf_op jit(solution)/shard_map/ppermute | solution.py:812
  121.7 43.2 %collective-permute-start.16 = (bf16[512,1408]{1,0:T(8,128)(2,1)S(1)}, bf16[512,1408]{1,0:T(8,128)(2,1)}, u32[]{:S(2)}, u32[]{:S(2)}) collective-permute-start(bf16[512,1408]{1,0:T(8,128)(2,1)S(1)} %gate_send.1.refs_3_), channel_id=1, source_target_pairs={{0,2},{2,0},{4,6},{6,4},{8,10},{10,8},{12,14},{14,12},{16,18},{18,... | collective-permute-start | bytes 4325384 | tf_op jit(solution)/shard_map/ppermute | solution.py:801
  124.5 45.6 %collective-permute-start.15 = (bf16[512,1408]{1,0:T(8,128)(2,1)S(1)}, bf16[512,1408]{1,0:T(8,128)(2,1)}, u32[]{:S(2)}, u32[]{:S(2)}) collective-permute-start(bf16[512,1408]{1,0:T(8,128)(2,1)S(1)} %up_send.1.refs_3_), channel_id=1, source_target_pairs={{0,4},{2,6},{4,0},{6,2},{8,12},{10,14},{12,8},{14,10},{16,20},{18,... | collective-permute-start | bytes 4325384 | tf_op jit(solution)/shard_map/ppermute | solution.py:801
  128.2 50.5 %collective-permute-start.14 = (bf16[512,1408]{1,0:T(8,128)(2,1)S(1)}, bf16[512,1408]{1,0:T(8,128)(2,1)}, u32[]{:S(2)}, u32[]{:S(2)}) collective-permute-start(bf16[512,1408]{1,0:T(8,128)(2,1)S(1)} %down_send.1.refs_10_), channel_id=1, source_target_pairs={{0,8},{2,10},{4,12},{6,14},{8,0},{10,2},{12,4},{14,6},{16,24},{18,... | collective-permute-start | bytes 4325384 | tf_op jit(solution)/shard_map/ppermute | solution.py:801
  130.6 26.5 %collective-permute-start.10 = (bf16[2,256,1024]{2,1,0:T(8,128)(2,1)}, bf16[2,256,1024]{2,1,0:T(8,128)(2,1)}, u32[]{:S(2)}, u32[]{:S(2)}) collective-permute-start(bf16[2,256,1024]{2,1,0:T(8,128)(2,1)} %get-tuple-element.141.refs_1_), channel_id=1, source_target_pairs={{0,1},{1,0},{2,3},{3,2},{4,5},{5,4},{6,7},{7,6},{8,9},{9,8},{10,11... | collective-permute-start | bytes 3145736 | tf_op jit(solution)/shard_map/ppermute | solution.py:812
  141.9 19.3 %collective-permute-start.12 = (bf16[4,128,256]{2,1,0:T(8,128)(2,1)}, bf16[4,128,256]{2,1,0:T(8,128)(2,1)}, u32[]{:S(2)}, u32[]{:S(2)}) collective-permute-start(bf16[4,128,256]{2,1,0:T(8,128)(2,1)} %bitcast.15), channel_id=1, source_target_pairs={{2,0},{4,2},{6,4},{8,6},{10,8},{12,10},{14,12},{16,14},{18,16},{20... | collective-permute-start | bytes 786440 | tf_op jit(solution)/shard_map/ppermute | solution.py:807
  163.6 20.4 %collective-permute-start.13 = (bf16[4,128,256]{2,1,0:T(8,128)(2,1)S(1)}, bf16[4,128,256]{2,1,0:T(8,128)(2,1)S(1)}, u32[]{:S(2)}, u32[]{:S(2)}) collective-permute-start(bf16[4,128,256]{2,1,0:T(8,128)(2,1)S(1)} %get-tuple-element.162.refs_4_), channel_id=1, source_target_pairs={{4,0},{6,2},{8,4},{10,6},{12,8},{14,10},{16,12},{18,14},{20,16},{2... | collective-permute-start | bytes 786440 | tf_op jit(solution)/shard_map/ppermute | solution.py:807
  167.4 35.4 %collective-permute-start.22 = (bf16[256,1408]{1,0:T(8,128)(2,1)S(1)}, bf16[256,1408]{1,0:T(8,128)(2,1)S(1)}, u32[]{:S(2)}, u32[]{:S(2)}) collective-permute-start(bf16[256,1408]{1,0:T(8,128)(2,1)S(1)} %get-tuple-element.171), channel_id=1, source_target_pairs={{0,4},{2,6},{4,0},{6,2},{8,12},{10,14},{12,8},{14,10},{16,20},{18,... | collective-permute-start | bytes 2162696 | tf_op jit(solution)/shard_map/ppermute | solution.py:801
  170.1 8.6 %copy-start.18 = (bf16[1024,512]{1,0:T(8,128)(2,1)S(1)}, bf16[1024,512]{1,0:T(8,128)(2,1)}, u32[]{:S(2)}) copy-start(bf16[1024,512]{1,0:T(8,128)(2,1)} %copy-done.17) | copy-start | bytes 3145732
  172.6 30.3 %collective-permute-start.21 = (bf16[256,1408]{1,0:T(8,128)(2,1)S(1)}, bf16[256,1408]{1,0:T(8,128)(2,1)S(1)}, u32[]{:S(2)}, u32[]{:S(2)}) collective-permute-start(bf16[256,1408]{1,0:T(8,128)(2,1)S(1)} %get-tuple-element.170), channel_id=1, source_target_pairs={{0,8},{2,10},{4,12},{6,14},{8,0},{10,2},{12,4},{14,6},{16,24},{18,... | collective-permute-start | bytes 2162696 | tf_op jit(solution)/shard_map/ppermute | solution.py:801
  181.1 18.0 %copy-start.33 = (bf16[4,144,128]{2,1,0:T(8,128)(2,1)S(1)}, bf16[4,144,128]{2,1,0:T(8,128)(2,1)}, u32[]{:S(2)}) copy-start(bf16[4,144,128]{2,1,0:T(8,128)(2,1)} %copy-done.32) | copy-start | bytes 442372
  181.1 21.9 %collective-permute-start.20 = (bf16[256,1408]{1,0:T(8,128)(2,1)S(1)}, bf16[256,1408]{1,0:T(8,128)(2,1)S(1)}, u32[]{:S(2)}, u32[]{:S(2)}) collective-permute-start(bf16[256,1408]{1,0:T(8,128)(2,1)S(1)} %get-tuple-element.169), channel_id=1, source_target_pairs={{0,2},{2,0},{4,6},{6,4},{8,10},{10,8},{12,14},{14,12},{16,18},{18,... | collective-permute-start | bytes 2162696 | tf_op jit(solution)/shard_map/ppermute | solution.py:801
  184.3 14.8 %collective-permute-start.17 = (bf16[4,128,256]{2,1,0:T(8,128)(2,1)S(1)}, bf16[4,128,256]{2,1,0:T(8,128)(2,1)S(1)}, u32[]{:S(2)}, u32[]{:S(2)}) collective-permute-start(bf16[4,128,256]{2,1,0:T(8,128)(2,1)S(1)} %get-tuple-element.167.refs_3_), channel_id=1, source_target_pairs={{8,0},{10,2},{12,4},{14,6},{16,8},{18,10},{20,12},{22,14},{24,16},... | collective-permute-start | bytes 786440 | tf_op jit(solution)/shard_map/ppermute | solution.py:807
  200.2 15.6 %collective-permute-start.18 = (bf16[4,128,256]{2,1,0:T(8,128)(2,1)S(1)}, bf16[4,128,256]{2,1,0:T(8,128)(2,1)S(1)}, u32[]{:S(2)}, u32[]{:S(2)}) collective-permute-start(bf16[4,128,256]{2,1,0:T(8,128)(2,1)S(1)} %get-tuple-element.168.refs_2_), channel_id=1, source_target_pairs={{2,0},{4,2},{6,4},{8,6},{10,8},{12,10},{14,12},{16,14},{18,16},{20... | collective-permute-start | bytes 786440 | tf_op jit(solution)/shard_map/ppermute | solution.py:807
  201.4 18.1 %collective-permute-start.19 = (bf16[4,128,256]{2,1,0:T(8,128)(2,1)S(1)}, bf16[4,128,256]{2,1,0:T(8,128)(2,1)S(1)}, u32[]{:S(2)}, u32[]{:S(2)}) collective-permute-start(bf16[4,128,256]{2,1,0:T(8,128)(2,1)S(1)} %get-tuple-element.168.refs_2_), channel_id=1, source_target_pairs={{18,0},{20,2},{22,4},{24,6},{26,8},{28,10},{30,12},{19,1},{21,3},{... | collective-permute-start | bytes 786440 | tf_op jit(solution)/shard_map/ppermute | solution.py:807
  203.1 16.4 %copy-start.37 = (bf16[4,144,128]{2,1,0:T(8,128)(2,1)S(1)}, bf16[4,144,128]{2,1,0:T(8,128)(2,1)}, u32[]{:S(2)}) copy-start(bf16[4,144,128]{2,1,0:T(8,128)(2,1)} %copy-done.36) | copy-start | bytes 442372
  203.1 16.7 %copy-start.14 = (bf16[1024,512]{1,0:T(8,128)(2,1)S(1)}, bf16[1024,512]{1,0:T(8,128)(2,1)}, u32[]{:S(2)}) copy-start(bf16[1024,512]{1,0:T(8,128)(2,1)} %copy-done.13) | copy-start | bytes 3145732
  203.1 16.7 %copy-start.20 = (bf16[2,256,512]{2,1,0:T(8,128)(2,1)S(1)}, bf16[2,256,512]{2,1,0:T(8,128)(2,1)}, u32[]{:S(2)}) copy-start(bf16[2,256,512]{2,1,0:T(8,128)(2,1)} %copy-done.19) | copy-start | bytes 1572868
  203.2 16.6 %copy-start = (bf16[1024,512]{1,0:T(8,128)(2,1)S(1)}, bf16[1024,512]{1,0:T(8,128)(2,1)}, u32[]{:S(2)}) copy-start(bf16[1024,512]{1,0:T(8,128)(2,1)} %get-tuple-element.180) | copy-start | bytes 3145732
  203.2 16.6 %copy-start.8 = (bf16[2,256,512]{2,1,0:T(8,128)(2,1)S(1)}, bf16[2,256,512]{2,1,0:T(8,128)(2,1)}, u32[]{:S(2)}) copy-start(bf16[2,256,512]{2,1,0:T(8,128)(2,1)} %copy-done.7) | copy-start | bytes 1572868
  203.3 38.2 %collective-permute-start.26 = (bf16[128,1408]{1,0:T(8,128)(2,1)S(1)}, bf16[128,1408]{1,0:T(8,128)(2,1)S(1)}, u32[]{:S(2)}, u32[]{:S(2)}) collective-permute-start(bf16[128,1408]{1,0:T(8,128)(2,1)S(1)} %get-tuple-element.187), channel_id=1, source_target_pairs={{0,4},{2,6},{4,0},{6,2},{8,12},{10,14},{12,8},{14,10},{16,20},{18,... | collective-permute-start | bytes 1081352 | tf_op jit(solution)/shard_map/ppermute | solution.py:801
  209.1 32.3 %collective-permute-start.25 = (bf16[128,1408]{1,0:T(8,128)(2,1)S(1)}, bf16[128,1408]{1,0:T(8,128)(2,1)S(1)}, u32[]{:S(2)}, u32[]{:S(2)}) collective-permute-start(bf16[128,1408]{1,0:T(8,128)(2,1)S(1)} %get-tuple-element.186), channel_id=1, source_target_pairs={{0,2},{2,0},{4,6},{6,4},{8,10},{10,8},{12,14},{14,12},{16,18},{18,... | collective-permute-start | bytes 1081352 | tf_op jit(solution)/shard_map/ppermute | solution.py:801
  209.1 32.3 %collective-permute-start.24 = (bf16[128,1408]{1,0:T(8,128)(2,1)S(1)}, bf16[128,1408]{1,0:T(8,128)(2,1)S(1)}, u32[]{:S(2)}, u32[]{:S(2)}) collective-permute-start(bf16[128,1408]{1,0:T(8,128)(2,1)S(1)} %get-tuple-element.185), channel_id=1, source_target_pairs={{0,8},{2,10},{4,12},{6,14},{8,0},{10,2},{12,4},{14,6},{16,24},{18,... | collective-permute-start | bytes 1081352 | tf_op jit(solution)/shard_map/ppermute | solution.py:801
  222.2 11.6 %copy-start.28 = (bf16[512,1024]{1,0:T(8,128)(2,1)S(1)}, bf16[512,1024]{1,0:T(8,128)(2,1)}, u32[]{:S(2)}) copy-start(bf16[512,1024]{1,0:T(8,128)(2,1)} %copy-done.27) | copy-start | bytes 3145732
  232.3 10.3 %collective-permute-start.23 = (f32[2,16,1024]{2,1,0:T(8,128)S(1)}, f32[2,16,1024]{2,1,0:T(8,128)S(1)}, u32[]{:S(2)}, u32[]{:S(2)}) collective-permute-start(f32[2,16,1024]{2,1,0:T(8,128)S(1)} %slice.25), channel_id=1, source_target_pairs={{2,0},{4,2},{6,4},{8,6},{10,8},{12,10},{14,12},{16,14},{18,16},{20... | collective-permute-start | bytes 393224 | tf_op jit(solution)/shard_map/ppermute | solution.py:807
  233.9 31.9 %collective-permute-start.28 = (bf16[512,1024]{1,0:T(8,128)(2,1)S(1)}, bf16[512,1024]{1,0:T(8,128)(2,1)S(1)}, u32[]{:S(2)}, u32[]{:S(2)}) collective-permute-start(bf16[512,1024]{1,0:T(8,128)(2,1)S(1)} %copy-done.28), channel_id=1, source_target_pairs={{0,8},{2,10},{4,12},{6,14},{8,0},{10,2},{12,4},{14,6},{16,24},{18,... | collective-permute-start | bytes 3145736 | tf_op jit(solution)/shard_map/ppermute | solution.py:801
  247.3 19.8 %collective-permute-start.27 = (bf16[2,256,1024]{2,1,0:T(8,128)(2,1)S(1)}, bf16[2,256,1024]{2,1,0:T(8,128)(2,1)S(1)}, u32[]{:S(2)}, u32[]{:S(2)}) collective-permute-start(bf16[2,256,1024]{2,1,0:T(8,128)(2,1)S(1)} %get-tuple-element.190.refs_4_.refs_1_), channel_id=1, source_target_pairs={{0,1},{1,0},{2,3},{3,2},{4,5},{5,4},{6,7},{7,6},{8,9},{9,8},{10,11... | collective-permute-start | bytes 3145736 | tf_op jit(solution)/shard_map/ppermute | solution.py:812
  248.5 22.3 %collective-permute-start.29 = (bf16[512,640]{1,0:T(8,128)(2,1)S(1)}, bf16[512,640]{1,0:T(8,128)(2,1)S(1)}, u32[]{:S(2)}, u32[]{:S(2)}) collective-permute-start(bf16[512,640]{1,0:T(8,128)(2,1)S(1)} %query_key_send.1.refs_3_), channel_id=1, source_target_pairs={{0,2},{2,0},{4,6},{6,4},{8,10},{10,8},{12,14},{14,12},{16,18},{18,... | collective-permute-start | bytes 1966088 | tf_op jit(solution)/shard_map/ppermute | solution.py:801
  249.6 22.5 %collective-permute-start.32 = (bf16[512,512]{1,0:T(8,128)(2,1)S(1)}, bf16[512,512]{1,0:T(8,128)(2,1)S(1)}, u32[]{:S(2)}, u32[]{:S(2)}) collective-permute-start(bf16[512,512]{1,0:T(8,128)(2,1)S(1)} %value_send.1.refs_6_), channel_id=1, source_target_pairs={{0,4},{2,6},{4,0},{6,2},{8,12},{10,14},{12,8},{14,10},{16,20},{18,... | collective-permute-start | bytes 1572872 | tf_op jit(solution)/shard_map/ppermute | solution.py:801
  254.7 12.4 %copy-start.55 = (f32[1,256]{1,0:T(1,128)S(1)}, f32[1,256]{1,0:T(1,128)}, u32[]{:S(2)}) copy-start(f32[1,256]{1,0:T(1,128)} %copy-done.54) | copy-start | bytes 3076
  254.7 12.5 %copy-start.10 = (bf16[2,256,1024]{2,1,0:T(8,128)(2,1)S(1)}, bf16[2,256,1024]{2,1,0:T(8,128)(2,1)}, u32[]{:S(2)}) copy-start(bf16[2,256,1024]{2,1,0:T(8,128)(2,1)} %refs_0_.1) | copy-start | bytes 3145732
  254.7 12.5 %copy-start.53 = (f32[1024]{0:T(1024)S(1)}, f32[1024]{0:T(1024)}, u32[]{:S(2)}) copy-start(f32[1024]{0:T(1024)} %param.36) | copy-start | bytes 12292
  254.7 26.6 %collective-permute-start.36 = (bf16[64,4224]{1,0:T(8,128)(2,1)S(1)}, bf16[64,4224]{1,0:T(8,128)(2,1)S(1)}, u32[]{:S(2)}, u32[]{:S(2)}) collective-permute-start(bf16[64,4224]{1,0:T(8,128)(2,1)S(1)} %get-tuple-element.206), channel_id=1, source_target_pairs={{0,16},{2,18},{4,20},{6,22},{8,24},{10,26},{12,28},{14,30},{16,0},... | collective-permute-start | bytes 1622024 | tf_op jit(solution)/shard_map/ppermute | solution.py:801
  267.0 15.4 %collective-permute-start.35 = (bf16[256,1024]{1,0:T(8,128)(2,1)S(1)}, bf16[256,1024]{1,0:T(8,128)(2,1)S(1)}, u32[]{:S(2)}, u32[]{:S(2)}) collective-permute-start(bf16[256,1024]{1,0:T(8,128)(2,1)S(1)} %get-tuple-element.205), channel_id=1, source_target_pairs={{0,2},{2,0},{4,6},{6,4},{8,10},{10,8},{12,14},{14,12},{16,18},{18,... | collective-permute-start | bytes 1572872 | tf_op jit(solution)/shard_map/ppermute | solution.py:801
  267.1 3.7 %collective-permute-start.30 = (f32[1,256]{1,0:T(1,128)S(1)}, f32[1,256]{1,0:T(1,128)S(1)}, u32[]{:S(2)}, u32[]{:S(2)}) collective-permute-start(f32[1,256]{1,0:T(1,128)S(1)} %copy-done.55), channel_id=1, source_target_pairs={{0,1},{1,0},{2,3},{3,2},{4,5},{5,4},{6,7},{7,6},{8,9},{9,8},{10,11... | collective-permute-start | bytes 3080 | tf_op jit(solution)/shard_map/ppermute | solution.py:812
  271.9 9.4 %copy-start.12 = (f32[64,4224]{1,0:T(8,128)S(1)}, f32[64,4224]{1,0:T(8,128)}, u32[]{:S(2)}) copy-start(f32[64,4224]{1,0:T(8,128)} %copy-done.11) | copy-start | bytes 3244036
  271.9 11.6 %collective-permute-start.31 = (bf16[256,640]{1,0:T(8,128)(2,1)S(1)}, bf16[256,640]{1,0:T(8,128)(2,1)S(1)}, u32[]{:S(2)}, u32[]{:S(2)}) collective-permute-start(bf16[256,640]{1,0:T(8,128)(2,1)S(1)} %get-tuple-element.202), channel_id=1, source_target_pairs={{0,4},{2,6},{4,0},{6,2},{8,12},{10,14},{12,8},{14,10},{16,20},{18,... | collective-permute-start | bytes 983048 | tf_op jit(solution)/shard_map/ppermute | solution.py:801
  273.0 10.5 %collective-permute-start.33 = (bf16[256,512]{1,0:T(8,128)(2,1)S(1)}, bf16[256,512]{1,0:T(8,128)(2,1)S(1)}, u32[]{:S(2)}, u32[]{:S(2)}) collective-permute-start(bf16[256,512]{1,0:T(8,128)(2,1)S(1)} %get-tuple-element.204), channel_id=1, source_target_pairs={{0,2},{2,0},{4,6},{6,4},{8,10},{10,8},{12,14},{14,12},{16,18},{18,... | collective-permute-start | bytes 786440 | tf_op jit(solution)/shard_map/ppermute | solution.py:801
  275.0 8.5 %collective-permute-start.34 = (f32[8,1024]{1,0:T(8,128)S(1)}, f32[8,1024]{1,0:T(8,128)S(1)}, u32[]{:S(2)}, u32[]{:S(2)}) collective-permute-start(f32[8,1024]{1,0:T(8,128)S(1)} %pack.1.refs_5_.refs_0_), channel_id=1, source_target_pairs={{0,2},{2,0},{4,6},{6,4},{8,10},{10,8},{12,14},{14,12},{16,18},{18,... | collective-permute-start | bytes 98312 | tf_op jit(solution)/shard_map/ppermute | solution.py:801
  283.7 10.1 %collective-permute-start.37 = (bf16[128,1152]{1,0:T(8,128)(2,1)S(1)}, bf16[128,1152]{1,0:T(8,128)(2,1)S(1)}, u32[]{:S(2)}, u32[]{:S(2)}) collective-permute-start(bf16[128,1152]{1,0:T(8,128)(2,1)S(1)} %get-tuple-element.210), channel_id=1, source_target_pairs={{0,8},{2,10},{4,12},{6,14},{8,0},{10,2},{12,4},{14,6},{16,24},{18,... | collective-permute-start | bytes 884744 | tf_op jit(solution)/shard_map/ppermute | solution.py:801
  285.1 8.6 %collective-permute-start.38 = (bf16[128,1024]{1,0:T(8,128)(2,1)S(1)}, bf16[128,1024]{1,0:T(8,128)(2,1)S(1)}, u32[]{:S(2)}, u32[]{:S(2)}) collective-permute-start(bf16[128,1024]{1,0:T(8,128)(2,1)S(1)} %get-tuple-element.211), channel_id=1, source_target_pairs={{0,4},{2,6},{4,0},{6,2},{8,12},{10,14},{12,8},{14,10},{16,20},{18,... | collective-permute-start | bytes 786440 | tf_op jit(solution)/shard_map/ppermute | solution.py:801
  286.9 6.9 %collective-permute-start.39 = (f32[8,1024]{1,0:T(8,128)S(1)}, f32[8,1024]{1,0:T(8,128)S(1)}, u32[]{:S(2)}, u32[]{:S(2)}) collective-permute-start(f32[8,1024]{1,0:T(8,128)S(1)} %small_sum.4.refs_4_.refs_0_), channel_id=1, source_target_pairs={{0,4},{2,6},{4,0},{6,2},{8,12},{10,14},{12,8},{14,10},{16,20},{18,... | collective-permute-start | bytes 98312 | tf_op jit(solution)/shard_map/ppermute | solution.py:801
  293.9 15.3 %collective-permute-start.40 = (bf16[64,2176]{1,0:T(8,128)(2,1)S(1)}, bf16[64,2176]{1,0:T(8,128)(2,1)S(1)}, u32[]{:S(2)}, u32[]{:S(2)}) collective-permute-start(bf16[64,2176]{1,0:T(8,128)(2,1)S(1)} %get-tuple-element.213), channel_id=1, source_target_pairs={{0,16},{2,18},{4,20},{6,22},{8,24},{10,26},{12,28},{14,30},{16,0},... | collective-permute-start | bytes 835592 | tf_op jit(solution)/shard_map/ppermute | solution.py:801
  296.4 4.5 %collective-permute-start.41 = (f32[8,1024]{1,0:T(8,128)S(1)}, f32[8,1024]{1,0:T(8,128)S(1)}, u32[]{:S(2)}, u32[]{:S(2)}) collective-permute-start(f32[8,1024]{1,0:T(8,128)S(1)} %small_sum.5.refs_4_.refs_0_), channel_id=1, source_target_pairs={{0,8},{2,10},{4,12},{6,14},{8,0},{10,2},{12,4},{14,6},{16,24},{18,... | collective-permute-start | bytes 98312 | tf_op jit(solution)/shard_map/ppermute | solution.py:801
  300.9 9.2 %collective-permute-start.42 = (f32[8,1024]{1,0:T(8,128)S(1)}, f32[8,1024]{1,0:T(8,128)S(1)}, u32[]{:S(2)}, u32[]{:S(2)}) collective-permute-start(f32[8,1024]{1,0:T(8,128)S(1)} %small_sum.6.refs_2_.refs_0_), channel_id=1, source_target_pairs={{0,16},{2,18},{4,20},{6,22},{8,24},{10,26},{12,28},{14,30},{16,0},... | collective-permute-start | bytes 98312 | tf_op jit(solution)/shard_map/ppermute | solution.py:801
  (64 other events, 156.5 us)
where the time goes:
time: 316 us; the launch traced here: 315 us
  Pallas kernels  95.2 us (30%)
  starting transfers between devices  92.3 us (29%)
  waiting for transfers between devices  91.2 us (29%)
  local copies, waits for them, and re-layouts  31.8 us (10%)
    pallas_call x9, Pallas kernels, call(): pl.pallas_call(without(body, len(operands), len(after)), grid=(seqs,), in...  68.8 us
    ppermute x15, waiting for transfers between devices, passed_along(): return lax.ppermute(block, axis, route)  55.9 us
    ppermute x23, starting transfers between devices, traded(): return lax.ppermute(block, 'seq', [(i, i ^ moved) for i in range(count)])  49.3 us
    ppermute x15, starting transfers between devices, passed_along(): return lax.ppermute(block, axis, route)  42.6 us
    ppermute x23, waiting for transfers between devices, traded(): return lax.ppermute(block, 'seq', [(i, i ^ moved) for i in range(count)])  32.5 us
    pallas_call x34, Pallas kernels, small_call(): pl.pallas_call(without(body, len(scalars) + len(arrays), len(after)), in_...  26.4 us
    unnamed x170, local copies, waits for them, and re-layouts  24.5 us
  transfers between devices with their start and end apart: 43, of which 17 were waited for; matrix products, arithmetic and copies ran while one was open for 1% of the time, Pallas kernels for 18%

commit v1 on v0

--- a/solution.py
+++ b/solution.py
@@ -20,7 +20,7 @@
 NT = ((1,), (1,))
 TN = ((0,), (0,))
 NOTE = 16
-VMEM_LIMIT = 48 * 1024 * 1024
+VMEM_LIMIT = 60 * 1024 * 1024
 SMALL_LIMIT = 20 * 1024 * 1024
 
 
@@ -82,19 +82,18 @@
     powers = [jnp.where(same, -lower, 0.0) for lower in lowers]
     inverses = [eye + power for power in powers]
     for _ in range(3):
-        powers = [dot3(power, power) for power in powers]
-        inverses = [inv + dot3(inv, power) for inv, power in zip(inverses, powers)]
+        powers = [dot(power, power) for power in powers]
+        inverses = [inv + dot(inv, power) for inv, power in zip(inverses, powers)]
     block = 16
     while block * 2 <= size:
         inside = ((rows // (2 * block)) == (cols // (2 * block))) & (
             (rows // block) != (cols // block)
         )
-        parts = [
-            dot3(jnp.where(inside, lower, 0.0), inv) for lower, inv in zip(lowers, inverses)
-        ]
-        inverses = [inv - dot3(inv, part) for inv, part in zip(inverses, parts)]
+        parts = [dot(jnp.where(inside, lower, 0.0), inv) for lower, inv in zip(lowers, inverses)]
+        inverses = [inv - dot(inv, part) for inv, part in zip(inverses, parts)]
         block *= 2
-    return inverses
+    errors = [eye - inv - dot3(lower, inv) for lower, inv in zip(lowers, inverses)]
+    return [inv + dot(inv, error) for inv, error in zip(inverses, errors)]
 
 
 def conv_pre(extended, taps):
@@ -119,14 +118,15 @@
 
 
 def first_body(
-    heads, x_ref, gain_ref, wq_ref, wk_ref, wv_ref, wg_ref, wgates_ref, bias_ref, cq_ref, ck_ref,
+    heads, halo_ref, x_ref, gain_ref, wq_ref, wk_ref, wv_ref, wg_ref, wgates_ref, bias_ref, cq_ref, ck_ref,
     cv_ref, proj_ref, pg_ref, gates_ref, sums_ref, inv_ref, mapk_ref, fresh_ref,
-    score_ref, reach_ref, local_ref, decay_ref, piece_ref, low_ref, maplow_ref, log_ref, turned_ref,
+    score_ref, reach_ref, local_ref, decay_ref, piece_ref, low_ref, maplow_ref, log_ref, mixhalo_ref, turned_ref,
 ):
-    x = x_ref[0].astype(F32)
+    x = jnp.concatenate([halo_ref[0], x_ref[0]], axis=0).astype(F32)
     mixed = x * lax.rsqrt(jnp.mean(x * x, axis=-1, keepdims=True) + 1e-06) * gain_ref[...]
     mixed = mixed.astype(BF16)
     main = mixed[HALO:]
+    mixhalo_ref[0] = mixed[:HALO]
     turned_ref[...] = jnp.transpose(main)
     proj_q = dot(mixed, wq_ref[...]).astype(BF16)
     proj_k = dot(mixed, wk_ref[...]).astype(BF16)
@@ -511,31 +511,34 @@
 
 
 def input_back_body(
-    dext_ref, edge_ref, dpg_ref, dgates_ref, wq_ref, wk_ref, wv_ref, wg_ref, wgates_ref,
-    dqk_ref, dv_ref, dmixed_ref,
+    dext_ref, dpg_ref, dgates_ref, wq_ref, wk_ref, wv_ref, wg_ref, wgates_ref, dqk_ref, dv_ref,
+    dqkhalo_ref, dvhalo_ref, dmixed_ref, dhalo_ref,
 ):
     wide = wq_ref.shape[1]
-    own = dext_ref[0, HALO:]
-    size = own.shape[0]
-    d_proj = jnp.concatenate([own[: size - HALO], own[size - HALO :] + edge_ref[0]], axis=0)
-    d_proj = d_proj.astype(BF16)
-    dqk_ref[0] = d_proj[:, : 2 * wide]
-    dv_ref[0] = d_proj[:, 2 * wide :]
+    d_proj = dext_ref[0].astype(BF16)
+    dqk_ref[0] = d_proj[HALO:, : 2 * wide]
+    dv_ref[0] = d_proj[HALO:, 2 * wide :]
+    dqkhalo_ref[0] = d_proj[:HALO, : 2 * wide]
+    dvhalo_ref[0] = d_proj[:HALO, 2 * wide :]
     d_mixed = dot(d_proj[:, :wide], wq_ref[...], NT)
     d_mixed = d_mixed + dot(d_proj[:, wide : 2 * wide], wk_ref[...], NT)
     d_mixed = d_mixed + dot(d_proj[:, 2 * wide :], wv_ref[...], NT)
-    d_mixed = d_mixed + dot(dpg_ref[0], wg_ref[...], NT)
-    d_mixed = d_mixed + dot(dgates_ref[0], wgates_ref[...], NT)
-    dmixed_ref[0] = d_mixed.astype(BF16)
+    dhalo_ref[0] = d_mixed[:HALO].astype(BF16)
+    main = d_mixed[HALO:] + dot(dpg_ref[0], wg_ref[...], NT)
+    main = main + dot(dgates_ref[0], wgates_ref[...], NT)
+    dmixed_ref[0] = main.astype(BF16)
 
 
 def last_body(
-    x_ref, mine_ref, other_ref, dresid_ref, gain_ref, grad_ref, dgain_ref,
+    x_ref, mine_ref, other_ref, halo_ref, halo_other_ref, dresid_ref, gain_ref, grad_ref, dgain_ref,
 ):
     x = x_ref[0].astype(F32)
     inverse = lax.rsqrt(jnp.mean(x * x, axis=-1, keepdims=True) + 1e-06)
     unit_x = x * inverse
     d_mixed = mine_ref[0].astype(F32) + other_ref[0].astype(F32)
+    halo = halo_ref[0].astype(F32) + halo_other_ref[0].astype(F32)
+    size = d_mixed.shape[0]
+    d_mixed = jnp.concatenate([d_mixed[: size - HALO], d_mixed[size - HALO :] + halo], axis=0)
     d_unit = d_mixed * gain_ref[...]
     back = inverse * (d_unit - unit_x * jnp.mean(d_unit * unit_x, axis=-1, keepdims=True))
     grad_ref[0] = dresid_ref[0] + back
@@ -558,31 +561,32 @@
 
 def held_rows(left_refs, index_ref, first, blocks, held):
     share = left_refs[0].shape[1]
-    for number, left_ref in enumerate(left_refs):
+    for left_ref, held_ref in zip(left_refs, held):
         for place in range(blocks):
-            held[number, place * share : (place + 1) * share] = left_ref[index_ref[first + place]]
-
-
-def send_body(terms, first, blocks, lefts, index_ref, *refs):
-    out_ref, held = refs[-2:]
+            held_ref[place * share : (place + 1) * share] = left_ref[index_ref[first + place]]
+
+
+def send_body(terms, first, blocks, lefts, rights, index_ref, *refs):
+    out_ref, held = refs[lefts + rights], refs[lefts + rights + 1 :]
     held_rows(refs[:lefts], index_ref, first, blocks, held)
     at = 0
-    for left, right, width in terms:
-        out_ref[:, at : at + width] = dot(held[left], refs[lefts + right][...]).astype(BF16)
+    for factors, width in terms:
+        total = sum(dot(held[left][...], refs[lefts + right][...]) for left, right in factors)
+        out_ref[:, at : at + width] = total.astype(BF16)
         at += width
 
 
-def keep_body(terms, blocks, parts, lefts, index_ref, *refs):
-    rights = len(terms)
-    got_ref = refs[lefts + rights]
-    keep_ref, held = refs[lefts + rights + 1], refs[-1]
-    send_refs = refs[lefts + rights + 2 : -1]
+def keep_body(terms, blocks, parts, lefts, rights, index_ref, *refs):
+    got_ref, keep_ref = refs[lefts + rights], refs[lefts + rights + 1]
+    send_refs = refs[lefts + rights + 2 : lefts + rights + 1 + parts]
+    held = refs[lefts + rights + 1 + parts :]
     held_rows(refs[:lefts], index_ref, 0, blocks, held)
     rows = keep_ref.shape[0]
     at = 0
-    for left, right, width in terms:
-        total = dot(held[left], refs[lefts + right][...])
-        total = total + got_ref[:, at : at + width].astype(F32)
+    for factors, width in terms:
+        total = got_ref[:, at : at + width].astype(F32)
+        for left, right in factors:
+            total = total + dot(held[left][...], refs[lefts + right][...])
         keep_ref[:, at : at + width] = total[:rows]
         for part in range(1, parts):
             send_refs[part - 1][:, at : at + width] = total[part * rows : (part + 1) * rows].astype(BF16)
@@ -630,6 +634,24 @@
     out_ref[5:6] = ffn_ref[...]
     out_ref[6:7] = mix_ref[...]
     out_ref[7:8, :DV] = ogain_ref[...] + other_ref[...]
+
+
+def unpack_body(heads, count, start_ref, *refs):
+    total = refs[0][...]
+    for ref in refs[1:count]:
+        total = total + ref[...]
+    tapq_ref, tapk_ref, tapv_ref, bias_ref, ogain_ref, gains_ref = refs[count:]
+    wide = tapq_ref.shape[1]
+    share = gains_ref.shape[1]
+    tapq_ref[...] = total[:CONV, :wide]
+    tapk_ref[...] = total[:CONV, wide : 2 * wide]
+    tapv_ref[...] = total[:CONV, 2 * wide :]
+    for row in range(2):
+        bias_ref[row : row + 1] = total[4:5, row * heads : (row + 1) * heads]
+    ogain_ref[...] = total[7:8, : ogain_ref.shape[1]]
+    width = total.shape[1]
+    turned = pltpu.roll(total, lax.rem(width - start_ref[0], width), 1)
+    gains_ref[...] = turned[5:7, :share]
 
 
 def sum_body(count, *refs):
@@ -701,8 +723,8 @@
         self.steps = steps
         self.index = block_index(order, me)
         self.count = 1 << len(order)
-        _, self.share, self.tokens = lefts[0].shape
-        self.columns = sum(width for _, _, width in terms)
+        self.share, self.tokens = lefts[0].shape[1:]
+        self.columns = sum(width for _, width in terms)
         self.done = 0
 
     def trade(self, sends):
@@ -720,7 +742,7 @@
         return small_call(
             body, self.name + suffix, list(self.lefts) + list(self.rights) + extra, outs, after,
             scalars=[self.index],
-            scratch=[pltpu.VMEM((len(self.lefts), blocks * self.share, self.tokens), BF16)],
+            scratch=[pltpu.VMEM((blocks * self.share, left.shape[2]), BF16) for left in self.lefts],
             flops=2 * blocks * self.share * self.tokens * self.columns,
         )
 
@@ -732,7 +754,9 @@
 
     def send(self, *after):
         blocks = self.count // 2
-        body = functools.partial(send_body, self.terms, blocks, blocks, len(self.lefts))
+        body = functools.partial(
+            send_body, self.terms, blocks, blocks, len(self.lefts), len(self.rights)
+        )
         rows = blocks * self.share
         sends = self.multiplied(body, "_send", [], [((rows, self.columns), BF16)], after)
         self.trade(sends)
@@ -741,7 +765,9 @@
     def keep(self, *after):
         blocks = self.count // 2
         parts, outs = self.outs(blocks * self.share)
-        body = functools.partial(keep_body, self.terms, blocks, parts, len(self.lefts))
+        body = functools.partial(
+            keep_body, self.terms, blocks, parts, len(self.lefts), len(self.rights)
+        )
         self.kept, *sends = self.multiplied(body, "_keep", self.gots, outs, after)
         self.trade(sends)
         return self.kept
@@ -826,7 +852,6 @@
     proj_wide = 2 * wide + out_wide
 
     halo = passed_along(tokens[:, size - HALO :], "seq", 1)
-    x_ext = jnp.concatenate([halo, tokens], axis=1)
     gates_w = jnp.swapaxes(w_gates, 0, 1).reshape(width, 2 * heads)
     gates_w = jnp.pad(gates_w, ((0, 0), (0, LANES - 2 * heads)))
     bias = jnp.pad(gate_bias.reshape(1, 2 * heads), ((0, 0), (0, LANES - 2 * heads)))
@@ -850,9 +875,9 @@
 
     (
         proj, proj_g, gates, sums, inv, mapk, fresh, score, reach, local, decay, piece, low,
-        map_low, log, mixed_t,
+        map_low, log, mixed_halo, mixed_t,
     ) = call(
-        functools.partial(first_body, heads), "project_and_local", seqs, [x_ext],
+        functools.partial(first_body, heads), "project_and_local", seqs, [halo, tokens],
         [mix_row, w_query, w_key, w_value, w_outgate, gates_w, bias, conv_query, conv_key, conv_value],
         [
             ((seqs, size + HALO, proj_wide), BF16),
@@ -861,6 +886,7 @@
             (by_value, F32), (square, F32), ((seqs, heads, DK, DK + DV), F32),
             ((seqs, heads, DK + NOTE, DK + DV), BF16),
             ((seqs, heads, DK + NOTE, DK), BF16), ((seqs, heads, 8, LANES), F32),
+            ((seqs, HALO, width), BF16),
         ],
         turned=[(turned_shape, BF16)],
         flops=1e10,
@@ -923,9 +949,9 @@
     down_other = swapped(down)
 
     normed_b, cot_b, mixed_b = in_blocks(normed_t), in_blocks(cot_t), in_blocks(mixed_t)
-    gate_sum = Halved("gate", steps_x, me, [normed_b], [flat(d_gate)], ((0, 0, units),))
-    up_sum = Halved("up", steps_yzx, me, [normed_b], [flat(d_up)], ((0, 0, units),))
-    down_sum = Halved("down", steps_zxy, me, [cot_b], [flat(hidden)], ((0, 0, units),))
+    gate_sum = Halved("gate", steps_x, me, [normed_b], [flat(d_gate)], ((((0, 0),), units),))
+    up_sum = Halved("up", steps_yzx, me, [normed_b], [flat(d_up)], ((((0, 0),), units),))
+    down_sum = Halved("down", steps_zxy, me, [cot_b], [flat(hidden)], ((((0, 0),), units),))
     done = down_sum.send(up_sum.send(gate_sum.send()))
 
     d_resid, d_out, d_pg, back, low, d_attn_t, d_ffn_gain, d_out_gain = call(
@@ -945,7 +971,7 @@
 
     outs_sum = Halved(
         "outs", steps_zxy, me, [in_blocks(d_attn_t), mixed_b], [flat(gated), flat(d_pg)],
-        ((0, 0, out_wide), (1, 1, out_wide)),
+        ((((0, 0),), out_wide), (((1, 1),), out_wide)),
     )
     back = back.reshape(state_shape)
     low = low.reshape(state_shape)
@@ -980,7 +1006,6 @@
         functools.partial(exit_body, pairs), "exit", [near_map, near, far], [(state_shape, F32)],
         after=[done],
     )
-    done = outs_sum.send(d_end)
     d_end = d_end.reshape(seqs, heads, DK, DV)
     d_ext, d_gates, dtap_kv, d_bias = call(
         functools.partial(late_body, heads), "delta_back_late", seqs,
@@ -990,31 +1015,41 @@
         [conv_key, conv_value],
         [((seqs, size + HALO, proj_wide), F32), ((seqs, size, LANES), BF16)],
         [((CONV, wide + out_wide), F32), ((1, LANES), F32)],
-        after=[done],
         flops=3e9,
     )
-    edges = passed_along(d_ext[:, :HALO], "seq", -1)
-    feed_sum = joined("feed_last", [gate_sum, up_sum, down_sum], d_bias)
+    done = outs_sum.send(d_bias)
+    feed_sum = joined("feed_last", [gate_sum, up_sum, down_sum], done)
     done = feed_sum.kept
-    d_qk, d_v, d_mixed = call(
-        input_back_body, "input_back", seqs, [d_ext, edges, d_pg, d_gates],
+    d_qk, d_v, d_qk_halo, d_v_halo, d_mixed, d_halo = call(
+        input_back_body, "input_back", seqs, [d_ext, d_pg, d_gates],
         [w_query, w_key, w_value, w_outgate, gates_w],
         [
             ((seqs, size, 2 * wide), BF16), ((seqs, size, out_wide), BF16),
-            ((seqs, size, width), BF16),
+            ((seqs, HALO, 2 * wide), BF16), ((seqs, HALO, out_wide), BF16),
+            ((seqs, size, width), BF16), ((seqs, HALO, width), BF16),
         ],
         after=[done],
         flops=1.7e9,
     )
     d_mixed_other = swapped(d_mixed)
+    halo_rows = seqs * HALO
+    halo_b = jnp.swapaxes(mixed_halo.reshape(halo_rows, width), 0, 1).reshape(count, share, halo_rows)
     query_sum = Halved(
-        "query_key", steps_x, me, [mixed_b], [flat(d_qk), flat(d_gates)],
-        ((0, 0, 2 * wide), (0, 1, LANES)),
-    )
-    value_sum = Halved("value", steps_y, me, [mixed_b], [flat(d_v)], ((0, 0, out_wide),))
-    done = outs_sum.keep(value_sum.send(query_sum.send(d_mixed)))
+        "query_key", steps_x, me, [mixed_b, halo_b],
+        [flat(d_qk), d_qk_halo.reshape(halo_rows, 2 * wide), flat(d_gates)],
+        ((((0, 0), (1, 1)), 2 * wide), (((0, 2),), LANES)),
+    )
+    value_sum = Halved(
+        "value", steps_y, me, [mixed_b, halo_b],
+        [flat(d_v), d_v_halo.reshape(halo_rows, out_wide)], ((((0, 0), (1, 1)), out_wide),),
+    )
+    done = value_sum.send(query_sum.send(d_mixed))
+    done = value_sum.keep(query_sum.keep(outs_sum.keep(done)))
+    halo_grad = passed_along(d_halo, "seq", -1)
+    halo_other = swapped(halo_grad)
     grad_input, d_mix_gain = call(
-        last_body, "first_norm_back", seqs, [tokens, d_mixed, d_mixed_other, d_resid], [mix_row],
+        last_body, "first_norm_back", seqs,
+        [tokens, d_mixed, d_mixed_other, halo_grad, halo_other, d_resid], [mix_row],
         [((seqs, size, width), F32)], [((1, width), F32)], after=[done],
     )
 
@@ -1029,31 +1064,42 @@
             done = group.add(done)
         return group.total(cuts, done)
 
-    def small_step(bit, done):
+    def small_others(bits):
+        return [
+            traded(small, sum(((part >> place) & 1) << bit for place, bit in enumerate(bits)))
+            for part in range(1, 1 << len(bits))
+        ]
+
+    def small_step(bits, done):
+        others = small_others(bits)
         return small_call(
-            functools.partial(sum_body, 2), "small_sum", [small, traded(small, 1 << bit)],
+            functools.partial(sum_body, 1 + len(others)), "small_sum", [small] + others,
             [(small.shape, F32)], after=[done], flops=1e4,
         )[0]
 
-    bits = [step[0] for step in steps_x]
-    done = value_sum.keep(query_sum.keep(small))
+    bits = [[0], [1]] + [[b for step in steps_x[at : at + 2] for b in step] for at in range(2, len(steps_x), 2)]
+    done = small = small_step(bits.pop(0), small)
+    ins_sum = joined("ins_join", [query_sum, value_sum], done)
+    done = outs_sum.add(ins_sum.kept)
     grad_gate, grad_up, grad_down = finish(feed_sum, [units] * 3, done)
-    done = outs_sum.add(grad_gate)
-    done = small = small_step(bits.pop(0), done)
-    ins_sum = joined("ins_join", [query_sum, value_sum], done)
-    done = small = small_step(bits.pop(0), ins_sum.kept)
+    done = small = small_step(bits.pop(0), grad_gate)
     ins_sum = joined("ins_last", [ins_sum, outs_sum], done)
-    done = small = small_step(bits.pop(0), ins_sum.kept)
+    while len(bits) > 1:
+        small = small_step(bits.pop(0), ins_sum.kept)
+    others = small_others(bits.pop(0))
+    tap_shape = (CONV, wide)
+    taps_q, taps_k, taps_v, grad_bias, gain_out, gains = small_call(
+        functools.partial(unpack_body, heads, 1 + len(others)), "unpack", [small] + others,
+        [
+            (tap_shape, F32), (tap_shape, F32), ((CONV, out_wide), F32), ((2, heads), F32),
+            ((1, DV), F32), ((2, share), F32),
+        ],
+        after=[ins_sum.kept], scalars=[(me * share).astype(jnp.int32).reshape(1)], flops=1e4,
+    )
     grad_query, grad_key, grad_gates, grad_value, grad_out, grad_outgate = finish(
-        ins_sum, [wide, wide, LANES, out_wide, out_wide, out_wide], done
-    )
-    done = grad_query
-    while bits:
-        done = small = small_step(bits.pop(0), done)
+        ins_sum, [wide, wide, LANES, out_wide, out_wide, out_wide], gains
+    )
     grad_gates = grad_gates[:, : 2 * heads].reshape(share, 2, heads)
-
-    def mine_of(row):
-        return lax.dynamic_slice(small, (row, me * share), (1, share)).reshape(share)
 
     return (
         result,
@@ -1063,14 +1109,14 @@
         grad_value,
         grad_outgate,
         jnp.swapaxes(grad_gates, 0, 1),
-        small[4, : 2 * heads].reshape(2, heads),
-        small[:CONV, :wide],
-        small[:CONV, wide : 2 * wide],
-        small[:CONV, 2 * wide : proj_wide],
-        small[7, :DV],
+        grad_bias,
+        taps_q,
+        taps_k,
+        taps_v,
+        gain_out.reshape(DV),
         jnp.swapaxes(grad_out, 0, 1),
-        mine_of(6),
-        mine_of(5),
+        gains[1],
+        gains[0],
         grad_gate,
         grad_up,
         jnp.swapaxes(grad_down, 0, 1),

time: 316 us -> 343 us (1.085)
  Pallas kernels: 95.2 us -> 114 us
  waiting for transfers between devices: 91.2 us -> 102 us
    ppermute x15, waiting for transfers between devices: 55.9 us -> 70 us  [passed_along(): return lax.ppermute(block, axis, route)]
    pallas_call x34 -> x33, Pallas kernels: 26.4 us -> 38 us  [small_call(): pl.pallas_call(without(body, len(scalars) + len(arrays), len(after)), in_...]
    pallas_call x9, Pallas kernels: 68.8 us -> 76.1 us  [call(): pl.pallas_call(without(body, len(operands), len(after)), grid=(seqs,), in...]
    ppermute x23 -> x24, starting transfers between devices: 49.3 us -> 54.1 us  [traded(): return lax.ppermute(block, 'seq', [(i, i ^ moved) for i in range(count)])]
    ppermute x23 -> x24, waiting for transfers between devices: 32.5 us -> 28.9 us  [traded(): return lax.ppermute(block, 'seq', [(i, i ^ moved) for i in range(count)])]
    unnamed x170 -> x132, local copies, waits for them, and re-layouts: 24.5 us -> 24.2 us
  transfers between devices with their start and end apart: 43 -> 45, of which waited for: 17 -> 18; matrix products, arithmetic and copies ran while one was open for 1% -> 1% of each run, Pallas kernels for 18% -> 21%
where the time goes in v1:
time: 343 us; the launch traced here: 342 us
  Pallas kernels  114 us (33%)
  waiting for transfers between devices  102 us (30%)
  starting transfers between devices  95.1 us (28%)
  local copies, waits for them, and re-layouts  29.3 us (9%)
    pallas_call x9, Pallas kernels, call(): pl.pallas_call(without(body, len(operands), len(after)), grid=(seqs,), in...  76.1 us
    ppermute x15, waiting for transfers between devices, passed_along(): return lax.ppermute(block, axis, route)  70 us
    ppermute x24, starting transfers between devices, traded(): return lax.ppermute(block, 'seq', [(i, i ^ moved) for i in range(count)])  54.1 us
    ppermute x15, starting transfers between devices, passed_along(): return lax.ppermute(block, axis, route)  40.3 us
    pallas_call x33, Pallas kernels, small_call(): pl.pallas_call(without(body, len(scalars) + len(arrays), len(after)), in_...  38 us
    ppermute x24, waiting for transfers between devices, traded(): return lax.ppermute(block, 'seq', [(i, i ^ moved) for i in range(count)])  28.9 us
    unnamed x132, local copies, waits for them, and re-layouts  24.2 us
  transfers between devices with their start and end apart: 45, of which 18 were waited for; matrix products, arithmetic and copies ran while one was open for 1% of the time, Pallas kernels for 21%

profile of v1, /device:TPU:0, one launch (start us, length us, event | category | flops | bytes accessed | tf_op | source)
XLA Modules:
  0.0 341.7 jit_solution(13140850954850528121)
XLA Ops:
  1.5 4.8 %collective-permute-start = (bf16[2,16,1024]{2,1,0:T(8,128)(2,1)S(1)}, bf16[2,16,1024]{2,1,0:T(8,128)(2,1)S(1)}, u32[]{:S(2)}, u32[]{:S(2)}) collective-permute-start(bf16[2,16,1024]{2,1,0:T(8,128)(2,1)S(1)} %slice.12), channel_id=1, source_target_pairs={{0,2},{2,4},{4,6},{6,8},{8,10},{10,12},{12,14},{14,16},{16,18},{18... | collective-permute-start | bytes 196616 | tf_op jit(solution)/shard_map/ppermute | solution.py:833
  9.9 16.0 %project_and_local.1 = (bf16[2,272,1024]{2,1,0:T(8,128)(2,1)}, f32[2,256,512]{2,1,0:T(8,128)}, f32[2,256,128]{2,1,0:T(8,128)}, f32[2,256,128]{2,1,0:T(8,128)}, f...) custom-call(bf16[2,16,1024]{2,1,0:T(8,128)(2,1)} %copy-done.61, ...), custom_call_target="tpu_custom_call" | custom-call | flops 10000000000 | bytes 16028160 | tf_op jit(solution)/shard_map/project_and_local/pallas_call | solution.py:686
  26.0 3.4 collective-permute-start.1
  29.4 9.4 %collective-permute-done.1.got_ref = bf16[4,144,384]{2,1,0:T(8,128)(2,1)S(1)} collective-permute-done((bf16[4,144,384]{2,1,0:T(8,128)(2,1)}, bf16[4,144,384]{2,1,0:T(8,128)(2,1)S(1)}, u32[]{:S(2)}, u32[]{:S(2)}) %collective-permute-start.1) | collective-permute-done | bytes 442400 | tf_op jit(solution)/shard_map/ppermute | solution.py:833
  41.0 5.2 %collective-permute-start.2 = (bf16[4,144,384]{2,1,0:T(8,128)(2,1)S(1)}, bf16[4,144,384]{2,1,0:T(8,128)(2,1)S(1)}, u32[]{:S(2)}, u32[]{:S(2)}) collective-permute-start(bf16[4,144,384]{2,1,0:T(8,128)(2,1)S(1)} %get-tuple-element.135), channel_id=1, source_target_pairs={{0,4},{2,6},{4,8},{6,10},{8,12},{10,14},{12,16},{14,18},{16,20},{1... | collective-permute-start | bytes 1327112 | tf_op jit(solution)/shard_map/ppermute | solution.py:833
  46.3 7.5 %collective-permute-done.2.got_ref = bf16[4,144,384]{2,1,0:T(8,128)(2,1)S(1)} collective-permute-done((bf16[4,144,384]{2,1,0:T(8,128)(2,1)S(1)}, bf16[4,144,384]{2,1,0:T(8,128)(2,1)S(1)}, u32[]{:S(2)}, u32[]{:S(2)}) %collective-permute-start.2) | collective-permute-done | bytes 442400 | tf_op jit(solution)/shard_map/ppermute | solution.py:833
  54.1 6.8 %collective-permute-start.3 = (bf16[4,144,384]{2,1,0:T(8,128)(2,1)S(1)}, bf16[4,144,384]{2,1,0:T(8,128)(2,1)S(1)}, u32[]{:S(2)}, u32[]{:S(2)}) collective-permute-start(bf16[4,144,384]{2,1,0:T(8,128)(2,1)S(1)} %get-tuple-element.138), channel_id=1, source_target_pairs={{0,8},{2,10},{4,12},{6,14},{8,16},{10,18},{12,20},{14,22},{16,24},... | collective-permute-start | bytes 1327112 | tf_op jit(solution)/shard_map/ppermute | solution.py:833
  60.9 6.4 %collective-permute-done.3.got_ref = bf16[4,144,384]{2,1,0:T(8,128)(2,1)S(1)} collective-permute-done((bf16[4,144,384]{2,1,0:T(8,128)(2,1)S(1)}, bf16[4,144,384]{2,1,0:T(8,128)(2,1)S(1)}, u32[]{:S(2)}, u32[]{:S(2)}) %collective-permute-start.3) | collective-permute-done | bytes 442400 | tf_op jit(solution)/shard_map/ppermute | solution.py:833
  68.6 2.4 collective-permute-start.4
  71.0 5.5 %collective-permute-start.5 = (bf16[4,128,256]{2,1,0:T(8,128)(2,1)S(1)}, bf16[4,128,256]{2,1,0:T(8,128)(2,1)S(1)}, u32[]{:S(2)}, u32[]{:S(2)}) collective-permute-start(bf16[4,128,256]{2,1,0:T(8,128)(2,1)S(1)} %get-tuple-element.140), channel_id=1, source_target_pairs={{0,18},{2,20},{4,22},{6,24},{8,26},{10,28},{12,30},{1,19},{3,21},{... | collective-permute-start | bytes 786440 | tf_op jit(solution)/shard_map/ppermute | solution.py:833
  76.5 1.3 collective-permute-start.7
  77.8 1.3 collective-permute-start.8
  79.1 1.5 collective-permute-start.6
  82.2 2.7 collective-permute-done.7.refs_9_.refs_0_
  85.0 3.3 collective-permute-done.8.refs_10_.refs_0_
  88.2 2.6 collective-permute-done.6.refs_8_.refs_0_
  91.5 4.9 %mixer_out.1 = (f32[2,2,256,256]{3,2,1,0:T(8,128)}, f32[2,256,512]{2,1,0:T(8,128)}, bf16[2,256,512]{2,1,0:T(8,128)(2,1)}, bf16[2,256,1024]{2,1,0:T(8,128)(2,1)}) custom-call(f32[2,2,128,256]{3,2,1,0:T(8,128)} %bitcast.72, f32[2,2,256,256]{3,2,1,0:T(8,128)} %get-tuple-element.141.refs_1_, f32[2,2,256,128]{3,2,1,0:T(8,128)} %get-tuple-element.142.refs_2_, ...), custom_call_target="tpu_custom_call" | custom-call | flops 1500000000 | bytes 9438208 | tf_op jit(solution)/shard_map/mixer_out/pallas_call | solution.py:686
  96.5 2.8 collective-permute-done.9.other_ref
  100.3 17.2 %feed_forward.1 = (f32[2,256,1024]{2,1,0:T(8,128)}, bf16[2,256,1408]{2,1,0:T(8,128)(2,1)}, bf16[2,256,1408]{2,1,0:T(8,128)(2,1)}, bf16[2,256,1408]{2,1,0:T(8,128...) custom-call(bf16[2,256,1024]{2,1,0:T(8,128)(2,1)} %refs_0_.1, ...), custom_call_target="tpu_custom_call" | custom-call | flops 12000000000 | bytes 23465984 | tf_op jit(solution)/shard_map/feed_forward/pallas_call | solution.py:686
  119.0 1.4 copy-done.4
  120.3 2.7 gate_send.1.refs_3_
  124.2 2.6 up_send.1.refs_3_
  126.8 1.7 collective-permute-start.15
  128.5 1.5 down_send.1.refs_10_
  130.0 2.9 collective-permute-start.14
  133.9 7.3 %mixer_back.1 = (f32[2,256,1024]{2,1,0:T(8,128)}, f32[2,256,512]{2,1,0:T(8,128)}, bf16[2,256,512]{2,1,0:T(8,128)(2,1)}, f32[2,2,128,256]{3,2,1,0:T(8,128)}, bf16...) custom-call(f32[2,256,1024]{2,1,0:T(8,128)} %get-tuple-element.150.refs_0_, ...), custom_call_target="tpu_custom_call" | custom-call | flops 1500000000 | bytes 14428160 | tf_op jit(solution)/shard_map/mixer_back/pallas_call | solution.py:686
  141.2 1.5 collective-permute-start.12
  142.7 7.2 %delta_back_early.1 = (f32[2,2,256,256]{3,2,1,0:T(8,128)}, f32[2,2,256,128]{3,2,1,0:T(8,128)}, f32[2,2,256,128]{3,2,1,0:T(8,128)}, f32[2,256,128]{2,1,0:T(8,128)...) custom-call(bf16[2,272,1024]{2,1,0:T(8,128)(2,1)} %get-tuple-element.152.proj_ref, ...), custom_call_target="tpu_custom_call" | custom-call | flops 3000000000 | bytes 10334208 | tf_op jit(solution)/shard_map/delta_back_early/pallas_call | solution.py:686
  149.9 3.2 result.1.refs_3_
  153.2 9.6 %collective-permute-done.12.refs_2_ = bf16[4,128,256]{2,1,0:T(8,128)(2,1)} collective-permute-done((bf16[4,128,256]{2,1,0:T(8,128)(2,1)}, bf16[4,128,256]{2,1,0:T(8,128)(2,1)}, u32[]{:S(2)}, u32[]{:S(2)}) %collective-permute-start.12) | collective-permute-done | bytes 262176 | tf_op jit(solution)/shard_map/ppermute | solution.py:833
  166.3 1.4 collective-permute-start.13
  167.7 2.4 gate_keep.1
  170.1 2.7 collective-permute-start.22
  172.8 2.5 up_keep.1
  175.3 7.0 %collective-permute-start.21 = (bf16[256,1408]{1,0:T(8,128)(2,1)S(1)}, bf16[256,1408]{1,0:T(8,128)(2,1)S(1)}, u32[]{:S(2)}, u32[]{:S(2)}) collective-permute-start(bf16[256,1408]{1,0:T(8,128)(2,1)S(1)} %get-tuple-element.180), channel_id=1, source_target_pairs={{0,8},{2,10},{4,12},{6,14},{8,0},{10,2},{12,4},{14,6},{16,24},{18,... | collective-permute-start | bytes 2162696 | tf_op jit(solution)/shard_map/ppermute | solution.py:827
  182.3 2.4 down_keep.1
  184.7 2.9 collective-permute-start.20
  187.9 1.3 collective-permute-start.17
  189.2 13.7 %collective-permute-done.17.refs_2_ = bf16[4,128,256]{2,1,0:T(8,128)(2,1)S(1)} collective-permute-done((bf16[4,128,256]{2,1,0:T(8,128)(2,1)S(1)}, bf16[4,128,256]{2,1,0:T(8,128)(2,1)S(1)}, u32[]{:S(2)}, u32[]{:S(2)}) %collective-permute-start.17) | collective-permute-done | bytes 262176 | tf_op jit(solution)/shard_map/ppermute | solution.py:833
  205.2 1.3 collective-permute-start.19
  209.4 5.8 %collective-permute-start.25 = (bf16[128,1408]{1,0:T(8,128)(2,1)}, bf16[128,1408]{1,0:T(8,128)(2,1)}, u32[]{:S(2)}, u32[]{:S(2)}) collective-permute-start(bf16[128,1408]{1,0:T(8,128)(2,1)} %get-tuple-element.194), channel_id=1, source_target_pairs={{0,4},{2,6},{4,0},{6,2},{8,12},{10,14},{12,8},{14,10},{16,20},{18,... | collective-permute-start | bytes 1081352 | tf_op jit(solution)/shard_map/ppermute | solution.py:827
  215.8 6.6 %collective-permute-done.18.refs_1_ = bf16[4,128,256]{2,1,0:T(8,128)(2,1)S(1)} collective-permute-done((bf16[4,128,256]{2,1,0:T(8,128)(2,1)S(1)}, bf16[4,128,256]{2,1,0:T(8,128)(2,1)S(1)}, u32[]{:S(2)}, u32[]{:S(2)}) %collective-permute-start.18) | collective-permute-done | bytes 262176 | tf_op jit(solution)/shard_map/ppermute | solution.py:833
  223.5 10.4 %delta_back_late.1 = (f32[2,272,1024]{2,1,0:T(8,128)}, bf16[2,256,128]{2,1,0:T(8,128)(2,1)}, f32[4,768]{1,0:T(4,128)}, f32[1,128]{1,0:T(1,128)}) custom-call(bf16[2,272,1024]{2,1,0:T(8,128)(2,1)} %get-tuple-element.152.proj_ref, f32[2,256,128]{2,1,0:T(8,128)} %get-tuple-element.153.gates_ref, f32[2,256,128]{2,1,0:T(8,128)} %get-tuple-element.154.sums_ref, ...), custom_call_target="tpu_custom_call" | custom-call | flops 3000000000 | bytes 10084864 | tf_op jit(solution)/shard_map/delta_back_late/pallas_call | solution.py:686
  241.4 2.1 feed_last.1
  244.5 5.7 %input_back.1 = (bf16[2,256,512]{2,1,0:T(8,128)(2,1)}, bf16[2,256,512]{2,1,0:T(8,128)(2,1)}, bf16[2,16,512]{2,1,0:T(8,128)(2,1)}, bf16[2,16,512]{2,1,0:T(8,128)(...) custom-call(f32[2,272,1024]{2,1,0:T(8,128)} %get-tuple-element.189.refs_0_, ...), custom_call_target="tpu_custom_call" | custom-call | flops 1700000000 | bytes 8519680 | tf_op jit(solution)/shard_map/input_back/pallas_call | solution.py:686
  254.5 2.4 collective-permute-start.30
  258.1 2.9 collective-permute-start.29
  261.0 2.8 outs_keep.1
  263.8 4.1 %collective-permute-start.37 = (bf16[256,1024]{1,0:T(8,128)(2,1)}, bf16[256,1024]{1,0:T(8,128)(2,1)}, u32[]{:S(2)}, u32[]{:S(2)}) collective-permute-start(bf16[256,1024]{1,0:T(8,128)(2,1)} %get-tuple-element.221), channel_id=1, source_target_pairs={{0,2},{2,0},{4,6},{6,4},{8,10},{10,8},{12,14},{14,12},{16,18},{18,... | collective-permute-start | bytes 1572872 | tf_op jit(solution)/shard_map/ppermute | solution.py:827
  269.2 3.3 collective-permute-done.30.refs_6_
  272.6 2.0 query_key_keep.1
  274.5 2.8 collective-permute-start.32
  277.4 7.6 %collective-permute-done.27.refs_3_ = bf16[2,16,1024]{2,1,0:T(8,128)(2,1)S(1)} collective-permute-done((bf16[2,16,1024]{2,1,0:T(8,128)(2,1)S(1)}, bf16[2,16,1024]{2,1,0:T(8,128)(2,1)S(1)}, u32[]{:S(2)}, u32[]{:S(2)}) %collective-permute-start.27) | collective-permute-done | bytes 65568 | tf_op jit(solution)/shard_map/ppermute | solution.py:833
  286.9 4.0 %collective-permute-start.33 = (bf16[256,512]{1,0:T(8,128)(2,1)S(1)}, bf16[256,512]{1,0:T(8,128)(2,1)S(1)}, u32[]{:S(2)}, u32[]{:S(2)}) collective-permute-start(bf16[256,512]{1,0:T(8,128)(2,1)S(1)} %get-tuple-element.213), channel_id=1, source_target_pairs={{0,2},{2,0},{4,6},{6,4},{8,10},{10,8},{12,14},{14,12},{16,18},{18,... | collective-permute-start | bytes 786440 | tf_op jit(solution)/shard_map/ppermute | solution.py:827
  292.1 4.3 %first_norm_back.1 = (f32[2,256,1024]{2,1,0:T(8,128)}, f32[1,1024]{1,0:T(1,128)}) custom-call(bf16[2,256,1024]{2,1,0:T(8,128)(2,1)} %refs_0_.1, bf16[2,256,1024]{2,1,0:T(8,128)(2,1)} %get-tuple-element.200.refs_6_.refs_1_, bf16[2,256,1024]{2,1,0:T(8,128)(2,1)} %copy-done.54, bf16[2,16,1024]{2,1,0:T(8,128)(2,1)} %copy-done.56, ...), custom_call_target="tpu_custom_call" | custom-call | bytes 7479296 | tf_op jit(solution)/shard_map/first_norm_back/pallas_call | solution.py:686
  297.2 3.8 %collective-permute-done.35.refs_1_ = f32[8,1024]{1,0:T(8,128)S(1)} collective-permute-done((f32[8,1024]{1,0:T(8,128)S(1)}, f32[8,1024]{1,0:T(8,128)S(1)}, u32[]{:S(2)}, u32[]{:S(2)}) %collective-permute-start.35) | collective-permute-done | bytes 32800 | tf_op jit(solution)/shard_map/ppermute | solution.py:827
  302.2 2.1 collective-permute-start.36
  305.5 2.0 collective-permute-start.39
  307.5 10.7 %collective-permute-done.40.refs_1_ = bf16[64,4224]{1,0:T(8,128)(2,1)S(1)} collective-permute-done((bf16[64,4224]{1,0:T(8,128)(2,1)}, bf16[64,4224]{1,0:T(8,128)(2,1)S(1)}, u32[]{:S(2)}, u32[]{:S(2)}) %collective-permute-start.40) | collective-permute-done | bytes 540704 | tf_op jit(solution)/shard_map/ppermute | solution.py:827
  320.9 2.9 collective-permute-start.41
  323.8 2.5 collective-permute-start.42
  326.4 2.3 collective-permute-start.44
  328.7 2.7 collective-permute-done.42.refs_2_
  331.4 7.7 %collective-permute-done.43.refs_3_ = f32[8,1024]{1,0:T(8,128)S(1)} collective-permute-done((f32[8,1024]{1,0:T(8,128)S(1)}, f32[8,1024]{1,0:T(8,128)S(1)}, u32[]{:S(2)}, u32[]{:S(2)}) %collective-permute-start.43) | collective-permute-done | bytes 32800 | tf_op jit(solution)/shard_map/ppermute | solution.py:827
  (213 shorter events, 52.7 us)
Async XLA Ops:
  1.5 7.8 %collective-permute-start = (bf16[2,16,1024]{2,1,0:T(8,128)(2,1)S(1)}, bf16[2,16,1024]{2,1,0:T(8,128)(2,1)S(1)}, u32[]{:S(2)}, u32[]{:S(2)}) collective-permute-start(bf16[2,16,1024]{2,1,0:T(8,128)(2,1)S(1)} %slice.12), channel_id=1, source_target_pairs={{0,2},{2,4},{4,6},{6,8},{8,10},{10,12},{12,14},{14,16},{16,18},{18... | collective-permute-start | bytes 196616 | tf_op jit(solution)/shard_map/ppermute | solution.py:833
  26.0 12.8 %collective-permute-start.1 = (bf16[4,144,384]{2,1,0:T(8,128)(2,1)}, bf16[4,144,384]{2,1,0:T(8,128)(2,1)S(1)}, u32[]{:S(2)}, u32[]{:S(2)}) collective-permute-start(bf16[4,144,384]{2,1,0:T(8,128)(2,1)} %bitcast.100), channel_id=1, source_target_pairs={{0,2},{2,4},{4,6},{6,8},{8,10},{10,12},{12,14},{14,16},{16,18},{18... | collective-permute-start | bytes 1327112 | tf_op jit(solution)/shard_map/ppermute | solution.py:833
  41.0 12.7 %collective-permute-start.2 = (bf16[4,144,384]{2,1,0:T(8,128)(2,1)S(1)}, bf16[4,144,384]{2,1,0:T(8,128)(2,1)S(1)}, u32[]{:S(2)}, u32[]{:S(2)}) collective-permute-start(bf16[4,144,384]{2,1,0:T(8,128)(2,1)S(1)} %get-tuple-element.135), channel_id=1, source_target_pairs={{0,4},{2,6},{4,8},{6,10},{8,12},{10,14},{12,16},{14,18},{16,20},{1... | collective-permute-start | bytes 1327112 | tf_op jit(solution)/shard_map/ppermute | solution.py:833
  54.1 13.2 %collective-permute-start.3 = (bf16[4,144,384]{2,1,0:T(8,128)(2,1)S(1)}, bf16[4,144,384]{2,1,0:T(8,128)(2,1)S(1)}, u32[]{:S(2)}, u32[]{:S(2)}) collective-permute-start(bf16[4,144,384]{2,1,0:T(8,128)(2,1)S(1)} %get-tuple-element.138), channel_id=1, source_target_pairs={{0,8},{2,10},{4,12},{6,14},{8,16},{10,18},{12,20},{14,22},{16,24},... | collective-permute-start | bytes 1327112 | tf_op jit(solution)/shard_map/ppermute | solution.py:833
  68.6 12.6 %collective-permute-start.4 = (bf16[4,144,384]{2,1,0:T(8,128)(2,1)S(1)}, bf16[4,144,384]{2,1,0:T(8,128)(2,1)S(1)}, u32[]{:S(2)}, u32[]{:S(2)}) collective-permute-start(bf16[4,144,384]{2,1,0:T(8,128)(2,1)S(1)} %get-tuple-element.139), channel_id=1, source_target_pairs={{0,2},{2,4},{4,6},{6,8},{8,10},{10,12},{12,14},{14,16},{16,18},{18... | collective-permute-start | bytes 1327112 | tf_op jit(solution)/shard_map/ppermute | solution.py:833
  71.0 10.2 %collective-permute-start.5 = (bf16[4,128,256]{2,1,0:T(8,128)(2,1)S(1)}, bf16[4,128,256]{2,1,0:T(8,128)(2,1)S(1)}, u32[]{:S(2)}, u32[]{:S(2)}) collective-permute-start(bf16[4,128,256]{2,1,0:T(8,128)(2,1)S(1)} %get-tuple-element.140), channel_id=1, source_target_pairs={{0,18},{2,20},{4,22},{6,24},{8,26},{10,28},{12,30},{1,19},{3,21},{... | collective-permute-start | bytes 786440 | tf_op jit(solution)/shard_map/ppermute | solution.py:833
  76.5 8.5 %collective-permute-start.7 = (bf16[4,144,128]{2,1,0:T(8,128)(2,1)S(1)}, bf16[4,144,128]{2,1,0:T(8,128)(2,1)S(1)}, u32[]{:S(2)}, u32[]{:S(2)}) collective-permute-start(bf16[4,144,128]{2,1,0:T(8,128)(2,1)S(1)} %get-tuple-element.147), channel_id=1, source_target_pairs={{2,0},{4,2},{6,4},{8,6},{10,8},{12,10},{14,12},{16,14},{18,16},{20... | collective-permute-start | bytes 442376 | tf_op jit(solution)/shard_map/ppermute | solution.py:833
  77.8 10.5 %collective-permute-start.8 = (bf16[4,144,128]{2,1,0:T(8,128)(2,1)S(1)}, bf16[4,144,128]{2,1,0:T(8,128)(2,1)S(1)}, u32[]{:S(2)}, u32[]{:S(2)}) collective-permute-start(bf16[4,144,128]{2,1,0:T(8,128)(2,1)S(1)} %get-tuple-element.148), channel_id=1, source_target_pairs={{6,0},{8,2},{10,4},{12,6},{14,8},{16,10},{18,12},{20,14},{22,16},{... | collective-permute-start | bytes 442376 | tf_op jit(solution)/shard_map/ppermute | solution.py:833
  79.1 11.7 %collective-permute-start.6 = (bf16[4,144,128]{2,1,0:T(8,128)(2,1)S(1)}, bf16[4,144,128]{2,1,0:T(8,128)(2,1)S(1)}, u32[]{:S(2)}, u32[]{:S(2)}) collective-permute-start(bf16[4,144,128]{2,1,0:T(8,128)(2,1)S(1)} %get-tuple-element.146), channel_id=1, source_target_pairs={{16,0},{18,2},{20,4},{22,6},{24,8},{26,10},{28,12},{30,14},{17,1},... | collective-permute-start | bytes 442376 | tf_op jit(solution)/shard_map/ppermute | solution.py:833
  84.9 5.9 %copy-start.36 = (bf16[4,144,128]{2,1,0:T(8,128)(2,1)}, bf16[4,144,128]{2,1,0:T(8,128)(2,1)S(1)}, u32[]{:S(2)}) copy-start(bf16[4,144,128]{2,1,0:T(8,128)(2,1)S(1)} %collective-permute-done.7.refs_9_.refs_0_) | copy-start | bytes 442372
  96.3 2.9 collective-permute-start.9
  117.5 15.4 %collective-permute-start.11 = (bf16[2,256,1024]{2,1,0:T(8,128)(2,1)}, bf16[2,256,1024]{2,1,0:T(8,128)(2,1)S(1)}, u32[]{:S(2)}, u32[]{:S(2)}) collective-permute-start(bf16[2,256,1024]{2,1,0:T(8,128)(2,1)} %get-tuple-element.155.refs_1_), channel_id=1, source_target_pairs={{0,1},{1,0},{2,3},{3,2},{4,5},{5,4},{6,7},{7,6},{8,9},{9,8},{10,11... | collective-permute-start | bytes 3145736 | tf_op jit(solution)/shard_map/ppermute | solution.py:838
  123.0 44.7 %collective-permute-start.16 = (bf16[512,1408]{1,0:T(8,128)(2,1)}, bf16[512,1408]{1,0:T(8,128)(2,1)}, u32[]{:S(2)}, u32[]{:S(2)}) collective-permute-start(bf16[512,1408]{1,0:T(8,128)(2,1)} %gate_send.1.refs_3_), channel_id=1, source_target_pairs={{0,2},{2,0},{4,6},{6,4},{8,10},{10,8},{12,14},{14,12},{16,18},{18,... | collective-permute-start | bytes 4325384 | tf_op jit(solution)/shard_map/ppermute | solution.py:827
  126.8 46.0 %collective-permute-start.15 = (bf16[512,1408]{1,0:T(8,128)(2,1)}, bf16[512,1408]{1,0:T(8,128)(2,1)}, u32[]{:S(2)}, u32[]{:S(2)}) collective-permute-start(bf16[512,1408]{1,0:T(8,128)(2,1)} %up_send.1.refs_3_), channel_id=1, source_target_pairs={{0,4},{2,6},{4,0},{6,2},{8,12},{10,14},{12,8},{14,10},{16,20},{18,... | collective-permute-start | bytes 4325384 | tf_op jit(solution)/shard_map/ppermute | solution.py:827
  130.0 52.3 %collective-permute-start.14 = (bf16[512,1408]{1,0:T(8,128)(2,1)S(1)}, bf16[512,1408]{1,0:T(8,128)(2,1)}, u32[]{:S(2)}, u32[]{:S(2)}) collective-permute-start(bf16[512,1408]{1,0:T(8,128)(2,1)S(1)} %down_send.1.refs_10_), channel_id=1, source_target_pairs={{0,8},{2,10},{4,12},{6,14},{8,0},{10,2},{12,4},{14,6},{16,24},{18,... | collective-permute-start | bytes 4325384 | tf_op jit(solution)/shard_map/ppermute | solution.py:827
  132.9 17.0 %collective-permute-start.10 = (bf16[2,256,1024]{2,1,0:T(8,128)(2,1)}, bf16[2,256,1024]{2,1,0:T(8,128)(2,1)}, u32[]{:S(2)}, u32[]{:S(2)}) collective-permute-start(bf16[2,256,1024]{2,1,0:T(8,128)(2,1)} %get-tuple-element.151.refs_1_), channel_id=1, source_target_pairs={{0,1},{1,0},{2,3},{3,2},{4,5},{5,4},{6,7},{7,6},{8,9},{9,8},{10,11... | collective-permute-start | bytes 3145736 | tf_op jit(solution)/shard_map/ppermute | solution.py:838
  141.2 21.6 %collective-permute-start.12 = (bf16[4,128,256]{2,1,0:T(8,128)(2,1)}, bf16[4,128,256]{2,1,0:T(8,128)(2,1)}, u32[]{:S(2)}, u32[]{:S(2)}) collective-permute-start(bf16[4,128,256]{2,1,0:T(8,128)(2,1)} %bitcast.102), channel_id=1, source_target_pairs={{2,0},{4,2},{6,4},{8,6},{10,8},{12,10},{14,12},{16,14},{18,16},{20... | collective-permute-start | bytes 786440 | tf_op jit(solution)/shard_map/ppermute | solution.py:833
  149.9 12.9 %copy-start.43 = (bf16[2,2,144,128]{3,2,1,0:T(8,128)(2,1)S(1)}, bf16[2,2,144,128]{3,2,1,0:T(8,128)(2,1)}, u32[]{:S(2)}) copy-start(bf16[2,2,144,128]{3,2,1,0:T(8,128)(2,1)} %get-tuple-element.168) | copy-start | bytes 442372
  149.9 17.8 %copy-start.5 = (bf16[2,256,1408]{2,1,0:T(8,128)(2,1)S(1)}, bf16[2,256,1408]{2,1,0:T(8,128)(2,1)}, u32[]{:S(2)}) copy-start(bf16[2,256,1408]{2,1,0:T(8,128)(2,1)} %get-tuple-element.161) | copy-start | bytes 4325380
  153.2 14.6 %copy-start.2 = (bf16[1024,512]{1,0:T(8,128)(2,1)S(1)}, bf16[1024,512]{1,0:T(8,128)(2,1)}, u32[]{:S(2)}) copy-start(bf16[1024,512]{1,0:T(8,128)(2,1)} %get-tuple-element.159) | copy-start | bytes 3145732
  166.3 6.5 %copy-start.9 = (bf16[2,256,1408]{2,1,0:T(8,128)(2,1)S(1)}, bf16[2,256,1408]{2,1,0:T(8,128)(2,1)}, u32[]{:S(2)}) copy-start(bf16[2,256,1408]{2,1,0:T(8,128)(2,1)} %get-tuple-element.160) | copy-start | bytes 4325380
  166.3 21.4 %collective-permute-start.13 = (bf16[4,128,256]{2,1,0:T(8,128)(2,1)S(1)}, bf16[4,128,256]{2,1,0:T(8,128)(2,1)S(1)}, u32[]{:S(2)}, u32[]{:S(2)}) collective-permute-start(bf16[4,128,256]{2,1,0:T(8,128)(2,1)S(1)} %get-tuple-element.172.refs_4_), channel_id=1, source_target_pairs={{4,0},{6,2},{8,4},{10,6},{12,8},{14,10},{16,12},{18,14},{20,16},{2... | collective-permute-start | bytes 786440 | tf_op jit(solution)/shard_map/ppermute | solution.py:833
  170.1 36.4 %collective-permute-start.22 = (bf16[256,1408]{1,0:T(8,128)(2,1)S(1)}, bf16[256,1408]{1,0:T(8,128)(2,1)S(1)}, u32[]{:S(2)}, u32[]{:S(2)}) collective-permute-start(bf16[256,1408]{1,0:T(8,128)(2,1)S(1)} %get-tuple-element.181), channel_id=1, source_target_pairs={{0,4},{2,6},{4,0},{6,2},{8,12},{10,14},{12,8},{14,10},{16,20},{18,... | collective-permute-start | bytes 2162696 | tf_op jit(solution)/shard_map/ppermute | solution.py:827
  172.8 9.5 %copy-start.7 = (bf16[2,256,1408]{2,1,0:T(8,128)(2,1)S(1)}, bf16[2,256,1408]{2,1,0:T(8,128)(2,1)}, u32[]{:S(2)}) copy-start(bf16[2,256,1408]{2,1,0:T(8,128)(2,1)} %get-tuple-element.158) | copy-start | bytes 4325380
  175.3 32.1 %collective-permute-start.21 = (bf16[256,1408]{1,0:T(8,128)(2,1)S(1)}, bf16[256,1408]{1,0:T(8,128)(2,1)S(1)}, u32[]{:S(2)}, u32[]{:S(2)}) collective-permute-start(bf16[256,1408]{1,0:T(8,128)(2,1)S(1)} %get-tuple-element.180), channel_id=1, source_target_pairs={{0,8},{2,10},{4,12},{6,14},{8,0},{10,2},{12,4},{14,6},{16,24},{18,... | collective-permute-start | bytes 2162696 | tf_op jit(solution)/shard_map/ppermute | solution.py:827
  182.3 5.3 %copy-start.37 = (bf16[4,144,128]{2,1,0:T(8,128)(2,1)S(1)}, bf16[4,144,128]{2,1,0:T(8,128)(2,1)}, u32[]{:S(2)}) copy-start(bf16[4,144,128]{2,1,0:T(8,128)(2,1)} %copy-done.36) | copy-start | bytes 442372
  184.7 18.2 %copy-start.35 = (bf16[4,144,128]{2,1,0:T(8,128)(2,1)S(1)}, bf16[4,144,128]{2,1,0:T(8,128)(2,1)}, u32[]{:S(2)}) copy-start(bf16[4,144,128]{2,1,0:T(8,128)(2,1)} %copy-done.34) | copy-start | bytes 442372
  184.7 23.7 %collective-permute-start.20 = (bf16[256,1408]{1,0:T(8,128)(2,1)S(1)}, bf16[256,1408]{1,0:T(8,128)(2,1)S(1)}, u32[]{:S(2)}, u32[]{:S(2)}) collective-permute-start(bf16[256,1408]{1,0:T(8,128)(2,1)S(1)} %get-tuple-element.179), channel_id=1, source_target_pairs={{0,2},{2,0},{4,6},{6,4},{8,10},{10,8},{12,14},{14,12},{16,18},{18,... | collective-permute-start | bytes 2162696 | tf_op jit(solution)/shard_map/ppermute | solution.py:827
  187.9 15.0 %collective-permute-start.17 = (bf16[4,128,256]{2,1,0:T(8,128)(2,1)S(1)}, bf16[4,128,256]{2,1,0:T(8,128)(2,1)S(1)}, u32[]{:S(2)}, u32[]{:S(2)}) collective-permute-start(bf16[4,128,256]{2,1,0:T(8,128)(2,1)S(1)} %get-tuple-element.177.refs_3_), channel_id=1, source_target_pairs={{8,0},{10,2},{12,4},{14,6},{16,8},{18,10},{20,12},{22,14},{24,16},... | collective-permute-start | bytes 786440 | tf_op jit(solution)/shard_map/ppermute | solution.py:833
  203.9 18.4 %collective-permute-start.18 = (bf16[4,128,256]{2,1,0:T(8,128)(2,1)S(1)}, bf16[4,128,256]{2,1,0:T(8,128)(2,1)S(1)}, u32[]{:S(2)}, u32[]{:S(2)}) collective-permute-start(bf16[4,128,256]{2,1,0:T(8,128)(2,1)S(1)} %get-tuple-element.178.refs_2_), channel_id=1, source_target_pairs={{2,0},{4,2},{6,4},{8,6},{10,8},{12,10},{14,12},{16,14},{18,16},{20... | collective-permute-start | bytes 786440 | tf_op jit(solution)/shard_map/ppermute | solution.py:833
  205.2 17.2 %collective-permute-start.19 = (bf16[4,128,256]{2,1,0:T(8,128)(2,1)S(1)}, bf16[4,128,256]{2,1,0:T(8,128)(2,1)S(1)}, u32[]{:S(2)}, u32[]{:S(2)}) collective-permute-start(bf16[4,128,256]{2,1,0:T(8,128)(2,1)S(1)} %get-tuple-element.178.refs_2_), channel_id=1, source_target_pairs={{18,0},{20,2},{22,4},{24,6},{26,8},{28,10},{30,12},{19,1},{21,3},{... | collective-permute-start | bytes 786440 | tf_op jit(solution)/shard_map/ppermute | solution.py:833
  208.4 14.0 %copy-start.39 = (bf16[4,144,128]{2,1,0:T(8,128)(2,1)S(1)}, bf16[4,144,128]{2,1,0:T(8,128)(2,1)}, u32[]{:S(2)}) copy-start(bf16[4,144,128]{2,1,0:T(8,128)(2,1)} %copy-done.38) | copy-start | bytes 442372
  209.4 14.1 %copy-start.22 = (f32[128,1408]{1,0:T(8,128)}, f32[128,1408]{1,0:T(8,128)S(1)}, u32[]{:S(2)}) copy-start(f32[128,1408]{1,0:T(8,128)S(1)} %get-tuple-element.184.refs_3_.refs_4_) | copy-start | bytes 2162692
  209.4 28.6 %collective-permute-start.25 = (bf16[128,1408]{1,0:T(8,128)(2,1)}, bf16[128,1408]{1,0:T(8,128)(2,1)}, u32[]{:S(2)}, u32[]{:S(2)}) collective-permute-start(bf16[128,1408]{1,0:T(8,128)(2,1)} %get-tuple-element.194), channel_id=1, source_target_pairs={{0,4},{2,6},{4,0},{6,2},{8,12},{10,14},{12,8},{14,10},{16,20},{18,... | collective-permute-start | bytes 1081352 | tf_op jit(solution)/shard_map/ppermute | solution.py:827
  215.2 22.8 %collective-permute-start.24 = (bf16[128,1408]{1,0:T(8,128)(2,1)}, bf16[128,1408]{1,0:T(8,128)(2,1)}, u32[]{:S(2)}, u32[]{:S(2)}) collective-permute-start(bf16[128,1408]{1,0:T(8,128)(2,1)} %get-tuple-element.193), channel_id=1, source_target_pairs={{0,2},{2,0},{4,6},{6,4},{8,10},{10,8},{12,14},{14,12},{16,18},{18,... | collective-permute-start | bytes 1081352 | tf_op jit(solution)/shard_map/ppermute | solution.py:827
  215.2 22.8 %collective-permute-start.23 = (bf16[128,1408]{1,0:T(8,128)(2,1)}, bf16[128,1408]{1,0:T(8,128)(2,1)}, u32[]{:S(2)}, u32[]{:S(2)}) collective-permute-start(bf16[128,1408]{1,0:T(8,128)(2,1)} %get-tuple-element.192), channel_id=1, source_target_pairs={{0,8},{2,10},{4,12},{6,14},{8,0},{10,2},{12,4},{14,6},{16,24},{18,... | collective-permute-start | bytes 1081352 | tf_op jit(solution)/shard_map/ppermute | solution.py:827
  223.5 10.4 %copy-start = (bf16[1024,512]{1,0:T(8,128)(2,1)S(1)}, bf16[1024,512]{1,0:T(8,128)(2,1)}, u32[]{:S(2)}) copy-start(bf16[1024,512]{1,0:T(8,128)(2,1)} %get-tuple-element.196) | copy-start | bytes 3145732
  223.5 10.4 %copy-start.10 = (bf16[2,256,512]{2,1,0:T(8,128)(2,1)S(1)}, bf16[2,256,512]{2,1,0:T(8,128)(2,1)}, u32[]{:S(2)}) copy-start(bf16[2,256,512]{2,1,0:T(8,128)(2,1)} %get-tuple-element.190.refs_1_) | copy-start | bytes 1572868
  223.5 10.4 %copy-start.14 = (bf16[1024,512]{1,0:T(8,128)(2,1)S(1)}, bf16[1024,512]{1,0:T(8,128)(2,1)}, u32[]{:S(2)}) copy-start(bf16[1024,512]{1,0:T(8,128)(2,1)} %get-tuple-element.195) | copy-start | bytes 3145732
  236.9 24.2 %collective-permute-start.31 = (bf16[512,1024]{1,0:T(8,128)(2,1)S(1)}, bf16[512,1024]{1,0:T(8,128)(2,1)}, u32[]{:S(2)}, u32[]{:S(2)}) collective-permute-start(bf16[512,1024]{1,0:T(8,128)(2,1)S(1)} %outs_send.1.refs_6_), channel_id=1, source_target_pairs={{0,8},{2,10},{4,12},{6,14},{8,0},{10,2},{12,4},{14,6},{16,24},{18,... | collective-permute-start | bytes 3145736 | tf_op jit(solution)/shard_map/ppermute | solution.py:827
  244.5 5.8 %copy-start.32 = (bf16[2,256,128]{2,1,0:T(8,128)(2,1)S(1)}, bf16[2,256,128]{2,1,0:T(8,128)(2,1)}, u32[]{:S(2)}) copy-start(bf16[2,256,128]{2,1,0:T(8,128)(2,1)} %get-tuple-element.191.refs_2_) | copy-start | bytes 393220
  250.2 40.8 %collective-permute-start.26 = (bf16[2,256,1024]{2,1,0:T(8,128)(2,1)}, bf16[2,256,1024]{2,1,0:T(8,128)(2,1)S(1)}, u32[]{:S(2)}, u32[]{:S(2)}) collective-permute-start(bf16[2,256,1024]{2,1,0:T(8,128)(2,1)} %get-tuple-element.200.refs_6_.refs_1_), channel_id=1, source_target_pairs={{0,1},{1,0},{2,3},{3,2},{4,5},{5,4},{6,7},{7,6},{8,9},{9,8},{10,11... | collective-permute-start | bytes 3145736 | tf_op jit(solution)/shard_map/ppermute | solution.py:838
  254.5 18.0 %collective-permute-start.30 = (bf16[512,640]{1,0:T(8,128)(2,1)S(1)}, bf16[512,640]{1,0:T(8,128)(2,1)S(1)}, u32[]{:S(2)}, u32[]{:S(2)}) collective-permute-start(bf16[512,640]{1,0:T(8,128)(2,1)S(1)} %query_key_send.1.refs_5_), channel_id=1, source_target_pairs={{0,2},{2,0},{4,6},{6,4},{8,10},{10,8},{12,14},{14,12},{16,18},{18,... | collective-permute-start | bytes 1966088 | tf_op jit(solution)/shard_map/ppermute | solution.py:827
  258.1 9.8 %copy-start.60 = (bf16[2,16,1024]{2,1,0:T(8,128)(2,1)S(1)}, bf16[2,16,1024]{2,1,0:T(8,128)(2,1)}, u32[]{:S(2)}) copy-start(bf16[2,16,1024]{2,1,0:T(8,128)(2,1)} %get-tuple-element.201) | copy-start | bytes 196612
  258.1 14.5 %copy-start.31 = (bf16[2,256,512]{2,1,0:T(8,128)(2,1)S(1)}, bf16[2,256,512]{2,1,0:T(8,128)(2,1)}, u32[]{:S(2)}) copy-start(bf16[2,256,512]{2,1,0:T(8,128)(2,1)} %get-tuple-element.206) | copy-start | bytes 1572868
  258.1 26.9 %collective-permute-start.29 = (bf16[512,512]{1,0:T(8,128)(2,1)S(1)}, bf16[512,512]{1,0:T(8,128)(2,1)S(1)}, u32[]{:S(2)}, u32[]{:S(2)}) collective-permute-start(bf16[512,512]{1,0:T(8,128)(2,1)S(1)} %value_send.1.refs_6_), channel_id=1, source_target_pairs={{0,4},{2,6},{4,0},{6,2},{8,12},{10,14},{12,8},{14,10},{16,20},{18,... | collective-permute-start | bytes 1572872 | tf_op jit(solution)/shard_map/ppermute | solution.py:827
  263.8 40.5 %collective-permute-start.37 = (bf16[256,1024]{1,0:T(8,128)(2,1)}, bf16[256,1024]{1,0:T(8,128)(2,1)}, u32[]{:S(2)}, u32[]{:S(2)}) collective-permute-start(bf16[256,1024]{1,0:T(8,128)(2,1)} %get-tuple-element.221), channel_id=1, source_target_pairs={{0,2},{2,0},{4,6},{6,4},{8,10},{10,8},{12,14},{14,12},{16,18},{18,... | collective-permute-start | bytes 1572872 | tf_op jit(solution)/shard_map/ppermute | solution.py:827
  267.9 17.1 %collective-permute-start.27 = (bf16[2,16,1024]{2,1,0:T(8,128)(2,1)S(1)}, bf16[2,16,1024]{2,1,0:T(8,128)(2,1)S(1)}, u32[]{:S(2)}, u32[]{:S(2)}) collective-permute-start(bf16[2,16,1024]{2,1,0:T(8,128)(2,1)S(1)} %copy-done.60), channel_id=1, source_target_pairs={{2,0},{4,2},{6,4},{8,6},{10,8},{12,10},{14,12},{16,14},{18,16},{20... | collective-permute-start | bytes 196616 | tf_op jit(solution)/shard_map/ppermute | solution.py:833
  274.5 26.6 %collective-permute-start.32 = (bf16[256,640]{1,0:T(8,128)(2,1)}, bf16[256,640]{1,0:T(8,128)(2,1)}, u32[]{:S(2)}, u32[]{:S(2)}) collective-permute-start(bf16[256,640]{1,0:T(8,128)(2,1)} %get-tuple-element.212), channel_id=1, source_target_pairs={{0,4},{2,6},{4,0},{6,2},{8,12},{10,14},{12,8},{14,10},{16,20},{18,... | collective-permute-start | bytes 983048 | tf_op jit(solution)/shard_map/ppermute | solution.py:827
  285.0 6.0 %collective-permute-start.28 = (bf16[2,16,1024]{2,1,0:T(8,128)(2,1)S(1)}, bf16[2,16,1024]{2,1,0:T(8,128)(2,1)S(1)}, u32[]{:S(2)}, u32[]{:S(2)}) collective-permute-start(bf16[2,16,1024]{2,1,0:T(8,128)(2,1)S(1)} %collective-permute-done.27.refs_3_), channel_id=1, source_target_pairs={{0,1},{1,0},{2,3},{3,2},{4,5},{5,4},{6,7},{7,6},{8,9},{9,8},{10,11... | collective-permute-start | bytes 196616 | tf_op jit(solution)/shard_map/ppermute | solution.py:838
  285.0 6.0 %copy-start.53 = (f32[1,256]{1,0:T(1,128)S(1)}, f32[1,256]{1,0:T(1,128)}, u32[]{:S(2)}) copy-start(f32[1,256]{1,0:T(1,128)} %get-tuple-element.218.ogain_ref) | copy-start | bytes 3076
  286.9 14.1 %collective-permute-start.33 = (bf16[256,512]{1,0:T(8,128)(2,1)S(1)}, bf16[256,512]{1,0:T(8,128)(2,1)S(1)}, u32[]{:S(2)}, u32[]{:S(2)}) collective-permute-start(bf16[256,512]{1,0:T(8,128)(2,1)S(1)} %get-tuple-element.213), channel_id=1, source_target_pairs={{0,2},{2,0},{4,6},{6,4},{8,10},{10,8},{12,14},{14,12},{16,18},{18,... | collective-permute-start | bytes 786440 | tf_op jit(solution)/shard_map/ppermute | solution.py:827
  291.0 27.2 %collective-permute-start.40 = (bf16[64,4224]{1,0:T(8,128)(2,1)}, bf16[64,4224]{1,0:T(8,128)(2,1)S(1)}, u32[]{:S(2)}, u32[]{:S(2)}) collective-permute-start(bf16[64,4224]{1,0:T(8,128)(2,1)} %get-tuple-element.224), channel_id=1, source_target_pairs={{0,16},{2,18},{4,20},{6,22},{8,24},{10,26},{12,28},{14,30},{16,0},... | collective-permute-start | bytes 1622024 | tf_op jit(solution)/shard_map/ppermute | solution.py:827
  291.0 5.3 %collective-permute-start.34 = (f32[1,256]{1,0:T(1,128)S(1)}, f32[1,256]{1,0:T(1,128)S(1)}, u32[]{:S(2)}, u32[]{:S(2)}) collective-permute-start(f32[1,256]{1,0:T(1,128)S(1)} %copy-done.53), channel_id=1, source_target_pairs={{0,1},{1,0},{2,3},{3,2},{4,5},{5,4},{6,7},{7,6},{8,9},{9,8},{10,11... | collective-permute-start | bytes 3080 | tf_op jit(solution)/shard_map/ppermute | solution.py:838
  292.1 9.0 %copy-start.29 = (f32[256,512]{1,0:T(8,128)S(1)}, f32[256,512]{1,0:T(8,128)}, u32[]{:S(2)}) copy-start(f32[256,512]{1,0:T(8,128)} %copy-done.28) | copy-start | bytes 1572868
  297.1 4.0 %collective-permute-start.35 = (f32[8,1024]{1,0:T(8,128)S(1)}, f32[8,1024]{1,0:T(8,128)S(1)}, u32[]{:S(2)}, u32[]{:S(2)}) collective-permute-start(f32[8,1024]{1,0:T(8,128)S(1)} %pack.1.refs_0_.refs_2_), channel_id=1, source_target_pairs={{0,2},{2,0},{4,6},{6,4},{8,10},{10,8},{12,14},{14,12},{16,18},{18,... | collective-permute-start | bytes 98312 | tf_op jit(solution)/shard_map/ppermute | solution.py:827
  302.2 16.0 %copy-start.13 = (f32[64,4224]{1,0:T(8,128)S(1)}, f32[64,4224]{1,0:T(8,128)}, u32[]{:S(2)}) copy-start(f32[64,4224]{1,0:T(8,128)} %copy-done.12) | copy-start | bytes 3244036
  302.2 18.6 %collective-permute-start.36 = (bf16[128,1152]{1,0:T(8,128)(2,1)S(1)}, bf16[128,1152]{1,0:T(8,128)(2,1)S(1)}, u32[]{:S(2)}, u32[]{:S(2)}) collective-permute-start(bf16[128,1152]{1,0:T(8,128)(2,1)S(1)} %get-tuple-element.220), channel_id=1, source_target_pairs={{0,8},{2,10},{4,12},{6,14},{8,0},{10,2},{12,4},{14,6},{16,24},{18,... | collective-permute-start | bytes 884744 | tf_op jit(solution)/shard_map/ppermute | solution.py:827
  305.4 15.4 %collective-permute-start.38 = (bf16[128,1024]{1,0:T(8,128)(2,1)S(1)}, bf16[128,1024]{1,0:T(8,128)(2,1)S(1)}, u32[]{:S(2)}, u32[]{:S(2)}) collective-permute-start(bf16[128,1024]{1,0:T(8,128)(2,1)S(1)} %get-tuple-element.223), channel_id=1, source_target_pairs={{0,4},{2,6},{4,0},{6,2},{8,12},{10,14},{12,8},{14,10},{16,20},{18,... | collective-permute-start | bytes 786440 | tf_op jit(solution)/shard_map/ppermute | solution.py:827
  305.5 13.8 %collective-permute-start.39 = (f32[8,1024]{1,0:T(8,128)S(1)}, f32[8,1024]{1,0:T(8,128)S(1)}, u32[]{:S(2)}, u32[]{:S(2)}) collective-permute-start(f32[8,1024]{1,0:T(8,128)S(1)} %small_sum.2.refs_4_.refs_0_), channel_id=1, source_target_pairs={{0,4},{2,6},{4,0},{6,2},{8,12},{10,14},{12,8},{14,10},{16,20},{18,... | collective-permute-start | bytes 98312 | tf_op jit(solution)/shard_map/ppermute | solution.py:827
  320.9 19.3 %collective-permute-start.41 = (bf16[64,2176]{1,0:T(8,128)(2,1)S(1)}, bf16[64,2176]{1,0:T(8,128)(2,1)S(1)}, u32[]{:S(2)}, u32[]{:S(2)}) collective-permute-start(bf16[64,2176]{1,0:T(8,128)(2,1)S(1)} %get-tuple-element.227), channel_id=1, source_target_pairs={{0,16},{2,18},{4,20},{6,22},{8,24},{10,26},{12,28},{14,30},{16,0},... | collective-permute-start | bytes 835592 | tf_op jit(solution)/shard_map/ppermute | solution.py:827
  323.8 7.5 %collective-permute-start.42 = (f32[8,1024]{1,0:T(8,128)S(1)}, f32[8,1024]{1,0:T(8,128)S(1)}, u32[]{:S(2)}, u32[]{:S(2)}) collective-permute-start(f32[8,1024]{1,0:T(8,128)S(1)} %small_sum.3.refs_4_.refs_1_), channel_id=1, source_target_pairs={{0,8},{2,10},{4,12},{6,14},{8,0},{10,2},{12,4},{14,6},{16,24},{18,... | collective-permute-start | bytes 98312 | tf_op jit(solution)/shard_map/ppermute | solution.py:827
  326.3 12.8 %collective-permute-start.43 = (f32[8,1024]{1,0:T(8,128)S(1)}, f32[8,1024]{1,0:T(8,128)S(1)}, u32[]{:S(2)}, u32[]{:S(2)}) collective-permute-start(f32[8,1024]{1,0:T(8,128)S(1)} %small_sum.3.refs_4_.refs_1_), channel_id=1, source_target_pairs={{0,16},{2,18},{4,20},{6,22},{8,24},{10,26},{12,28},{14,30},{16,0},... | collective-permute-start | bytes 98312 | tf_op jit(solution)/shard_map/ppermute | solution.py:827
  326.4 12.7 %collective-permute-start.44 = (f32[8,1024]{1,0:T(8,128)S(1)}, f32[8,1024]{1,0:T(8,128)S(1)}, u32[]{:S(2)}, u32[]{:S(2)}) collective-permute-start(f32[8,1024]{1,0:T(8,128)S(1)} %small_sum.3.refs_4_.refs_1_), channel_id=1, source_target_pairs={{0,24},{2,26},{4,28},{6,30},{8,16},{10,18},{12,20},{14,22},{16,8},... | collective-permute-start | bytes 98312 | tf_op jit(solution)/shard_map/ppermute | solution.py:827
  (47 other events, 99.9 us)

commit v2 on v1

--- a/solution.py
+++ b/solution.py
@@ -20,7 +20,8 @@
 NT = ((1,), (1,))
 TN = ((0,), (0,))
 NOTE = 16
-VMEM_LIMIT = 60 * 1024 * 1024
+VMEM_LIMIT = 48 * 1024 * 1024
+WHOLE_LIMIT = 60 * 1024 * 1024
 SMALL_LIMIT = 20 * 1024 * 1024
 
 
@@ -678,7 +679,7 @@
     return shorter if count else body
 
 
-def call(body, name, seqs, parts, shared, outs, sums=(), turned=(), after=(), flops=0):
+def call(body, name, seqs, parts, shared, outs, sums=(), turned=(), after=(), flops=0, limit=None):
     operands = list(parts) + list(shared)
     listed = list(outs) + list(turned) + list(sums)
     out_shape = [jax.ShapeDtypeStruct(shape, kind) for shape, kind in listed]
@@ -693,7 +694,7 @@
         + [pl.BlockSpec((shape[0], shape[1] // seqs), lambda s: (0, s)) for shape, _ in turned]
         + [whole(shape) for shape, _ in sums],
         out_shape=out_shape,
-        compiler_params=pltpu.CompilerParams(vmem_limit_bytes=VMEM_LIMIT),
+        compiler_params=pltpu.CompilerParams(vmem_limit_bytes=limit or VMEM_LIMIT),
         cost_estimate=pl.CostEstimate(flops=int(flops), bytes_accessed=int(moved), transcendentals=0),
         name=name,
     )(*operands, *after)
@@ -890,6 +891,7 @@
         ],
         turned=[(turned_shape, BF16)],
         flops=1e10,
+        limit=WHOLE_LIMIT,
     )
 
     piece = piece.reshape(pairs, DK, DK + DV)
@@ -984,6 +986,7 @@
         ],
         [((CONV, wide), F32)],
         flops=3e9,
+        limit=WHOLE_LIMIT,
     )
     (result,) = call(
         result_body, "result", seqs, [resid, down, down_other], [],
@@ -992,8 +995,6 @@
     done = result
     for level, d in enumerate(dists):
         got = passed_along(low, "seq", -d)
-        if level == 1:
-            done = down_sum.keep(up_sum.keep(gate_sum.keep(done)))
         back, low = small_call(
             functools.partial(back_body, pairs), "join_back", [back_maps[level], back, got],
             [(state_shape, F32), (state_shape, BF16)], after=[done],
@@ -1001,11 +1002,11 @@
         done = low
     near = passed_along(low, "seq", -1)
     far = passed_along(low, "seq", -1 - reach_by)
-    done = down_sum.add(up_sum.add(gate_sum.add(done)))
     (d_end,) = small_call(
         functools.partial(exit_body, pairs), "exit", [near_map, near, far], [(state_shape, F32)],
         after=[done],
     )
+    done = outs_sum.send(down_sum.keep(up_sum.keep(gate_sum.keep(d_end))))
     d_end = d_end.reshape(seqs, heads, DK, DV)
     d_ext, d_gates, dtap_kv, d_bias = call(
         functools.partial(late_body, heads), "delta_back_late", seqs,
@@ -1015,11 +1016,11 @@
         [conv_key, conv_value],
         [((seqs, size + HALO, proj_wide), F32), ((seqs, size, LANES), BF16)],
         [((CONV, wide + out_wide), F32), ((1, LANES), F32)],
+        after=[done],
         flops=3e9,
-    )
-    done = outs_sum.send(d_bias)
-    feed_sum = joined("feed_last", [gate_sum, up_sum, down_sum], done)
-    done = feed_sum.kept
+        limit=WHOLE_LIMIT,
+    )
+    done = down_sum.add(up_sum.add(gate_sum.add(d_bias)))
     d_qk, d_v, d_qk_halo, d_v_halo, d_mixed, d_halo = call(
         input_back_body, "input_back", seqs, [d_ext, d_pg, d_gates],
         [w_query, w_key, w_value, w_outgate, gates_w],
@@ -1044,6 +1045,8 @@
         [flat(d_v), d_v_halo.reshape(halo_rows, out_wide)], ((((0, 0), (1, 1)), out_wide),),
     )
     done = value_sum.send(query_sum.send(d_mixed))
+    feed_sum = joined("feed_last", [gate_sum, up_sum, down_sum], done)
+    done = feed_sum.kept
     done = value_sum.keep(query_sum.keep(outs_sum.keep(done)))
     halo_grad = passed_along(d_halo, "seq", -1)
     halo_other = swapped(halo_grad)
@@ -1078,11 +1081,11 @@
         )[0]
 
     bits = [[0], [1]] + [[b for step in steps_x[at : at + 2] for b in step] for at in range(2, len(steps_x), 2)]
-    done = small = small_step(bits.pop(0), small)
+    grad_gate, grad_up, grad_down = finish(feed_sum, [units] * 3, small)
+    done = outs_sum.add(grad_gate)
+    done = small = small_step(bits.pop(0), done)
     ins_sum = joined("ins_join", [query_sum, value_sum], done)
-    done = outs_sum.add(ins_sum.kept)
-    grad_gate, grad_up, grad_down = finish(feed_sum, [units] * 3, done)
-    done = small = small_step(bits.pop(0), grad_gate)
+    done = small = small_step(bits.pop(0), ins_sum.kept)
     ins_sum = joined("ins_last", [ins_sum, outs_sum], done)
     while len(bits) > 1:
         small = small_step(bits.pop(0), ins_sum.kept)

time: 343 us -> 329 us (0.959)
  starting transfers between devices: 95.1 us -> 78 us
  waiting for transfers between devices: 102 us -> 109 us
    ppermute x24, starting transfers between devices: 54.1 us -> 36.4 us  [traded(): return lax.ppermute(block, 'seq', [(i, i ^ moved) for i in range(count)])]
    pallas_call x9, Pallas kernels: 76.1 us -> 68.9 us  [call(): pl.pallas_call(without(body, len(operands), len(after)), grid=(seqs,), in...]
    ppermute x24, waiting for transfers between devices: 28.9 us -> 33.4 us  [traded(): return lax.ppermute(block, 'seq', [(i, i ^ moved) for i in range(count)])]
    pallas_call x33, Pallas kernels: 38 us -> 41.9 us  [small_call(): pl.pallas_call(without(body, len(scalars) + len(arrays), len(after)), in_...]
    unnamed x132 -> x144, local copies, waits for them, and re-layouts: 24.2 us -> 22.9 us
  transfers between devices with their start and end apart: 45 -> 45, of which waited for: 18 -> 19; matrix products, arithmetic and copies ran while one was open for 1% -> 1% of each run, Pallas kernels for 21% -> 22%
where the time goes in v2:
time: 329 us; the launch traced here: 328 us
  Pallas kernels  111 us (34%)
  waiting for transfers between devices  109 us (33%)
  starting transfers between devices  78 us (24%)
  local copies, waits for them, and re-layouts  28.1 us (9%)
    ppermute x15, waiting for transfers between devices, passed_along(): return lax.ppermute(block, axis, route)  73 us
    pallas_call x9, Pallas kernels, call(): pl.pallas_call(without(body, len(operands), len(after)), grid=(seqs,), in...  68.9 us
    pallas_call x33, Pallas kernels, small_call(): pl.pallas_call(without(body, len(scalars) + len(arrays), len(after)), in_...  41.9 us
    ppermute x15, starting transfers between devices, passed_along(): return lax.ppermute(block, axis, route)  41 us
    ppermute x24, starting transfers between devices, traded(): return lax.ppermute(block, 'seq', [(i, i ^ moved) for i in range(count)])  36.4 us
    ppermute x24, waiting for transfers between devices, traded(): return lax.ppermute(block, 'seq', [(i, i ^ moved) for i in range(count)])  33.4 us
    unnamed x144, local copies, waits for them, and re-layouts  22.9 us
  transfers between devices with their start and end apart: 45, of which 19 were waited for; matrix products, arithmetic and copies ran while one was open for 1% of the time, Pallas kernels for 22%

profile of v2, /device:TPU:0, one launch (start us, length us, event | category | flops | bytes accessed | tf_op | source)
XLA Modules:
  0.0 327.5 jit_solution(15344891266978534277)
XLA Ops:
  1.5 4.8 %collective-permute-start = (bf16[2,16,1024]{2,1,0:T(8,128)(2,1)S(1)}, bf16[2,16,1024]{2,1,0:T(8,128)(2,1)S(1)}, u32[]{:S(2)}, u32[]{:S(2)}) collective-permute-start(bf16[2,16,1024]{2,1,0:T(8,128)(2,1)S(1)} %slice.12), channel_id=1, source_target_pairs={{0,2},{2,4},{4,6},{6,8},{8,10},{10,12},{12,14},{14,16},{16,18},{18... | collective-permute-start | bytes 196616 | tf_op jit(solution)/shard_map/ppermute | solution.py:834
  9.9 16.0 %project_and_local.1 = (bf16[2,272,1024]{2,1,0:T(8,128)(2,1)}, f32[2,256,512]{2,1,0:T(8,128)}, f32[2,256,128]{2,1,0:T(8,128)}, f32[2,256,128]{2,1,0:T(8,128)}, f...) custom-call(bf16[2,16,1024]{2,1,0:T(8,128)(2,1)} %copy-done.67, ...), custom_call_target="tpu_custom_call" | custom-call | flops 10000000000 | bytes 16028160 | tf_op jit(solution)/shard_map/project_and_local/pallas_call | solution.py:687
  26.0 3.4 %collective-permute-start.1 = (bf16[4,144,384]{2,1,0:T(8,128)(2,1)}, bf16[4,144,384]{2,1,0:T(8,128)(2,1)S(1)}, u32[]{:S(2)}, u32[]{:S(2)}) collective-permute-start(bf16[4,144,384]{2,1,0:T(8,128)(2,1)} %bitcast.100), channel_id=1, source_target_pairs={{0,2},{2,4},{4,6},{6,8},{8,10},{10,12},{12,14},{14,16},{16,18},{18... | collective-permute-start | bytes 1327112 | tf_op jit(solution)/shard_map/ppermute | solution.py:834
  29.4 9.4 %collective-permute-done.1.got_ref = bf16[4,144,384]{2,1,0:T(8,128)(2,1)S(1)} collective-permute-done((bf16[4,144,384]{2,1,0:T(8,128)(2,1)}, bf16[4,144,384]{2,1,0:T(8,128)(2,1)S(1)}, u32[]{:S(2)}, u32[]{:S(2)}) %collective-permute-start.1) | collective-permute-done | bytes 442400 | tf_op jit(solution)/shard_map/ppermute | solution.py:834
  41.0 5.2 %collective-permute-start.2 = (bf16[4,144,384]{2,1,0:T(8,128)(2,1)S(1)}, bf16[4,144,384]{2,1,0:T(8,128)(2,1)S(1)}, u32[]{:S(2)}, u32[]{:S(2)}) collective-permute-start(bf16[4,144,384]{2,1,0:T(8,128)(2,1)S(1)} %get-tuple-element.135), channel_id=1, source_target_pairs={{0,4},{2,6},{4,8},{6,10},{8,12},{10,14},{12,16},{14,18},{16,20},{1... | collective-permute-start | bytes 1327112 | tf_op jit(solution)/shard_map/ppermute | solution.py:834
  46.3 7.5 %collective-permute-done.2.got_ref = bf16[4,144,384]{2,1,0:T(8,128)(2,1)S(1)} collective-permute-done((bf16[4,144,384]{2,1,0:T(8,128)(2,1)S(1)}, bf16[4,144,384]{2,1,0:T(8,128)(2,1)S(1)}, u32[]{:S(2)}, u32[]{:S(2)}) %collective-permute-start.2) | collective-permute-done | bytes 442400 | tf_op jit(solution)/shard_map/ppermute | solution.py:834
  54.1 7.0 %collective-permute-start.3 = (bf16[4,144,384]{2,1,0:T(8,128)(2,1)S(1)}, bf16[4,144,384]{2,1,0:T(8,128)(2,1)S(1)}, u32[]{:S(2)}, u32[]{:S(2)}) collective-permute-start(bf16[4,144,384]{2,1,0:T(8,128)(2,1)S(1)} %get-tuple-element.138), channel_id=1, source_target_pairs={{0,8},{2,10},{4,12},{6,14},{8,16},{10,18},{12,20},{14,22},{16,24},... | collective-permute-start | bytes 1327112 | tf_op jit(solution)/shard_map/ppermute | solution.py:834
  61.1 6.4 %collective-permute-done.3.got_ref = bf16[4,144,384]{2,1,0:T(8,128)(2,1)S(1)} collective-permute-done((bf16[4,144,384]{2,1,0:T(8,128)(2,1)S(1)}, bf16[4,144,384]{2,1,0:T(8,128)(2,1)S(1)}, u32[]{:S(2)}, u32[]{:S(2)}) %collective-permute-start.3) | collective-permute-done | bytes 442400 | tf_op jit(solution)/shard_map/ppermute | solution.py:834
  68.8 2.4 collective-permute-start.4
  71.2 5.5 %collective-permute-start.5 = (bf16[4,128,256]{2,1,0:T(8,128)(2,1)S(1)}, bf16[4,128,256]{2,1,0:T(8,128)(2,1)S(1)}, u32[]{:S(2)}, u32[]{:S(2)}) collective-permute-start(bf16[4,128,256]{2,1,0:T(8,128)(2,1)S(1)} %get-tuple-element.140), channel_id=1, source_target_pairs={{0,18},{2,20},{4,22},{6,24},{8,26},{10,28},{12,30},{1,19},{3,21},{... | collective-permute-start | bytes 786440 | tf_op jit(solution)/shard_map/ppermute | solution.py:834
  76.6 1.3 collective-permute-start.7
  77.9 1.3 collective-permute-start.8
  79.2 1.5 collective-permute-start.6
  81.6 3.5 %collective-permute-done.7.refs_9_.refs_0_ = bf16[4,144,128]{2,1,0:T(8,128)(2,1)S(1)} collective-permute-done((bf16[4,144,128]{2,1,0:T(8,128)(2,1)S(1)}, bf16[4,144,128]{2,1,0:T(8,128)(2,1)S(1)}, u32[]{:S(2)}, u32[]{:S(2)}) %collective-permute-start.7) | collective-permute-done | bytes 147488 | tf_op jit(solution)/shard_map/ppermute | solution.py:834
  85.1 3.3 %collective-permute-done.8.refs_10_.refs_0_ = bf16[4,144,128]{2,1,0:T(8,128)(2,1)S(1)} collective-permute-done((bf16[4,144,128]{2,1,0:T(8,128)(2,1)S(1)}, bf16[4,144,128]{2,1,0:T(8,128)(2,1)S(1)}, u32[]{:S(2)}, u32[]{:S(2)}) %collective-permute-start.8) | collective-permute-done | bytes 147488 | tf_op jit(solution)/shard_map/ppermute | solution.py:834
  88.4 2.6 collective-permute-done.6.refs_8_.refs_0_
  91.0 3.6 %mixer_out.1 = (f32[2,2,256,256]{3,2,1,0:T(8,128)S(1)}, f32[2,256,512]{2,1,0:T(8,128)S(1)}, bf16[2,256,512]{2,1,0:T(8,128)(2,1)S(1)}, bf16[2,256,1024]{2,1,0:T(8,128)(2,1)S(1)}) custom-call(f32[2,2,128,256]{3,2,1,0:T(8,128)S(1)} %bitcast.70, f32[2,2,256,256]{3,2,1,0:T(8,128)} %get-tuple-element.141.refs_1_, f32[2,2,256,128]{3,2,1,0:T(8,128)S(1)} %copy-done.44, ...), custom_call_target="tpu_custom_call" | custom-call | flops 1500000000 | bytes 9438208 | tf_op jit(solution)/shard_map/mixer_out/pallas_call | solution.py:687
  97.5 2.7 collective-permute-done.9.other_ref
  101.1 16.1 %feed_forward.1 = (f32[2,256,1024]{2,1,0:T(8,128)}, bf16[2,256,1408]{2,1,0:T(8,128)(2,1)}, bf16[2,256,1408]{2,1,0:T(8,128)(2,1)}, bf16[2,256,1408]{2,1,0:T(8,128...) custom-call(bf16[2,256,1024]{2,1,0:T(8,128)(2,1)S(1)} %copy-done.32,, ...), custom_call_target="tpu_custom_call" | custom-call | flops 12000000000 | bytes 23465984 | tf_op jit(solution)/shard_map/feed_forward/pallas_call | solution.py:687
  118.8 1.4 copy-done.2
  120.2 2.7 gate_send.1.refs_3_
  124.0 2.6 up_send.1.refs_3_
  126.6 1.7 collective-permute-start.18
  128.3 2.6 down_send.1.refs_10_
  131.0 2.8 collective-permute-start.17
  133.8 7.0 %mixer_back.1 = (f32[2,256,1024]{2,1,0:T(8,128)}, f32[2,256,512]{2,1,0:T(8,128)S(1)}, bf16[2,256,512]{2,1,0:T(8,128)(2,1)S(1)}, f32[2,2,128,256]{3,2,1,0:T(8,128...) custom-call(f32[2,256,1024]{2,1,0:T(8,128)} %get-tuple-element.150.r, ...), custom_call_target="tpu_custom_call" | custom-call | flops 1500000000 | bytes 14428160 | tf_op jit(solution)/shard_map/mixer_back/pallas_call | solution.py:687
  143.5 1.5 collective-permute-start.12
  145.0 7.4 %delta_back_early.1 = (f32[2,2,256,256]{3,2,1,0:T(8,128)}, f32[2,2,256,128]{3,2,1,0:T(8,128)}, f32[2,2,256,128]{3,2,1,0:T(8,128)}, f32[2,256,128]{2,1,0:T(8,128)...) custom-call(bf16[2,272,1024]{2,1,0:T(8,128)(2,1)} %get-tuple-element.152.proj_ref.refs_0_, ...), custom_call_target="tpu_custom_call" | custom-call | flops 3000000000 | bytes 10334208 | tf_op jit(solution)/shard_map/delta_back_early/pallas_call | solution.py:687
  154.6 2.2 result.1.refs_3_
  156.8 5.6 %collective-permute-done.12.refs_2_ = bf16[4,128,256]{2,1,0:T(8,128)(2,1)} collective-permute-done((bf16[4,128,256]{2,1,0:T(8,128)(2,1)}, bf16[4,128,256]{2,1,0:T(8,128)(2,1)}, u32[]{:S(2)}, u32[]{:S(2)}) %collective-permute-start.12) | collective-permute-done | bytes 262176 | tf_op jit(solution)/shard_map/ppermute | solution.py:834
  164.9 1.4 collective-permute-start.13
  166.3 8.1 %collective-permute-done.13.refs_2_ = bf16[4,128,256]{2,1,0:T(8,128)(2,1)S(1)} collective-permute-done((bf16[4,128,256]{2,1,0:T(8,128)(2,1)S(1)}, bf16[4,128,256]{2,1,0:T(8,128)(2,1)S(1)}, u32[]{:S(2)}, u32[]{:S(2)}) %collective-permute-start.13) | collective-permute-done | bytes 262176 | tf_op jit(solution)/shard_map/ppermute | solution.py:834
  174.7 1.4 collective-permute-start.14
  176.1 13.0 %collective-permute-done.14.refs_2_ = bf16[4,128,256]{2,1,0:T(8,128)(2,1)S(1)} collective-permute-done((bf16[4,128,256]{2,1,0:T(8,128)(2,1)S(1)}, bf16[4,128,256]{2,1,0:T(8,128)(2,1)S(1)}, u32[]{:S(2)}, u32[]{:S(2)}) %collective-permute-start.14) | collective-permute-done | bytes 262176 | tf_op jit(solution)/shard_map/ppermute | solution.py:834
  190.1 1.3 collective-permute-start.15
  191.4 1.3 collective-permute-start.16
  192.7 11.4 %collective-permute-done.15.refs_1_ = bf16[4,128,256]{2,1,0:T(8,128)(2,1)S(1)} collective-permute-done((bf16[4,128,256]{2,1,0:T(8,128)(2,1)S(1)}, bf16[4,128,256]{2,1,0:T(8,128)(2,1)S(1)}, u32[]{:S(2)}, u32[]{:S(2)}) %collective-permute-start.15) | collective-permute-done | bytes 262176 | tf_op jit(solution)/shard_map/ppermute | solution.py:834
  204.1 1.4 collective-permute-done.16.refs_2_
  205.8 3.4 %gate_keep.1 = (f32[256,1408]{1,0:T(8,128)S(1)}, bf16[256,1408]{1,0:T(8,128)(2,1)}) custom-call(s32[16]{0:T(128)S(1)} %broadcast_xor_fusion.1.index_ref.refs_0_, bf16[16,64,512]{2,1,0:T(8,128)(2,1)S(1)} %bitcast.52, bf16[512,1408]{1,0:T(8,128)(2,1)S(1)} %bitcast.59, bf16[512,1408]{1,0:T(8,128)(2,1)} %collective-permute-done.19.refs_3_, ...), custom_call_target="tpu_custom_call" | custom-call | flops 738197504 | bytes 6094848 | tf_op jit(solution)/shard_map/gate_keep/pallas_call | solution.py:706
  209.2 6.4 %collective-permute-start.22 = (bf16[256,1408]{1,0:T(8,128)(2,1)}, bf16[256,1408]{1,0:T(8,128)(2,1)}, u32[]{:S(2)}, u32[]{:S(2)}) collective-permute-start(bf16[256,1408]{1,0:T(8,128)(2,1)} %get-tuple-element.191), channel_id=1, source_target_pairs={{0,4},{2,6},{4,0},{6,2},{8,12},{10,14},{12,8},{14,10},{16,20},{18,... | collective-permute-start | bytes 2162696 | tf_op jit(solution)/shard_map/ppermute | solution.py:828
  215.6 3.4 %up_keep.1 = (f32[256,1408]{1,0:T(8,128)S(1)}, bf16[256,1408]{1,0:T(8,128)(2,1)}) custom-call(s32[16]{0:T(128)S(1)} %broadcast_xor_fusion.2.refs_0_, bf16[16,64,512]{2,1,0:T(8,128)(2,1)S(1)} %bitcast.53, bf16[512,1408]{1,0:T(8,128)(2,1)S(1)} %bitcast.63, bf16[512,1408]{1,0:T(8,128)(2,1)} %collective-permute-done.18.refs_3_, ...), custom_call_target="tpu_custom_call" | custom-call | flops 738197504 | bytes 6094848 | tf_op jit(solution)/shard_map/up_keep/pallas_call | solution.py:706
  219.0 3.7 %down_keep.1 = (f32[256,1408]{1,0:T(8,128)S(1)}, bf16[256,1408]{1,0:T(8,128)(2,1)}) custom-call(s32[16]{0:T(128)S(1)} %broadcast_xor_fusion.3.refs_0_, bf16[16,64,512]{2,1,0:T(8,128)(2,1)S(1)} %bitcast.69, bf16[512,1408]{1,0:T(8,128)(2,1)S(1)} %bitcast.61, bf16[512,1408]{1,0:T(8,128)(2,1)} %collective-permute-done.17.refs_3_, ...), custom_call_target="tpu_custom_call" | custom-call | flops 738197504 | bytes 6094848 | tf_op jit(solution)/shard_map/down_keep/pallas_call | solution.py:706
  223.3 2.2 outs_send.1.refs_14_
  225.5 1.6 collective-permute-start.28
  227.2 10.2 %delta_back_late.1 = (f32[2,272,1024]{2,1,0:T(8,128)}, bf16[2,256,128]{2,1,0:T(8,128)(2,1)}, f32[4,768]{1,0:T(4,128)}, f32[1,128]{1,0:T(1,128)}) custom-call(bf16[2,272,1024]{2,1,0:T(8,128)(2,1)} %get-tuple-element.152.proj_ref.refs_0_, f32[2,256,128]{2,1,0:T(8,128)} %get-tuple-element.153.gates_ref.refs_1_, ...), custom_call_target="tpu_custom_call" | custom-call | flops 3000000000 | bytes 10084864 | tf_op jit(solution)/shard_map/delta_back_late/pallas_call | solution.py:687
  240.2 1.5 up_add.1
  242.0 2.1 down_add.1
  251.5 4.0 %input_back.1 = (bf16[2,256,512]{2,1,0:T(8,128)(2,1)S(1)}, bf16[2,256,512]{2,1,0:T(8,128)(2,1)S(1)}, bf16[2,16,512]{2,1,0:T(8,128)(2,1)S(1)}, bf16[2,16,512]{2,1...) custom-call(f32[2,272,1024]{2,1,0:T(8,128)} %get-tuple-element.187.refs_0_, ...), custom_call_target="tpu_custom_call" | custom-call | flops 1700000000 | bytes 8519680 | tf_op jit(solution)/shard_map/input_back/pallas_call | solution.py:687
  256.9 1.8 collective-permute-start.27
  260.6 5.5 %collective-permute-done.29.refs_1_ = bf16[128,1408]{1,0:T(8,128)(2,1)S(1)} collective-permute-done((bf16[128,1408]{1,0:T(8,128)(2,1)}, bf16[128,1408]{1,0:T(8,128)(2,1)S(1)}, u32[]{:S(2)}, u32[]{:S(2)}) %collective-permute-start.29) | collective-permute-done | bytes 360480 | tf_op jit(solution)/shard_map/ppermute | solution.py:828
  266.2 1.7 collective-permute-start.24
  269.1 3.3 %collective-permute-start.37 = (bf16[64,4224]{1,0:T(8,128)(2,1)S(1)}, bf16[64,4224]{1,0:T(8,128)(2,1)S(1)}, u32[]{:S(2)}, u32[]{:S(2)}) collective-permute-start(bf16[64,4224]{1,0:T(8,128)(2,1)S(1)} %get-tuple-element.220), channel_id=1, source_target_pairs={{0,16},{2,18},{4,20},{6,22},{8,24},{10,26},{12,28},{14,30},{16,0},... | collective-permute-start | bytes 1622024 | tf_op jit(solution)/shard_map/ppermute | solution.py:828
  272.4 2.7 outs_keep.1
  275.4 2.0 collective-permute-start.36
  277.4 1.3 query_key_keep.1
  279.9 2.1 collective-permute-start.33
  282.1 2.4 first_norm_back.1
  284.9 10.4 %collective-permute-done.37.refs_1_ = bf16[64,4224]{1,0:T(8,128)(2,1)S(1)} collective-permute-done((bf16[64,4224]{1,0:T(8,128)(2,1)S(1)}, bf16[64,4224]{1,0:T(8,128)(2,1)S(1)}, u32[]{:S(2)}, u32[]{:S(2)}) %collective-permute-start.37) | collective-permute-done | bytes 540704 | tf_op jit(solution)/shard_map/ppermute | solution.py:828
  297.6 3.2 collective-permute-start.38
  300.7 2.0 collective-permute-start.39
  302.8 6.0 %collective-permute-done.40.refs_1_ = f32[8,1024]{1,0:T(8,128)S(1)} collective-permute-done((f32[8,1024]{1,0:T(8,128)S(1)}, f32[8,1024]{1,0:T(8,128)S(1)}, u32[]{:S(2)}, u32[]{:S(2)}) %collective-permute-start.40) | collective-permute-done | bytes 32800 | tf_op jit(solution)/shard_map/ppermute | solution.py:828
  309.4 2.8 collective-permute-start.43
  313.4 1.6 collective-permute-done.42.refs_2_
  315.0 9.9 %collective-permute-done.43.refs_3_ = f32[8,1024]{1,0:T(8,128)S(1)} collective-permute-done((f32[8,1024]{1,0:T(8,128)S(1)}, f32[8,1024]{1,0:T(8,128)S(1)}, u32[]{:S(2)}, u32[]{:S(2)}) %collective-permute-start.43) | collective-permute-done | bytes 32800 | tf_op jit(solution)/shard_map/ppermute | solution.py:828
  (225 shorter events, 48.7 us)
Async XLA Ops:
  1.5 7.8 %collective-permute-start = (bf16[2,16,1024]{2,1,0:T(8,128)(2,1)S(1)}, bf16[2,16,1024]{2,1,0:T(8,128)(2,1)S(1)}, u32[]{:S(2)}, u32[]{:S(2)}) collective-permute-start(bf16[2,16,1024]{2,1,0:T(8,128)(2,1)S(1)} %slice.12), channel_id=1, source_target_pairs={{0,2},{2,4},{4,6},{6,8},{8,10},{10,12},{12,14},{14,16},{16,18},{18... | collective-permute-start | bytes 196616 | tf_op jit(solution)/shard_map/ppermute | solution.py:834
  26.0 12.8 %collective-permute-start.1 = (bf16[4,144,384]{2,1,0:T(8,128)(2,1)}, bf16[4,144,384]{2,1,0:T(8,128)(2,1)S(1)}, u32[]{:S(2)}, u32[]{:S(2)}) collective-permute-start(bf16[4,144,384]{2,1,0:T(8,128)(2,1)} %bitcast.100), channel_id=1, source_target_pairs={{0,2},{2,4},{4,6},{6,8},{8,10},{10,12},{12,14},{14,16},{16,18},{18... | collective-permute-start | bytes 1327112 | tf_op jit(solution)/shard_map/ppermute | solution.py:834
  41.0 12.7 %collective-permute-start.2 = (bf16[4,144,384]{2,1,0:T(8,128)(2,1)S(1)}, bf16[4,144,384]{2,1,0:T(8,128)(2,1)S(1)}, u32[]{:S(2)}, u32[]{:S(2)}) collective-permute-start(bf16[4,144,384]{2,1,0:T(8,128)(2,1)S(1)} %get-tuple-element.135), channel_id=1, source_target_pairs={{0,4},{2,6},{4,8},{6,10},{8,12},{10,14},{12,16},{14,18},{16,20},{1... | collective-permute-start | bytes 1327112 | tf_op jit(solution)/shard_map/ppermute | solution.py:834
  54.1 36.9 %copy-start.26 = (f32[2,2,256,128]{3,2,1,0:T(8,128)S(1)}, f32[2,2,256,128]{3,2,1,0:T(8,128)}, u32[]{:S(2)}) copy-start(f32[2,2,256,128]{3,2,1,0:T(8,128)} %get-tuple-element.143.refs_3_.refs_6_) | copy-start | bytes 1572868
  54.1 36.9 %copy-start.44 = (f32[2,2,256,128]{3,2,1,0:T(8,128)S(1)}, f32[2,2,256,128]{3,2,1,0:T(8,128)}, u32[]{:S(2)}) copy-start(f32[2,2,256,128]{3,2,1,0:T(8,128)} %get-tuple-element.142.refs_2_) | copy-start | bytes 1572868
  54.1 36.8 %copy-start.56 = (f32[256]{0:T(256)S(1)}, f32[256]{0:T(256)}, u32[]{:S(2)}) copy-start(f32[256]{0:T(256)} %param.34) | copy-start | bytes 3076
  54.1 13.4 %collective-permute-start.3 = (bf16[4,144,384]{2,1,0:T(8,128)(2,1)S(1)}, bf16[4,144,384]{2,1,0:T(8,128)(2,1)S(1)}, u32[]{:S(2)}, u32[]{:S(2)}) collective-permute-start(bf16[4,144,384]{2,1,0:T(8,128)(2,1)S(1)} %get-tuple-element.138), channel_id=1, source_target_pairs={{0,8},{2,10},{4,12},{6,14},{8,16},{10,18},{12,20},{14,22},{16,24},... | collective-permute-start | bytes 1327112 | tf_op jit(solution)/shard_map/ppermute | solution.py:834
  68.8 12.6 %collective-permute-start.4 = (bf16[4,144,384]{2,1,0:T(8,128)(2,1)S(1)}, bf16[4,144,384]{2,1,0:T(8,128)(2,1)S(1)}, u32[]{:S(2)}, u32[]{:S(2)}) collective-permute-start(bf16[4,144,384]{2,1,0:T(8,128)(2,1)S(1)} %get-tuple-element.139), channel_id=1, source_target_pairs={{0,2},{2,4},{4,6},{6,8},{8,10},{10,12},{12,14},{14,16},{16,18},{18... | collective-permute-start | bytes 1327112 | tf_op jit(solution)/shard_map/ppermute | solution.py:834
  71.2 10.2 %collective-permute-start.5 = (bf16[4,128,256]{2,1,0:T(8,128)(2,1)S(1)}, bf16[4,128,256]{2,1,0:T(8,128)(2,1)S(1)}, u32[]{:S(2)}, u32[]{:S(2)}) collective-permute-start(bf16[4,128,256]{2,1,0:T(8,128)(2,1)S(1)} %get-tuple-element.140), channel_id=1, source_target_pairs={{0,18},{2,20},{4,22},{6,24},{8,26},{10,28},{12,30},{1,19},{3,21},{... | collective-permute-start | bytes 786440 | tf_op jit(solution)/shard_map/ppermute | solution.py:834
  76.6 8.5 %collective-permute-start.7 = (bf16[4,144,128]{2,1,0:T(8,128)(2,1)S(1)}, bf16[4,144,128]{2,1,0:T(8,128)(2,1)S(1)}, u32[]{:S(2)}, u32[]{:S(2)}) collective-permute-start(bf16[4,144,128]{2,1,0:T(8,128)(2,1)S(1)} %get-tuple-element.147), channel_id=1, source_target_pairs={{2,0},{4,2},{6,4},{8,6},{10,8},{12,10},{14,12},{16,14},{18,16},{20... | collective-permute-start | bytes 442376 | tf_op jit(solution)/shard_map/ppermute | solution.py:834
  77.9 10.5 %collective-permute-start.8 = (bf16[4,144,128]{2,1,0:T(8,128)(2,1)S(1)}, bf16[4,144,128]{2,1,0:T(8,128)(2,1)S(1)}, u32[]{:S(2)}, u32[]{:S(2)}) collective-permute-start(bf16[4,144,128]{2,1,0:T(8,128)(2,1)S(1)} %get-tuple-element.148), channel_id=1, source_target_pairs={{6,0},{8,2},{10,4},{12,6},{14,8},{16,10},{18,12},{20,14},{22,16},{... | collective-permute-start | bytes 442376 | tf_op jit(solution)/shard_map/ppermute | solution.py:834
  79.2 11.7 %collective-permute-start.6 = (bf16[4,144,128]{2,1,0:T(8,128)(2,1)S(1)}, bf16[4,144,128]{2,1,0:T(8,128)(2,1)S(1)}, u32[]{:S(2)}, u32[]{:S(2)}) collective-permute-start(bf16[4,144,128]{2,1,0:T(8,128)(2,1)S(1)} %get-tuple-element.146), channel_id=1, source_target_pairs={{16,0},{18,2},{20,4},{22,6},{24,8},{26,10},{28,12},{30,14},{17,1},... | collective-permute-start | bytes 442376 | tf_op jit(solution)/shard_map/ppermute | solution.py:834
  81.6 13.1 %copy-start.25 = (f32[4,128,256]{2,1,0:T(8,128)}, f32[4,128,256]{2,1,0:T(8,128)S(1)}, u32[]{:S(2)}) copy-start(f32[4,128,256]{2,1,0:T(8,128)S(1)} %entry.1) | copy-start | bytes 1572868
  91.0 10.1 %copy-start.32 = (bf16[2,256,1024]{2,1,0:T(8,128)(2,1)S(1)}, bf16[2,256,1024]{2,1,0:T(8,128)(2,1)}, u32[]{:S(2)}) copy-start(bf16[2,256,1024]{2,1,0:T(8,128)(2,1)} %refs_0_.1) | copy-start | bytes 3145732
  91.0 10.1 %copy-start.54 = (f32[1024]{0:T(1024)S(1)}, f32[1024]{0:T(1024)}, u32[]{:S(2)}) copy-start(f32[1024]{0:T(1024)} %param.37) | copy-start | bytes 12292
  97.5 2.7 collective-permute-start.9
  101.1 17.3 %copy-start.71 = (s32[16]{0:T(128)S(1)}, s32[16]{0:T(128)}, u32[]{:S(2)}) copy-start(s32[16]{0:T(128)} %constant.21.clone) | copy-start | bytes 196
  101.1 17.7 %copy-start.70 = (s32[16]{0:T(128)S(1)}, s32[16]{0:T(128)}, u32[]{:S(2)}) copy-start(s32[16]{0:T(128)} %constant.22.clone) | copy-start | bytes 196
  101.1 17.7 %copy-start.69 = (s32[16]{0:T(128)S(1)}, s32[16]{0:T(128)}, u32[]{:S(2)}) copy-start(s32[16]{0:T(128)} %constant.23.clone) | copy-start | bytes 196
  118.3 10.0 %copy-start.17 = (bf16[1024,512]{1,0:T(8,128)(2,1)}, bf16[1024,512]{1,0:T(8,128)(2,1)S(1)}, u32[]{:S(2)}) copy-start(bf16[1024,512]{1,0:T(8,128)(2,1)S(1)} %get-tuple-element.157) | copy-start | bytes 3145732
  118.3 15.5 %collective-permute-start.11 = (bf16[2,256,1024]{2,1,0:T(8,128)(2,1)}, bf16[2,256,1024]{2,1,0:T(8,128)(2,1)}, u32[]{:S(2)}, u32[]{:S(2)}) collective-permute-start(bf16[2,256,1024]{2,1,0:T(8,128)(2,1)} %get-tuple-element.155.refs_1_), channel_id=1, source_target_pairs={{0,1},{1,0},{2,3},{3,2},{4,5},{5,4},{6,7},{7,6},{8,9},{9,8},{10,11... | collective-permute-start | bytes 3145736 | tf_op jit(solution)/shard_map/ppermute | solution.py:839
  118.4 34.0 %collective-permute-start.10 = (bf16[2,256,1024]{2,1,0:T(8,128)(2,1)}, bf16[2,256,1024]{2,1,0:T(8,128)(2,1)}, u32[]{:S(2)}, u32[]{:S(2)}) collective-permute-start(bf16[2,256,1024]{2,1,0:T(8,128)(2,1)} %copy-done.38), channel_id=1, source_target_pairs={{0,1},{1,0},{2,3},{3,2},{4,5},{5,4},{6,7},{7,6},{8,9},{9,8},{10,11... | collective-permute-start | bytes 3145736 | tf_op jit(solution)/shard_map/ppermute | solution.py:839
  122.9 82.9 %collective-permute-start.19 = (bf16[512,1408]{1,0:T(8,128)(2,1)}, bf16[512,1408]{1,0:T(8,128)(2,1)}, u32[]{:S(2)}, u32[]{:S(2)}) collective-permute-start(bf16[512,1408]{1,0:T(8,128)(2,1)} %gate_send.1.refs_3_), channel_id=1, source_target_pairs={{0,2},{2,0},{4,6},{6,4},{8,10},{10,8},{12,14},{14,12},{16,18},{18,... | collective-permute-start | bytes 4325384 | tf_op jit(solution)/shard_map/ppermute | solution.py:828
  126.6 89.0 %collective-permute-start.18 = (bf16[512,1408]{1,0:T(8,128)(2,1)}, bf16[512,1408]{1,0:T(8,128)(2,1)}, u32[]{:S(2)}, u32[]{:S(2)}) collective-permute-start(bf16[512,1408]{1,0:T(8,128)(2,1)} %up_send.1.refs_3_), channel_id=1, source_target_pairs={{0,4},{2,6},{4,0},{6,2},{8,12},{10,14},{12,8},{14,10},{16,20},{18,... | collective-permute-start | bytes 4325384 | tf_op jit(solution)/shard_map/ppermute | solution.py:828
  131.0 88.0 %collective-permute-start.17 = (bf16[512,1408]{1,0:T(8,128)(2,1)}, bf16[512,1408]{1,0:T(8,128)(2,1)}, u32[]{:S(2)}, u32[]{:S(2)}) collective-permute-start(bf16[512,1408]{1,0:T(8,128)(2,1)} %down_send.1.refs_10_), channel_id=1, source_target_pairs={{0,8},{2,10},{4,12},{6,14},{8,0},{10,2},{12,4},{14,6},{16,24},{18,... | collective-permute-start | bytes 4325384 | tf_op jit(solution)/shard_map/ppermute | solution.py:828
  143.5 79.8 %copy-start.12 = (bf16[2,256,512]{2,1,0:T(8,128)(2,1)}, bf16[2,256,512]{2,1,0:T(8,128)(2,1)S(1)}, u32[]{:S(2)}) copy-start(bf16[2,256,512]{2,1,0:T(8,128)(2,1)S(1)} %get-tuple-element.183.refs_1_) | copy-start | bytes 1572868
  143.5 18.9 %collective-permute-start.12 = (bf16[4,128,256]{2,1,0:T(8,128)(2,1)}, bf16[4,128,256]{2,1,0:T(8,128)(2,1)}, u32[]{:S(2)}, u32[]{:S(2)}) collective-permute-start(bf16[4,128,256]{2,1,0:T(8,128)(2,1)} %bitcast.15), channel_id=1, source_target_pairs={{2,0},{4,2},{6,4},{8,6},{10,8},{12,10},{14,12},{16,14},{18,16},{20... | collective-permute-start | bytes 786440 | tf_op jit(solution)/shard_map/ppermute | solution.py:834
  145.0 7.4 %copy-start.1 = (f32[2,256,1024]{2,1,0:T(8,128)S(1)}, f32[2,256,1024]{2,1,0:T(8,128)}, u32[]{:S(2)}) copy-start(f32[2,256,1024]{2,1,0:T(8,128)} %get-tuple-element.150.refs_0_) | copy-start | bytes 6291460
  154.6 7.8 %copy-start.46 = (f32[2,2,128,256]{3,2,1,0:T(8,128)S(1)}, f32[2,2,128,256]{3,2,1,0:T(8,128)}, u32[]{:S(2)}) copy-start(f32[2,2,128,256]{3,2,1,0:T(8,128)} %copy-done.45) | copy-start | bytes 1572868
  154.6 7.8 %copy-start.51 = (bf16[2,2,144,128]{3,2,1,0:T(8,128)(2,1)S(1)}, bf16[2,2,144,128]{3,2,1,0:T(8,128)(2,1)}, u32[]{:S(2)}) copy-start(bf16[2,2,144,128]{3,2,1,0:T(8,128)(2,1)} %get-tuple-element.168) | copy-start | bytes 442372
  164.9 40.6 %copy-start.43 = (bf16[4,144,128]{2,1,0:T(8,128)(2,1)S(1)}, bf16[4,144,128]{2,1,0:T(8,128)(2,1)}, u32[]{:S(2)}) copy-start(bf16[4,144,128]{2,1,0:T(8,128)(2,1)} %copy-done.42) | copy-start | bytes 442372
  164.9 9.5 %collective-permute-start.13 = (bf16[4,128,256]{2,1,0:T(8,128)(2,1)S(1)}, bf16[4,128,256]{2,1,0:T(8,128)(2,1)S(1)}, u32[]{:S(2)}, u32[]{:S(2)}) collective-permute-start(bf16[4,128,256]{2,1,0:T(8,128)(2,1)S(1)} %get-tuple-element.172.refs_3_), channel_id=1, source_target_pairs={{4,0},{6,2},{8,4},{10,6},{12,8},{14,10},{16,12},{18,14},{20,16},{2... | collective-permute-start | bytes 786440 | tf_op jit(solution)/shard_map/ppermute | solution.py:834
  174.7 31.1 %copy-start.3 = (bf16[2,256,1408]{2,1,0:T(8,128)(2,1)S(1)}, bf16[2,256,1408]{2,1,0:T(8,128)(2,1)}, u32[]{:S(2)}) copy-start(bf16[2,256,1408]{2,1,0:T(8,128)(2,1)} %get-tuple-element.161) | copy-start | bytes 4325380
  174.7 14.4 %collective-permute-start.14 = (bf16[4,128,256]{2,1,0:T(8,128)(2,1)S(1)}, bf16[4,128,256]{2,1,0:T(8,128)(2,1)S(1)}, u32[]{:S(2)}, u32[]{:S(2)}) collective-permute-start(bf16[4,128,256]{2,1,0:T(8,128)(2,1)S(1)} %get-tuple-element.174.refs_3_), channel_id=1, source_target_pairs={{8,0},{10,2},{12,4},{14,6},{16,8},{18,10},{20,12},{22,14},{24,16},... | collective-permute-start | bytes 786440 | tf_op jit(solution)/shard_map/ppermute | solution.py:834
  190.1 14.0 %collective-permute-start.15 = (bf16[4,128,256]{2,1,0:T(8,128)(2,1)S(1)}, bf16[4,128,256]{2,1,0:T(8,128)(2,1)S(1)}, u32[]{:S(2)}, u32[]{:S(2)}) collective-permute-start(bf16[4,128,256]{2,1,0:T(8,128)(2,1)S(1)} %get-tuple-element.175.refs_3_), channel_id=1, source_target_pairs={{2,0},{4,2},{6,4},{8,6},{10,8},{12,10},{14,12},{16,14},{18,16},{20... | collective-permute-start | bytes 786440 | tf_op jit(solution)/shard_map/ppermute | solution.py:834
  191.4 14.0 %collective-permute-start.16 = (bf16[4,128,256]{2,1,0:T(8,128)(2,1)S(1)}, bf16[4,128,256]{2,1,0:T(8,128)(2,1)S(1)}, u32[]{:S(2)}, u32[]{:S(2)}) collective-permute-start(bf16[4,128,256]{2,1,0:T(8,128)(2,1)S(1)} %get-tuple-element.175.refs_3_), channel_id=1, source_target_pairs={{18,0},{20,2},{22,4},{24,6},{26,8},{28,10},{30,12},{19,1},{21,3},{... | collective-permute-start | bytes 786440 | tf_op jit(solution)/shard_map/ppermute | solution.py:834
  205.7 9.8 %copy-start.11 = (bf16[2,256,1408]{2,1,0:T(8,128)(2,1)S(1)}, bf16[2,256,1408]{2,1,0:T(8,128)(2,1)}, u32[]{:S(2)}) copy-start(bf16[2,256,1408]{2,1,0:T(8,128)(2,1)} %get-tuple-element.160) | copy-start | bytes 4325380
  209.2 28.2 %collective-permute-start.22 = (bf16[256,1408]{1,0:T(8,128)(2,1)}, bf16[256,1408]{1,0:T(8,128)(2,1)}, u32[]{:S(2)}, u32[]{:S(2)}) collective-permute-start(bf16[256,1408]{1,0:T(8,128)(2,1)} %get-tuple-element.191), channel_id=1, source_target_pairs={{0,4},{2,6},{4,0},{6,2},{8,12},{10,14},{12,8},{14,10},{16,20},{18,... | collective-permute-start | bytes 2162696 | tf_op jit(solution)/shard_map/ppermute | solution.py:828
  219.0 21.2 %collective-permute-start.21 = (bf16[256,1408]{1,0:T(8,128)(2,1)}, bf16[256,1408]{1,0:T(8,128)(2,1)}, u32[]{:S(2)}, u32[]{:S(2)}) collective-permute-start(bf16[256,1408]{1,0:T(8,128)(2,1)} %get-tuple-element.190), channel_id=1, source_target_pairs={{0,8},{2,10},{4,12},{6,14},{8,0},{10,2},{12,4},{14,6},{16,24},{18,... | collective-permute-start | bytes 2162696 | tf_op jit(solution)/shard_map/ppermute | solution.py:828
  222.8 18.9 %collective-permute-start.20 = (bf16[256,1408]{1,0:T(8,128)(2,1)}, bf16[256,1408]{1,0:T(8,128)(2,1)}, u32[]{:S(2)}, u32[]{:S(2)}) collective-permute-start(bf16[256,1408]{1,0:T(8,128)(2,1)} %get-tuple-element.189), channel_id=1, source_target_pairs={{0,2},{2,0},{4,6},{6,4},{8,10},{10,8},{12,14},{14,12},{16,18},{18,... | collective-permute-start | bytes 2162696 | tf_op jit(solution)/shard_map/ppermute | solution.py:828
  225.5 43.5 %collective-permute-start.28 = (bf16[512,1024]{1,0:T(8,128)(2,1)}, bf16[512,1024]{1,0:T(8,128)(2,1)}, u32[]{:S(2)}, u32[]{:S(2)}) collective-permute-start(bf16[512,1024]{1,0:T(8,128)(2,1)} %outs_send.1.refs_14_), channel_id=1, source_target_pairs={{0,8},{2,10},{4,12},{6,14},{8,0},{10,2},{12,4},{14,6},{16,24},{18,... | collective-permute-start | bytes 3145736 | tf_op jit(solution)/shard_map/ppermute | solution.py:828
  244.9 11.9 %collective-permute-start.31 = (bf16[128,1408]{1,0:T(8,128)(2,1)}, bf16[128,1408]{1,0:T(8,128)(2,1)}, u32[]{:S(2)}, u32[]{:S(2)}) collective-permute-start(bf16[128,1408]{1,0:T(8,128)(2,1)} %get-tuple-element.206), channel_id=1, source_target_pairs={{0,4},{2,6},{4,0},{6,2},{8,12},{10,14},{12,8},{14,10},{16,20},{18,... | collective-permute-start | bytes 1081352 | tf_op jit(solution)/shard_map/ppermute | solution.py:828
  246.3 13.5 %collective-permute-start.30 = (bf16[128,1408]{1,0:T(8,128)(2,1)}, bf16[128,1408]{1,0:T(8,128)(2,1)S(1)}, u32[]{:S(2)}, u32[]{:S(2)}) collective-permute-start(bf16[128,1408]{1,0:T(8,128)(2,1)} %copy-done.64), channel_id=1, source_target_pairs={{0,2},{2,0},{4,6},{6,4},{8,10},{10,8},{12,14},{14,12},{16,18},{18,... | collective-permute-start | bytes 1081352 | tf_op jit(solution)/shard_map/ppermute | solution.py:828
  246.7 19.5 %collective-permute-start.29 = (bf16[128,1408]{1,0:T(8,128)(2,1)}, bf16[128,1408]{1,0:T(8,128)(2,1)S(1)}, u32[]{:S(2)}, u32[]{:S(2)}) collective-permute-start(bf16[128,1408]{1,0:T(8,128)(2,1)} %copy-done.63), channel_id=1, source_target_pairs={{0,8},{2,10},{4,12},{6,14},{8,0},{10,2},{12,4},{14,6},{16,24},{18,... | collective-permute-start | bytes 1081352 | tf_op jit(solution)/shard_map/ppermute | solution.py:828
  255.5 26.5 %collective-permute-start.23 = (bf16[2,256,1024]{2,1,0:T(8,128)(2,1)S(1)}, bf16[2,256,1024]{2,1,0:T(8,128)(2,1)S(1)}, u32[]{:S(2)}, u32[]{:S(2)}) collective-permute-start(bf16[2,256,1024]{2,1,0:T(8,128)(2,1)S(1)} %get-tuple-element.196.refs_6_.refs_1_), channel_id=1, source_target_pairs={{0,1},{1,0},{2,3},{3,2},{4,5},{5,4},{6,7},{7,6},{8,9},{9,8},{10,11... | collective-permute-start | bytes 3145736 | tf_op jit(solution)/shard_map/ppermute | solution.py:839
  256.9 20.6 %collective-permute-start.27 = (bf16[512,640]{1,0:T(8,128)(2,1)S(1)}, bf16[512,640]{1,0:T(8,128)(2,1)S(1)}, u32[]{:S(2)}, u32[]{:S(2)}) collective-permute-start(bf16[512,640]{1,0:T(8,128)(2,1)S(1)} %query_key_send.1.refs_5_), channel_id=1, source_target_pairs={{0,2},{2,0},{4,6},{6,4},{8,10},{10,8},{12,14},{14,12},{16,18},{18,... | collective-permute-start | bytes 1966088 | tf_op jit(solution)/shard_map/ppermute | solution.py:828
  258.7 9.2 %copy-start.20 = (f32[128,1408]{1,0:T(8,128)S(1)}, f32[128,1408]{1,0:T(8,128)}, u32[]{:S(2)}) copy-start(f32[128,1408]{1,0:T(8,128)} %copy-done.19) | copy-start | bytes 2162692
  258.7 9.2 %copy-start.22 = (f32[128,1408]{1,0:T(8,128)S(1)}, f32[128,1408]{1,0:T(8,128)}, u32[]{:S(2)}) copy-start(f32[128,1408]{1,0:T(8,128)} %copy-done.21) | copy-start | bytes 2162692
  259.8 18.9 %collective-permute-start.26 = (bf16[512,512]{1,0:T(8,128)(2,1)S(1)}, bf16[512,512]{1,0:T(8,128)(2,1)S(1)}, u32[]{:S(2)}, u32[]{:S(2)}) collective-permute-start(bf16[512,512]{1,0:T(8,128)(2,1)S(1)} %value_send.1.refs_6_), channel_id=1, source_target_pairs={{0,4},{2,6},{4,0},{6,2},{8,12},{10,14},{12,8},{14,10},{16,20},{18,... | collective-permute-start | bytes 1572872 | tf_op jit(solution)/shard_map/ppermute | solution.py:828
  266.2 9.3 %collective-permute-start.24 = (bf16[2,16,1024]{2,1,0:T(8,128)(2,1)S(1)}, bf16[2,16,1024]{2,1,0:T(8,128)(2,1)S(1)}, u32[]{:S(2)}, u32[]{:S(2)}) collective-permute-start(bf16[2,16,1024]{2,1,0:T(8,128)(2,1)S(1)} %get-tuple-element.197), channel_id=1, source_target_pairs={{2,0},{4,2},{6,4},{8,6},{10,8},{12,10},{14,12},{16,14},{18,16},{20... | collective-permute-start | bytes 196616 | tf_op jit(solution)/shard_map/ppermute | solution.py:834
  269.1 26.2 %collective-permute-start.37 = (bf16[64,4224]{1,0:T(8,128)(2,1)S(1)}, bf16[64,4224]{1,0:T(8,128)(2,1)S(1)}, u32[]{:S(2)}, u32[]{:S(2)}) collective-permute-start(bf16[64,4224]{1,0:T(8,128)(2,1)S(1)} %get-tuple-element.220), channel_id=1, source_target_pairs={{0,16},{2,18},{4,20},{6,22},{8,24},{10,26},{12,28},{14,30},{16,0},... | collective-permute-start | bytes 1622024 | tf_op jit(solution)/shard_map/ppermute | solution.py:828
  275.4 20.9 %collective-permute-start.36 = (bf16[256,1024]{1,0:T(8,128)(2,1)}, bf16[256,1024]{1,0:T(8,128)(2,1)S(1)}, u32[]{:S(2)}, u32[]{:S(2)}) collective-permute-start(bf16[256,1024]{1,0:T(8,128)(2,1)} %get-tuple-element.219), channel_id=1, source_target_pairs={{0,2},{2,0},{4,6},{6,4},{8,10},{10,8},{12,14},{14,12},{16,18},{18,... | collective-permute-start | bytes 1572872 | tf_op jit(solution)/shard_map/ppermute | solution.py:828
  277.4 2.5 collective-permute-start.25
  278.7 18.7 %collective-permute-start.32 = (bf16[256,640]{1,0:T(8,128)(2,1)S(1)}, bf16[256,640]{1,0:T(8,128)(2,1)S(1)}, u32[]{:S(2)}, u32[]{:S(2)}) collective-permute-start(bf16[256,640]{1,0:T(8,128)(2,1)S(1)} %get-tuple-element.212), channel_id=1, source_target_pairs={{0,4},{2,6},{4,0},{6,2},{8,12},{10,14},{12,8},{14,10},{16,20},{18,... | collective-permute-start | bytes 983048 | tf_op jit(solution)/shard_map/ppermute | solution.py:828
  279.9 17.5 %collective-permute-start.33 = (bf16[256,512]{1,0:T(8,128)(2,1)S(1)}, bf16[256,512]{1,0:T(8,128)(2,1)S(1)}, u32[]{:S(2)}, u32[]{:S(2)}) collective-permute-start(bf16[256,512]{1,0:T(8,128)(2,1)S(1)} %get-tuple-element.213), channel_id=1, source_target_pairs={{0,2},{2,0},{4,6},{6,4},{8,10},{10,8},{12,14},{14,12},{16,18},{18,... | collective-permute-start | bytes 786440 | tf_op jit(solution)/shard_map/ppermute | solution.py:828
  282.0 2.4 collective-permute-start.34
  284.5 12.9 %collective-permute-start.35 = (f32[8,1024]{1,0:T(8,128)S(1)}, f32[8,1024]{1,0:T(8,128)S(1)}, u32[]{:S(2)}, u32[]{:S(2)}) collective-permute-start(f32[8,1024]{1,0:T(8,128)S(1)} %pack.1.refs_2_.refs_0_), channel_id=1, source_target_pairs={{0,2},{2,0},{4,6},{6,4},{8,10},{10,8},{12,14},{14,12},{16,18},{18,... | collective-permute-start | bytes 98312 | tf_op jit(solution)/shard_map/ppermute | solution.py:828
  297.6 11.2 %collective-permute-start.38 = (bf16[128,1152]{1,0:T(8,128)(2,1)S(1)}, bf16[128,1152]{1,0:T(8,128)(2,1)S(1)}, u32[]{:S(2)}, u32[]{:S(2)}) collective-permute-start(bf16[128,1152]{1,0:T(8,128)(2,1)S(1)} %get-tuple-element.224), channel_id=1, source_target_pairs={{0,8},{2,10},{4,12},{6,14},{8,0},{10,2},{12,4},{14,6},{16,24},{18,... | collective-permute-start | bytes 884744 | tf_op jit(solution)/shard_map/ppermute | solution.py:828
  300.7 8.0 %collective-permute-start.39 = (bf16[128,1024]{1,0:T(8,128)(2,1)S(1)}, bf16[128,1024]{1,0:T(8,128)(2,1)S(1)}, u32[]{:S(2)}, u32[]{:S(2)}) collective-permute-start(bf16[128,1024]{1,0:T(8,128)(2,1)S(1)} %get-tuple-element.225), channel_id=1, source_target_pairs={{0,4},{2,6},{4,0},{6,2},{8,12},{10,14},{12,8},{14,10},{16,20},{18,... | collective-permute-start | bytes 786440 | tf_op jit(solution)/shard_map/ppermute | solution.py:828
  302.7 6.0 %collective-permute-start.40 = (f32[8,1024]{1,0:T(8,128)S(1)}, f32[8,1024]{1,0:T(8,128)S(1)}, u32[]{:S(2)}, u32[]{:S(2)}) collective-permute-start(f32[8,1024]{1,0:T(8,128)S(1)} %small_sum.2.refs_4_.refs_0_), channel_id=1, source_target_pairs={{0,4},{2,6},{4,0},{6,2},{8,12},{10,14},{12,8},{14,10},{16,20},{18,... | collective-permute-start | bytes 98312 | tf_op jit(solution)/shard_map/ppermute | solution.py:828
  308.9 17.1 %collective-permute-start.41 = (bf16[64,2176]{1,0:T(8,128)(2,1)S(1)}, bf16[64,2176]{1,0:T(8,128)(2,1)S(1)}, u32[]{:S(2)}, u32[]{:S(2)}) collective-permute-start(bf16[64,2176]{1,0:T(8,128)(2,1)S(1)} %get-tuple-element.227), channel_id=1, source_target_pairs={{0,16},{2,18},{4,20},{6,22},{8,24},{10,26},{12,28},{14,30},{16,0},... | collective-permute-start | bytes 835592 | tf_op jit(solution)/shard_map/ppermute | solution.py:828
  309.0 6.0 %collective-permute-start.42 = (f32[8,1024]{1,0:T(8,128)S(1)}, f32[8,1024]{1,0:T(8,128)S(1)}, u32[]{:S(2)}, u32[]{:S(2)}) collective-permute-start(f32[8,1024]{1,0:T(8,128)S(1)} %small_sum.3.refs_4_.refs_1_), channel_id=1, source_target_pairs={{0,8},{2,10},{4,12},{6,14},{8,0},{10,2},{12,4},{14,6},{16,24},{18,... | collective-permute-start | bytes 98312 | tf_op jit(solution)/shard_map/ppermute | solution.py:828
  309.4 15.5 %collective-permute-start.43 = (f32[8,1024]{1,0:T(8,128)S(1)}, f32[8,1024]{1,0:T(8,128)S(1)}, u32[]{:S(2)}, u32[]{:S(2)}) collective-permute-start(f32[8,1024]{1,0:T(8,128)S(1)} %small_sum.3.refs_4_.refs_1_), channel_id=1, source_target_pairs={{0,16},{2,18},{4,20},{6,22},{8,24},{10,26},{12,28},{14,30},{16,0},... | collective-permute-start | bytes 98312 | tf_op jit(solution)/shard_map/ppermute | solution.py:828
  312.2 12.6 %collective-permute-start.44 = (f32[8,1024]{1,0:T(8,128)S(1)}, f32[8,1024]{1,0:T(8,128)S(1)}, u32[]{:S(2)}, u32[]{:S(2)}) collective-permute-start(f32[8,1024]{1,0:T(8,128)S(1)} %small_sum.3.refs_4_.refs_1_), channel_id=1, source_target_pairs={{0,24},{2,26},{4,28},{6,30},{8,16},{10,18},{12,20},{14,22},{16,8},... | collective-permute-start | bytes 98312 | tf_op jit(solution)/shard_map/ppermute | solution.py:828
  (53 other events, 128.7 us)
